TPU v7x, 256 devices: a whole 4x4x8 slice. The times are simulated.
256 devices in a mesh: row: 16 (over z, core), col: 16 (over x, y).
Axes of the slice: x: 4, y: 4, z: 8, core: 2. Of those that a mesh axis runs over, the one named last changes fastest.
Arguments:
- kernel: bfloat16 [4096, 16, 128, 128], P('row', 'col'), may hold values from -110 to 130
- tile_cols: int32 [4096, 16], P('row', 'col'), may hold values from 0 to 4095, as said below
- start_pot: float32 [524288], P('col'), may hold values from -452 to 2
- log_source: float32 [524288], P('row'), may hold values from -1 to 1
- log_target: float32 [524288], P('col'), may hold values from -1 to 1
- dustbin: float32 [524288], P('col'), may hold values from -1 to 2
Outputs:
- source_pot: float32 [524288], P('row')
- target_pot: float32 [524288], P('col')
Inputs may be any that keep to these rules, and one draw needn't show every extreme that they name: `tile_cols`: the 16 slots of one source tile name distinct column tiles. Among the tiles held by one device (one index of row and of col), at most 48 name column tiles of any one col block, and in each row block one col block is named by exactly 48 tiles of every device.
All inputs are finite; a program needn't handle non-finite values.
Results may differ from a plain program's by a relative error of at most 0.0003.
Values sent between devices are 32-bit elements; how exact they have to be, the bound alone decides.
No kernel may reach another device: no remote copies, remote signals or barrier semaphores. Data moves between devices by JAX's collectives and lax.ppermute only.
A program may use at most 64 MiB of HBM per device.

v0:
```python
import jax
import jax.numpy as jnp
from jax import lax
from jax.sharding import PartitionSpec as P

ITERS = 2


NEGATIVE = -1e30


def body(kernel, tile_cols, start_pot, log_source, log_target, dustbin):
    row_tiles, local_slots, tile_width, _ = kernel.shape
    col_count = lax.axis_size("col")
    block_tiles = start_pot.shape[0] // tile_width
    tile_count = row_tiles * local_slots
    capacity = min(tile_count // 2, 3 * tile_count // col_count)
    flat_cols = tile_cols.reshape(tile_count)
    owner = flat_cols // block_tiles
    local_tile = flat_cols % block_tiles
    one_hot = (owner[:, None] == jnp.arange(col_count)[None, :]).astype(jnp.int32)
    ranking = jnp.sum((jnp.cumsum(one_hot, axis=0) - one_hot) * one_hot, axis=1)
    slot_index = owner * capacity + ranking
    target_now = start_pot.reshape(block_tiles, tile_width)
    source_rows = log_source.reshape(row_tiles, tile_width)
    target_rows = log_target.reshape(block_tiles, tile_width)
    dust_rows = dustbin.reshape(block_tiles, tile_width)
    source_now = source_rows
    for repeat in range(ITERS):
        whole_target = lax.all_gather(target_now, "col", axis=0, tiled=True)
        slot_values = whole_target[flat_cols]
        scores = kernel.astype(jnp.float32) + slot_values.reshape(
            row_tiles, local_slots, 1, tile_width
        )
        peak_row = jnp.max(scores, axis=(1, 3))
        sum_row = jnp.sum(jnp.exp(scores - peak_row[:, None, :, None]), axis=(1, 3))
        highest = lax.pmax(peak_row, "col")
        sum_row = lax.psum(sum_row * jnp.exp(peak_row - highest), "col")
        row_lse = highest + jnp.log(sum_row)
        source_now = source_rows - row_lse
        scores = kernel.astype(jnp.float32) + source_now[:, None, :, None]
        peak_col = jnp.max(scores, axis=2)
        sum_col = jnp.sum(jnp.exp(scores - peak_col[:, :, None, :]), axis=2)
        peak_col = peak_col.reshape(tile_count, tile_width)
        sum_col = sum_col.reshape(tile_count, tile_width)
        send_tile = (
            jnp.full((col_count * capacity,), float(block_tiles), jnp.float32)
            .at[slot_index]
            .set(local_tile.astype(jnp.float32))
        )
        send_peak = (
            jnp.full((col_count * capacity, tile_width), NEGATIVE, jnp.float32)
            .at[slot_index]
            .set(peak_col)
        )
        send_sum = (
            jnp.zeros((col_count * capacity, tile_width), jnp.float32).at[slot_index].set(sum_col)
        )
        got_peak, got_sum, got_tile = (
            lax.all_to_all(
                send_peak.reshape(col_count, capacity, tile_width),
                "col",
                split_axis=0,
                concat_axis=0,
                tiled=True,
            ),
            lax.all_to_all(
                send_sum.reshape(col_count, capacity, tile_width),
                "col",
                split_axis=0,
                concat_axis=0,
                tiled=True,
            ),
            lax.all_to_all(
                send_tile.reshape(col_count, capacity),
                "col",
                split_axis=0,
                concat_axis=0,
                tiled=True,
            ),
        )
        segment = got_tile.reshape(col_count * capacity).astype(jnp.int32)
        got_peak = got_peak.reshape(col_count * capacity, tile_width)
        got_sum = got_sum.reshape(col_count * capacity, tile_width)
        part_peak = jnp.maximum(
            jax.ops.segment_max(got_peak, segment, num_segments=block_tiles + 1), NEGATIVE
        )
        part_sum = jax.ops.segment_sum(
            got_sum * jnp.exp(got_peak - part_peak[segment]), segment, num_segments=block_tiles + 1
        )
        part_peak = part_peak[:block_tiles]
        part_sum = part_sum[:block_tiles]
        block_peak = lax.pmax(part_peak, "row")
        block_sum = lax.psum(part_sum * jnp.exp(part_peak - block_peak), "row")
        top_value = jnp.maximum(block_peak, dust_rows)
        col_lse = top_value + jnp.log(
            block_sum * jnp.exp(block_peak - top_value) + jnp.exp(dust_rows - top_value)
        )
        target_now = target_rows - col_lse
    return (
        source_now.reshape(row_tiles * tile_width),
        target_now.reshape(block_tiles * tile_width),
    )


def solution(mesh):
    placed = (P("row", "col", None, None), P("row", "col"), P("col"), P("row"), P("col"), P("col"))
    return jax.shard_map(
        body, mesh=mesh, in_specs=placed, out_specs=(P("row"), P("col")), check_vma=False
    )
```

profile of v0, /device:TPU:1, one launch (start us, length us, event | category | flops | bytes accessed | tf_op | source)
XLA Modules:
  0.0 1047.0 jit_solution(5118723435786977364)
XLA Ops:
  9.6 53.8 %all-gather.3.cloned.1.call-done = f32[4096,128]{1,0:T(8,128)} async-done(((f32[256,128]{1,0:T(8,128)}), f32[4096,128]{1,0:T(8,128)}) %all-gather.3.cloned.1.call-update) | async-done | bytes 2097168 | tf_op jit(solution)/shard_map/all_gather | solution.py:30
  63.4 2.3 gather_fusion
  65.7 8.5 fusion.1
  74.2 11.2 %fusion.15 = f32[256,128]{1,0:T(8,128)S(1)} fusion(bf16[256,1,128,128]{3,2,1,0:T(8,128)(2,1)} %param.6, f32[256,128]{1,0:T(8,128)} %fusion.1, f32[256,128]{1,0:T(8,128)S(1)} %gather_fusion), kind=kLoop, calls=%fused_computation.32 | loop fusion | flops 16744448 | bytes 8781824 | tf_op jit(solution)/shard_map/reduce_sum | solution.py:36
  85.5 80.0 %all-reduce.9.cloned.1.call-done = f32[256,128]{1,0:T(8,128)} async-done(((f32[256,128]{1,0:T(8,128)}), f32[256,128]{1,0:T(8,128)}) %all-reduce.9.cloned.1.call-update) | async-done | bytes 131088 | tf_op jit(solution)/shard_map/pmax | solution.py:37
  168.7 10.7 %all_to_all.30 = f32[16,1,48]{2,1,0:T(1,128)S(1)} all-to-all(f32[16,1,48]{2,1,0:T(1,128)S(1)} %all_to_all.19), channel_id=1, replica_groups=mesh['row'=16,'col'=16] {'col'}, dimensions={0} | all-to-all | bytes 6144 | tf_op jit(solution)/shard_map/all_to_all | solution.py:74
  179.5 82.0 %all-reduce.11.cloned.1.call-done = f32[256,128]{1,0:T(8,128)} async-done(((f32[256,128]{1,0:T(8,128)}), f32[256,128]{1,0:T(8,128)}) %all-reduce.11.cloned.1.call-update) | async-done | bytes 131088 | tf_op jit(solution)/shard_map/psum | solution.py:38
  262.5 8.3 fusion.3
  270.8 1.9 scatter_custom_fusion.1
  272.7 4.5 all-to-all-start.1
  277.2 8.4 fusion.13
  285.6 1.9 scatter_custom_fusion.3
  287.4 6.7 all-to-all-start.2
  294.4 6.5 scatter_custom_fusion.2
  303.4 6.5 scatter_custom_fusion.4
  309.9 103.5 %all-reduce.13.cloned.1.call-done = f32[256,128]{1,0:T(8,128)} async-done(((f32[256,128]{1,0:T(8,128)}), f32[256,128]{1,0:T(8,128)}) %all-reduce.13.cloned.1.call-update) | async-done | bytes 131088 | tf_op jit(solution)/shard_map/pmax | solution.py:93
  415.1 109.0 %all-reduce.15.cloned.1.call-done = f32[256,128]{1,0:T(8,128)} async-done(((f32[256,128]{1,0:T(8,128)}), f32[256,128]{1,0:T(8,128)}) %all-reduce.15.cloned.1.call-update) | async-done | bytes 131088 | tf_op jit(solution)/shard_map/psum | solution.py:94
  525.9 50.6 %all-gather.5.cloned.1.call-done = f32[4096,128]{1,0:T(8,128)} async-done(((f32[256,128]{1,0:T(8,128)}), f32[4096,128]{1,0:T(8,128)}) %all-gather.5.cloned.1.call-update) | async-done | bytes 2097168 | tf_op jit(solution)/shard_map/all_gather | solution.py:30
  576.5 2.3 gather_fusion.2
  578.8 8.4 fusion.5
  587.5 11.2 %fusion.11 = f32[256,128]{1,0:T(8,128)S(1)} fusion(bf16[256,1,128,128]{3,2,1,0:T(8,128)(2,1)} %param.6, f32[256,128]{1,0:T(8,128)} %fusion.5, f32[256,128]{1,0:T(8,128)S(1)} %gather_fusion.2), kind=kLoop, calls=%fused_computation.28 | loop fusion | flops 16744448 | bytes 8781824 | tf_op jit(solution)/shard_map/reduce_sum | solution.py:36
  598.8 79.8 %all-reduce.17.cloned.1.call-done = f32[256,128]{1,0:T(8,128)} async-done(((f32[256,128]{1,0:T(8,128)}), f32[256,128]{1,0:T(8,128)}) %all-reduce.17.cloned.1.call-update) | async-done | bytes 131088 | tf_op jit(solution)/shard_map/pmax | solution.py:37
  680.2 94.3 %all-reduce.19.cloned.1.call-done = f32[256,128]{1,0:T(8,128)} async-done(((f32[256,128]{1,0:T(8,128)}), f32[256,128]{1,0:T(8,128)}) %all-reduce.19.cloned.1.call-update) | async-done | bytes 131088 | tf_op jit(solution)/shard_map/psum | solution.py:38
  775.5 8.4 fusion.7
  783.9 1.9 scatter_custom_fusion.5
  785.7 4.5 all-to-all-start.3
  790.2 8.3 fusion.9
  800.4 6.7 all-to-all-start.4
  807.2 6.5 scatter_custom_fusion.6
  816.1 6.5 scatter_custom_fusion.8
  822.7 105.2 %all-reduce.21.cloned.1.call-done = f32[256,128]{1,0:T(8,128)} async-done(((f32[256,128]{1,0:T(8,128)}), f32[256,128]{1,0:T(8,128)}) %all-reduce.21.cloned.1.call-update) | async-done | bytes 131088 | tf_op jit(solution)/shard_map/pmax | solution.py:93
  929.4 109.1 %all-reduce.23.cloned.1.call-done = f32[256,128]{1,0:T(8,128)} async-done(((f32[256,128]{1,0:T(8,128)}), f32[256,128]{1,0:T(8,128)}) %all-reduce.23.cloned.1.call-update) | async-done | bytes 131088 | tf_op jit(solution)/shard_map/psum | solution.py:94
  (73 shorter events, 23.3 us)
Async XLA Ops:
  7.2 56.2 %all-gather.3.cloned.1.call-start = ((), (), s32[]{:S(2)}) async-start(), calls=%async_computation.5 | async-start | bytes 2228224 | tf_op jit(solution)/shard_map/all_gather | solution.py:30
  7.9 157.6 %all-reduce.9.cloned.1.call-start = ((), (), s32[]{:S(2)}) async-start(), calls=%async_computation.6 | async-start | bytes 262144 | tf_op jit(solution)/shard_map/pmax | solution.py:37
  65.7 101.4 %copy-start.6 = (s32[256,1]{0,1:T(1,128)S(1)}, s32[256,1]{0,1:T(1,128)}, u32[]{:S(2)}) copy-start(s32[256,1]{0,1:T(1,128)} %param.7) | copy-start | bytes 3076
  65.7 195.8 %copy-start.5 = (f32[32768]{0:T(1024)S(1)}, f32[32768]{0:T(1024)}, u32[]{:S(2)}) copy-start(f32[32768]{0:T(1024)} %param.9) | copy-start | bytes 393220
  74.2 91.3 %copy-start = (f32[256,128]{1,0:T(8,128)S(1)}, f32[256,128]{1,0:T(8,128)}, u32[]{:S(2)}) copy-start(f32[256,128]{1,0:T(8,128)} %fusion.1) | copy-start | bytes 393220
  74.2 187.3 %all-reduce.11.cloned.1.call-start = ((), (), s32[]{:S(2)}) async-start(), calls=%async_computation.7 | async-start | bytes 262144 | tf_op jit(solution)/shard_map/psum | solution.py:38
  272.7 14.8 %all-to-all-start.1 = ((f32[16,48,128]{2,1,0:T(8,128)}), f32[16,48,128]{2,1,0:T(8,128)S(1)}, u32[]{:S(2)}, u32[]{:S(2)}) async-start(f32[16,48,128]{2,1,0:T(8,128)} %bitcast.10), calls=%async_computation.1 | async-start | bytes 786432 | tf_op jit(solution)/shard_map/all_to_all | solution.py:60
  277.1 247.0 %copy-start.3 = (f32[32768]{0:T(1024)S(1)}, f32[32768]{0:T(1024)}, u32[]{:S(2)}) copy-start(f32[32768]{0:T(1024)} %param.11) | copy-start | bytes 393220
  277.2 247.0 %copy-start.4 = (f32[32768]{0:T(1024)S(1)}, f32[32768]{0:T(1024)}, u32[]{:S(2)}) copy-start(f32[32768]{0:T(1024)} %param.10) | copy-start | bytes 393220
  287.4 15.9 %all-to-all-start.2 = ((f32[16,48,128]{2,1,0:T(8,128)}), f32[16,48,128]{2,1,0:T(8,128)S(1)}, u32[]{:S(2)}, u32[]{:S(2)}) async-start(f32[16,48,128]{2,1,0:T(8,128)} %bitcast.13), calls=%async_computation.2 | async-start | bytes 786432 | tf_op jit(solution)/shard_map/all_to_all | solution.py:67
  294.1 119.4 %all-reduce.13.cloned.1.call-start = ((), (), s32[]{:S(2)}) async-start(), calls=%async_computation.8 | async-start | bytes 262144 | tf_op jit(solution)/shard_map/pmax | solution.py:93
  301.7 222.5 %all-reduce.15.cloned.1.call-start = ((), (), s32[]{:S(2)}) async-start(), calls=%async_computation.9 | async-start | bytes 262144 | tf_op jit(solution)/shard_map/psum | solution.py:94
  415.1 161.4 %all-gather.5.cloned.1.call-start = ((), (), s32[]{:S(2)}) async-start(), calls=%async_computation.10 | async-start | bytes 2228224 | tf_op jit(solution)/shard_map/all_gather | solution.py:30
  525.9 152.7 %all-reduce.17.cloned.1.call-start = ((), (), s32[]{:S(2)}) async-start(), calls=%async_computation.11 | async-start | bytes 262144 | tf_op jit(solution)/shard_map/pmax | solution.py:37
  587.2 91.3 %copy-start.1 = (f32[256,128]{1,0:T(8,128)S(1)}, f32[256,128]{1,0:T(8,128)}, u32[]{:S(2)}) copy-start(f32[256,128]{1,0:T(8,128)} %fusion.5) | copy-start | bytes 393220
  587.3 187.2 %all-reduce.19.cloned.1.call-start = ((), (), s32[]{:S(2)}) async-start(), calls=%async_computation.12 | async-start | bytes 262144 | tf_op jit(solution)/shard_map/psum | solution.py:38
  775.5 23.1 %copy-start.2 = (f32[256,128]{1,0:T(8,128)}, f32[256,128]{1,0:T(8,128)S(1)}, u32[]{:S(2)}) copy-start(f32[256,128]{1,0:T(8,128)S(1)} %bitcast_subtract_fusion.2) | copy-start | bytes 393220
  785.7 14.7 %all-to-all-start.3 = ((f32[16,48,128]{2,1,0:T(8,128)}), f32[16,48,128]{2,1,0:T(8,128)S(1)}, u32[]{:S(2)}, u32[]{:S(2)}) async-start(f32[16,48,128]{2,1,0:T(8,128)} %bitcast.16), calls=%async_computation.3 | async-start | bytes 786432 | tf_op jit(solution)/shard_map/all_to_all | solution.py:60
  800.4 15.6 %all-to-all-start.4 = ((f32[16,48,128]{2,1,0:T(8,128)}), f32[16,48,128]{2,1,0:T(8,128)S(1)}, u32[]{:S(2)}, u32[]{:S(2)}) async-start(f32[16,48,128]{2,1,0:T(8,128)} %bitcast.18), calls=%async_computation.4 | async-start | bytes 786432 | tf_op jit(solution)/shard_map/all_to_all | solution.py:67
  807.1 120.7 %all-reduce.21.cloned.1.call-start = ((), (), s32[]{:S(2)}) async-start(), calls=%async_computation.13 | async-start | bytes 262144 | tf_op jit(solution)/shard_map/pmax | solution.py:93
  816.0 222.5 %all-reduce.23.cloned.1.call-start = ((), (), s32[]{:S(2)}) async-start(), calls=%async_computation.14 | async-start | bytes 262144 | tf_op jit(solution)/shard_map/psum | solution.py:94
Sparse Core Ops, SparseCore 0:
  10.4 52.8 all-gather.2
  74.3 91.1 all-reduce.8
  169.6 91.8 all-reduce.10
  301.8 111.6 all-reduce.12
  416.3 107.7 all-reduce.14
  527.0 49.4 all-gather.4
  587.4 91.1 all-reduce.16
  682.7 91.7 all-reduce.18
  816.1 111.6 all-reduce.20
  930.7 107.7 all-reduce.22
where the time goes:
time: 1050 us
  waiting for transfers between devices  868 us (83%)
  other arithmetic  112 us (11%)
  starting transfers between devices  23 us (2%)
  local copies, waits for them, and re-layouts  18.4 us (2%)
  between operations  14.5 us (1%)
  blocking collectives  10.7 us (1%)
    psum x2, waiting for transfers between devices, body(): block_sum = lax.psum(part_sum * jnp.exp(part_peak - block_peak), 'row')  218 us
    pmax x2, waiting for transfers between devices, body(): block_peak = lax.pmax(part_peak, 'row')  209 us
    psum x2, waiting for transfers between devices, body(): sum_row = lax.psum(sum_row * jnp.exp(peak_row - highest), 'col')  176 us
    pmax x2, waiting for transfers between devices, body(): highest = lax.pmax(peak_row, 'col')  160 us
    all_gather x2, waiting for transfers between devices, body(): whole_target = lax.all_gather(target_now, 'col', axis=0, tiled=True)  104 us
    reduce_sum x2, other arithmetic, body(): sum_row = jnp.sum(jnp.exp(scores - peak_row[:, None, :, None]), axis=(1, 3))  22.5 us
  transfers between devices with their start and end apart: 14, of which 10 were waited for; matrix products, arithmetic and copies ran while one was open for 7% of the time, Pallas kernels for 0%

commit v1 on v0

v1 whole, which is shorter than its diff:
```python
import functools

import jax
import jax.numpy as jnp
from jax import lax
from jax.experimental import pallas as pl
from jax.experimental.pallas import tpu as pltpu
from jax.sharding import PartitionSpec as P

ITERS = 2
NEGATIVE = -1e30
VMEM = pltpu.VMEM
SMEM = pltpu.SMEM
VMEM_BYTES = 24 << 20
UNROLL = 16


def spec(space):
    return pl.BlockSpec(memory_space=space)


def params():
    return pltpu.CompilerParams(vmem_limit_bytes=VMEM_BYTES)


def plan_kernel(block_tiles, capacity, cols_ref, slot_ref, ask_ref, count_ref):
    tile_count = slot_ref.shape[0]
    asked = ask_ref.shape[0]

    def clear(step, carry):
        for k in range(16):
            ask_ref[step * 16 + k] = block_tiles
        return carry

    lax.fori_loop(0, asked // 16, clear, 0)
    for k in range(count_ref.shape[0]):
        count_ref[k] = 0

    def place(step, carry):
        for k in range(8):
            n = step * 8 + k
            column = cols_ref[n]
            owner = column // block_tiles
            rank = count_ref[owner]
            count_ref[owner] = rank + 1
            slot = owner * capacity + rank
            slot_ref[n] = slot
            ask_ref[slot] = column - owner * block_tiles
        return carry

    lax.fori_loop(0, tile_count // 8, place, 0)


def plan(cols, block_tiles, capacity, owners):
    return pl.pallas_call(
        functools.partial(plan_kernel, block_tiles, capacity),
        name="plan",
        out_shape=(
            jax.ShapeDtypeStruct(cols.shape, jnp.int32),
            jax.ShapeDtypeStruct((owners * capacity,), jnp.int32),
        ),
        in_specs=[spec(SMEM)],
        out_specs=(spec(SMEM), spec(SMEM)),
        scratch_shapes=[SMEM((owners,), jnp.int32)],
    )(cols)


def pick_kernel(ids_ref, rows_ref, out_ref):
    last = rows_ref.shape[0] - 1

    def step(p, carry):
        for k in range(16):
            n = p * 16 + k
            out_ref[pl.ds(n, 1), :] = rows_ref[pl.ds(jnp.minimum(ids_ref[n], last), 1), :]
        return carry

    lax.fori_loop(0, out_ref.shape[0] // 16, step, 0)


def pick(ids, rows):
    return pl.pallas_call(
        pick_kernel,
        name="pick",
        out_shape=jax.ShapeDtypeStruct((ids.shape[0], rows.shape[1]), jnp.float32),
        in_specs=[spec(SMEM), spec(VMEM)],
        out_specs=spec(VMEM),
        compiler_params=params(),
    )(ids, rows)


def row_kernel(slot_ref, tiles_ref, pots_ref, out_ref):
    def step(g, carry):
        tops, sums = [], []
        for k in range(UNROLL):
            n = g * UNROLL + k
            pot = pots_ref[pl.ds(slot_ref[n], 1), :]
            scores = jnp.transpose(tiles_ref[n].astype(jnp.float32) + pot)
            top = jnp.max(scores, axis=0, keepdims=True)
            tops.append(top)
            sums.append(jnp.sum(jnp.exp(scores - top), axis=0, keepdims=True))
        block = pl.ds(pl.multiple_of(g * UNROLL, UNROLL), UNROLL)
        out_ref[block, :] = jnp.concatenate(tops, 0) + jnp.log(jnp.concatenate(sums, 0))
        return carry

    lax.fori_loop(0, tiles_ref.shape[0] // UNROLL, step, 0)


def row_pass(slot, tiles, pots):
    return pl.pallas_call(
        row_kernel,
        name="row_pass",
        out_shape=jax.ShapeDtypeStruct(tiles.shape[:2], jnp.float32),
        in_specs=[spec(SMEM), spec(VMEM), spec(VMEM)],
        out_specs=spec(VMEM),
        compiler_params=params(),
    )(slot, tiles, pots)


def col_kernel(slot_ref, tiles_ref, pots_ref, out_ref, row_ref):
    out_ref[...] = jnp.full(out_ref.shape, NEGATIVE, jnp.float32)
    width = tiles_ref.shape[1]

    def step(g, carry):
        tops, sums = [], []
        for k in range(UNROLL):
            n = g * UNROLL + k
            pot = jnp.broadcast_to(pots_ref[pl.ds(n, 1), :], (width, width))
            scores = tiles_ref[n].astype(jnp.float32) + jnp.transpose(pot)
            top = jnp.max(scores, axis=0, keepdims=True)
            tops.append(top)
            sums.append(jnp.sum(jnp.exp(scores - top), axis=0, keepdims=True))
        row_ref[...] = jnp.concatenate(tops, 0) + jnp.log(jnp.concatenate(sums, 0))
        for k in range(UNROLL):
            out_ref[pl.ds(slot_ref[g * UNROLL + k], 1), :] = row_ref[pl.ds(k, 1), :]
        return carry

    lax.fori_loop(0, tiles_ref.shape[0] // UNROLL, step, 0)


def col_pass(slot, tiles, pots, slots):
    width = tiles.shape[1]
    return pl.pallas_call(
        col_kernel,
        name="col_pass",
        out_shape=jax.ShapeDtypeStruct((slots, width), jnp.float32),
        in_specs=[spec(SMEM), spec(VMEM), spec(VMEM)],
        out_specs=spec(VMEM),
        scratch_shapes=[VMEM((UNROLL, width), jnp.float32)],
        compiler_params=params(),
    )(slot, tiles, pots)


def segment_kernel(ids_ref, rows_ref, out_ref, top_ref, *parts):
    groups = len(parts)
    each = rows_ref.shape[0] // groups
    for part in parts:
        part[...] = jnp.full(part.shape, NEGATIVE, jnp.float32)

    def highest(p, carry):
        for k in range(4):
            for g, part in enumerate(parts):
                n = g * each + p * 4 + k
                here = pl.ds(ids_ref[n], 1)
                part[here, :] = jnp.maximum(part[here, :], rows_ref[pl.ds(n, 1), :])
        return carry

    lax.fori_loop(0, each // 4, highest, 0)
    top = parts[0][...]
    for part in parts[1:]:
        top = jnp.maximum(top, part[...])
    top_ref[...] = top
    for part in parts:
        part[...] = jnp.zeros(part.shape, jnp.float32)

    def add(p, carry):
        for k in range(4):
            for g, part in enumerate(parts):
                n = g * each + p * 4 + k
                here = pl.ds(ids_ref[n], 1)
                part[here, :] = part[here, :] + jnp.exp(rows_ref[pl.ds(n, 1), :] - top_ref[here, :])
        return carry

    lax.fori_loop(0, each // 4, add, 0)
    total = parts[0][...]
    for part in parts[1:]:
        total = total + part[...]
    count = out_ref.shape[0]
    total = total[:count]
    some = total > 0.0
    out_ref[...] = jnp.where(
        some, top_ref[:count, :] + jnp.log(jnp.where(some, total, 1.0)), NEGATIVE
    )


def segment(ids, rows, count):
    width = rows.shape[1]
    return pl.pallas_call(
        segment_kernel,
        name="segment",
        out_shape=jax.ShapeDtypeStruct((count, width), jnp.float32),
        in_specs=[spec(SMEM), spec(VMEM)],
        out_specs=spec(VMEM),
        scratch_shapes=[VMEM((count + 8, width), jnp.float32)] * 9,
        compiler_params=params(),
    )(ids, rows)


def exchange(value, owners):
    shape = value.shape
    return lax.all_to_all(
        value.reshape((owners, shape[0] // owners) + shape[1:]),
        "col",
        split_axis=0,
        concat_axis=0,
        tiled=True,
    ).reshape(shape)


def log_add(a, b):
    return jnp.maximum(a, b) + jnp.log(1.0 + jnp.exp(-jnp.abs(a - b)))


def swap(value, axis, partner):
    return lax.ppermute(value, axis, [(i, j) for i, j in enumerate(partner)])


def col_partners(count):
    return [
        [i ^ 1 for i in range(count)],
        [i ^ 3 for i in range(count)],
        [i ^ 4 for i in range(count)],
        [i ^ 12 for i in range(count)],
    ]


def row_partners(count):
    steps = ([1, 0, 3, 2, 5, 4, 7, 6], [7, 2, 1, 4, 3, 6, 5, 0], [3, 6, 5, 0, 7, 2, 1, 4])
    return [[2 * z[i // 2] + i % 2 for i in range(count)] for z in steps]


def body(kernel, tile_cols, start_pot, log_source, log_target, dustbin):
    row_tiles, local_slots, width, _ = kernel.shape
    owners = lax.axis_size("col")
    block_tiles = start_pot.shape[0] // width
    tile_count = row_tiles * local_slots
    capacity = min(tile_count // 2, 3 * tile_count // owners)
    slots = owners * capacity
    half = block_tiles // 2
    core = lax.axis_index("row") % 2
    other_core = [i ^ 1 for i in range(lax.axis_size("row"))]

    tiles = kernel.reshape(tile_count, width, width)
    target_now = start_pot.reshape(block_tiles, width)
    source_rows = log_source.reshape(row_tiles, width)

    def mine(value, side):
        return lax.dynamic_slice_in_dim(value, side * half, half, 0)

    target_half = mine(log_target.reshape(block_tiles, width), core)
    dust_half = mine(dustbin.reshape(block_tiles, width), core)

    slot, ask = plan(tile_cols.reshape(tile_count), block_tiles, capacity, owners)
    ids = exchange(ask, owners)
    for repeat in range(ITERS):
        pots = exchange(pick(ids, target_now), owners)
        row_lse = row_pass(slot, tiles, pots)
        for partner in col_partners(owners):
            row_lse = log_add(row_lse, swap(row_lse, "col", partner))
        source_now = source_rows - row_lse
        rows = exchange(col_pass(slot, tiles, source_now, slots), owners)
        part = segment(ids, rows, block_tiles)
        col_lse = log_add(mine(part, core), swap(mine(part, 1 - core), "row", other_core))
        for partner in row_partners(len(other_core)):
            col_lse = log_add(col_lse, swap(col_lse, "row", partner))
        here = target_half - log_add(col_lse, dust_half)
        there = swap(here, "row", other_core)
        target_now = jnp.where(
            core == 0, jnp.concatenate([here, there]), jnp.concatenate([there, here])
        )
    return source_now.reshape(log_source.shape), target_now.reshape(start_pot.shape)


def solution(mesh):
    placed = (P("row", "col", None, None), P("row", "col"), P("col"), P("row"), P("col"), P("col"))
    return jax.shard_map(
        body, mesh=mesh, in_specs=placed, out_specs=(P("row"), P("col")), check_vma=False
    )
```

time: 1050 us -> 208 us (0.20)
  waiting for transfers between devices: 868 us -> 60 us
  other arithmetic: 112 us -> 2.1 us
  Pallas kernels: 0 us -> 42.7 us
  blocking collectives: 10.7 us -> 47.6 us
  starting transfers between devices: 23 us -> 44.2 us
  between operations: 14.5 us -> 0.85 us
    psum x4 -> x0, waiting for transfers between devices: 394 us -> none  [the longest x2 218 us: body(): block_sum = lax.psum(part_sum * jnp.exp(part_peak - block_peak), 'row')]
    pmax x4 -> x0, waiting for transfers between devices: 369 us -> none  [the longest x2 209 us: body(): block_peak = lax.pmax(part_peak, 'row')]
    all_gather x2 -> x0, waiting for transfers between devices: 104 us -> none  [body(): whole_target = lax.all_gather(target_now, 'col', axis=0, tiled=True)]
    ppermute x0 -> x18, waiting for transfers between devices: none -> 52.1 us  [swap(): return lax.ppermute(value, axis, [(i, j) for i, j in enumerate(partner)])]
    pallas_call x0 -> x9, Pallas kernels: none -> 42.7 us  [the longest x2 15.6 us: col_pass(): pl.pallas_call(col_kernel, name='col_pass', out_shape=jax.ShapeDtypeStruc...]
    ppermute x0 -> x18, starting transfers between devices: none -> 40.7 us  [swap(): return lax.ppermute(value, axis, [(i, j) for i, j in enumerate(partner)])]
    reduce_sum x5 -> x0, other arithmetic: 39.3 us -> none  [the longest x2 22.5 us: body(): sum_row = jnp.sum(jnp.exp(scores - peak_row[:, None, :, None]), axis=(1, 3))]
    all_to_all x1 -> x4, blocking collectives: 10.7 us -> 47.6 us  [exchange(): lax.all_to_all(value.reshape((owners, shape[0] // owners) + shape[1:]), '...]
  transfers between devices with their start and end apart: 14 -> 19, of which waited for: 10 -> 19; matrix products, arithmetic and copies ran while one was open for 7% -> 0% of each run, Pallas kernels for 0% -> 0%
where the time goes in v1:
time: 208 us; the launch traced here: 207 us
  waiting for transfers between devices  60 us (29%)
  blocking collectives  47.6 us (23%)
  starting transfers between devices  44.2 us (21%)
  Pallas kernels  42.7 us (21%)
  local copies, waits for them, and re-layouts  9.76 us (5%)
  other arithmetic  2.1 us (1%)
    ppermute x18, waiting for transfers between devices, swap(): return lax.ppermute(value, axis, [(i, j) for i, j in enumerate(partner)])  52.1 us
    all_to_all x4, blocking collectives, exchange(): lax.all_to_all(value.reshape((owners, shape[0] // owners) + shape[1:]), '...  47.6 us
    ppermute x18, starting transfers between devices, swap(): return lax.ppermute(value, axis, [(i, j) for i, j in enumerate(partner)])  40.7 us
    pallas_call x2, Pallas kernels, col_pass(): pl.pallas_call(col_kernel, name='col_pass', out_shape=jax.ShapeDtypeStruc...  15.6 us
    pallas_call x2, Pallas kernels, row_pass(): pl.pallas_call(row_kernel, name='row_pass', out_shape=jax.ShapeDtypeStruc...  13.8 us
    unnamed x18, local copies, waits for them, and re-layouts  8.38 us
    all_to_all x1, waiting for transfers between devices, exchange(): lax.all_to_all(value.reshape((owners, shape[0] // owners) + shape[1:]), '...  7.91 us
    pallas_call x2, Pallas kernels, segment(): pl.pallas_call(segment_kernel, name='segment', out_shape=jax.ShapeDtypeSt...  5.5 us
  transfers between devices with their start and end apart: 19, of which 19 were waited for; matrix products, arithmetic and copies ran while one was open for 0% of the time, Pallas kernels for 0%

profile of v1, /device:TPU:1, one launch (start us, length us, event | category | flops | bytes accessed | tf_op | source)
XLA Modules:
  0.0 207.3 jit_solution(11191777304072887403)
XLA Ops:
  0.6 4.1 %plan.1 = (s32[256]{0:T(256)}, s32[768]{0:T(1024)}) custom-call(s32[256]{0:T(256)} %bitcast.36), custom_call_target="tpu_custom_call" | custom-call | tf_op jit(solution)/shard_map/plan/pallas_call | solution.py:55
  5.5 13.8 %all_to_all.29 = s32[16,1,48]{2,1,0:T(1,128)S(1)} all-to-all(s32[16,1,48]{2,1,0:T(1,128)S(1)} %all_to_all.18), channel_id=1, replica_groups=mesh['row'=16,'col'=16] {'col'}, dimensions={0} | all-to-all | bytes 6144 | tf_op jit(solution)/shard_map/all_to_all | solution.py:210
  23.3 10.7 %all_to_all.30 = f32[16,48,128]{2,1,0:T(8,128)S(1)} all-to-all(f32[16,48,128]{2,1,0:T(8,128)S(1)} %bitcast.29), channel_id=1, replica_groups=mesh['row'=16,'col'=16] {'col'}, dimensions={0} | all-to-all | bytes 786432 | tf_op jit(solution)/shard_map/all_to_all | solution.py:210
  34.1 3.4 %copy-done = bf16[256,1,128,128]{3,2,1,0:T(8,128)(2,1)S(1)} copy-done((bf16[256,1,128,128]{3,2,1,0:T(8,128)(2,1)S(1)}, bf16[256,1,128,128]{3,2,1,0:T(8,128)(2,1)}, u32[]{:S(2)}) %copy-start) | copy-done | bytes 8388632
  38.1 6.9 %row_pass.2 = f32[256,128]{1,0:T(8,128)S(1)} custom-call(s32[256]{0:T(256)S(1)} %copy-done.4, bf16[256,128,128]{2,1,0:T(8,128)(2,1)S(1)} %bitcast.19, f32[768,128]{1,0:T(8,128)S(1)} %bitcast.23), custom_call_target="tpu_custom_call" | custom-call | tf_op jit(solution)/shard_map/row_pass/pallas_call | solution.py:109
  45.2 3.7 %collective-permute-done = f32[256,128]{1,0:T(8,128)S(1)} collective-permute-done((f32[256,128]{1,0:T(8,128)S(1)}, f32[256,128]{1,0:T(8,128)S(1)}, u32[]{:S(2)}, u32[]{:S(2)}) %collective-permute-start) | collective-permute-done | bytes 131104 | tf_op jit(solution)/shard_map/ppermute | solution.py:224
  49.8 4.3 %collective-permute-done.1 = f32[256,128]{1,0:T(8,128)S(1)} collective-permute-done((f32[256,128]{1,0:T(8,128)S(1)}, f32[256,128]{1,0:T(8,128)S(1)}, u32[]{:S(2)}, u32[]{:S(2)}) %collective-permute-start.1) | collective-permute-done | bytes 131104 | tf_op jit(solution)/shard_map/ppermute | solution.py:224
  54.3 4.1 %collective-permute-done.2 = f32[256,128]{1,0:T(8,128)S(1)} collective-permute-done((f32[256,128]{1,0:T(8,128)S(1)}, f32[256,128]{1,0:T(8,128)S(1)}, u32[]{:S(2)}, u32[]{:S(2)}) %collective-permute-start.2) | collective-permute-done | bytes 131104 | tf_op jit(solution)/shard_map/ppermute | solution.py:224
  59.5 4.0 %collective-permute-done.3 = f32[256,128]{1,0:T(8,128)S(1)} collective-permute-done((f32[256,128]{1,0:T(8,128)S(1)}, f32[256,128]{1,0:T(8,128)S(1)}, u32[]{:S(2)}, u32[]{:S(2)}) %collective-permute-start.3) | collective-permute-done | bytes 131104 | tf_op jit(solution)/shard_map/ppermute | solution.py:224
  63.6 8.2 %col_pass.2 = f32[768,128]{1,0:T(8,128)} custom-call(s32[256]{0:T(256)S(1)} %copy-done.4, bf16[256,128,128]{2,1,0:T(8,128)(2,1)S(1)} %bitcast.20, f32[256,128]{1,0:T(8,128)S(1)} %bitcast_subtract_fusion.1.pots_ref), custom_call_target="tpu_custom_call" | custom-call | tf_op jit(solution)/shard_map/col_pass/pallas_call | solution.py:142
  71.8 3.6 %all-to-all-start.2 = ((f32[16,48,128]{2,1,0:T(8,128)}), f32[16,48,128]{2,1,0:T(8,128)S(1)}, u32[]{:S(2)}, u32[]{:S(2)}) async-start(f32[16,48,128]{2,1,0:T(8,128)} %bitcast.7), calls=%async_computation.2 | async-start | bytes 786432 | tf_op jit(solution)/shard_map/all_to_all | solution.py:210
  75.4 7.9 %all-to-all-done.2 = f32[16,48,128]{2,1,0:T(8,128)S(1)} async-done(((f32[16,48,128]{2,1,0:T(8,128)}), f32[16,48,128]{2,1,0:T(8,128)S(1)}, u32[]{:S(2)}, u32[]{:S(2)}) %all-to-all-start.2) | async-done | bytes 393248 | tf_op jit(solution)/shard_map/all_to_all | solution.py:210
  83.3 2.8 %segment.2 = f32[256,128]{1,0:T(8,128)S(1)} custom-call(s32[768]{0:T(1024)S(1)} %reshape.65.ids_ref, f32[768,128]{1,0:T(8,128)S(1)} %bitcast.26), custom_call_target="tpu_custom_call" | custom-call | tf_op jit(solution)/shard_map/segment/pallas_call | solution.py:197
  86.1 9.0 %collective-permute-start.4 = (f32[128,128]{1,0:T(8,128)S(1)}, f32[128,128]{1,0:T(8,128)S(1)}, u32[]{:S(2)}, u32[]{:S(2)}) collective-permute-start(f32[128,128]{1,0:T(8,128)S(1)} %constant_dynamic-slice_fusion.1), channel_id=1, source_target_pairs={{0,16},{16,0},{32,48},{48,32},{64,80},{80,64},{96,112},{112,96},{1... | collective-permute-start | bytes 196616 | tf_op jit(solution)/shard_map/ppermute | solution.py:224
  99.9 5.1 %collective-permute-start.6 = (f32[128,128]{1,0:T(8,128)S(1)}, f32[128,128]{1,0:T(8,128)S(1)}, u32[]{:S(2)}, u32[]{:S(2)}) collective-permute-start(f32[128,128]{1,0:T(8,128)S(1)} %log_add_fusion.10), channel_id=1, source_target_pairs={{0,224},{16,240},{32,64},{48,80},{64,32},{80,48},{96,128},{112,144... | collective-permute-start | bytes 196616 | tf_op jit(solution)/shard_map/ppermute | solution.py:224
  108.3 4.0 %collective-permute-done.7 = f32[128,128]{1,0:T(8,128)S(1)} collective-permute-done((f32[128,128]{1,0:T(8,128)S(1)}, f32[128,128]{1,0:T(8,128)S(1)}, u32[]{:S(2)}, u32[]{:S(2)}) %collective-permute-start.7) | collective-permute-done | bytes 65568 | tf_op jit(solution)/shard_map/ppermute | solution.py:224
  112.4 3.6 %collective-permute-start.8 = (f32[128,128]{1,0:T(8,128)S(1)}, f32[128,128]{1,0:T(8,128)S(1)}, u32[]{:S(2)}, u32[]{:S(2)}) collective-permute-start(f32[128,128]{1,0:T(8,128)S(1)} %add_subtract_fusion.1), channel_id=1, source_target_pairs={{0,16},{16,0},{32,48},{48,32},{64,80},{80,64},{96,112},{112,96},{1... | collective-permute-start | bytes 196616 | tf_op jit(solution)/shard_map/ppermute | solution.py:224
  118.8 12.5 %all_to_all.31 = f32[16,48,128]{2,1,0:T(8,128)S(1)} all-to-all(f32[16,48,128]{2,1,0:T(8,128)S(1)} %bitcast.28), channel_id=1, replica_groups=mesh['row'=16,'col'=16] {'col'}, dimensions={0} | all-to-all | bytes 786432 | tf_op jit(solution)/shard_map/all_to_all | solution.py:210
  131.3 3.4 %copy-done.1 = bf16[256,1,128,128]{3,2,1,0:T(8,128)(2,1)S(1)} copy-done((bf16[256,1,128,128]{3,2,1,0:T(8,128)(2,1)S(1)}, bf16[256,1,128,128]{3,2,1,0:T(8,128)(2,1)}, u32[]{:S(2)}) %copy-start.1) | copy-done | bytes 8388632
  134.7 6.9 %row_pass.3 = f32[256,128]{1,0:T(8,128)S(1)} custom-call(s32[256]{0:T(256)S(1)} %copy-done.5, bf16[256,128,128]{2,1,0:T(8,128)(2,1)S(1)} %bitcast.21, f32[768,128]{1,0:T(8,128)S(1)} %bitcast.24), custom_call_target="tpu_custom_call" | custom-call | tf_op jit(solution)/shard_map/row_pass/pallas_call | solution.py:109
  141.9 3.5 %collective-permute-done.9 = f32[256,128]{1,0:T(8,128)S(1)} collective-permute-done((f32[256,128]{1,0:T(8,128)S(1)}, f32[256,128]{1,0:T(8,128)S(1)}, u32[]{:S(2)}, u32[]{:S(2)}) %collective-permute-start.9) | collective-permute-done | bytes 131104 | tf_op jit(solution)/shard_map/ppermute | solution.py:224
  146.1 4.5 %collective-permute-done.10 = f32[256,128]{1,0:T(8,128)S(1)} collective-permute-done((f32[256,128]{1,0:T(8,128)S(1)}, f32[256,128]{1,0:T(8,128)S(1)}, u32[]{:S(2)}, u32[]{:S(2)}) %collective-permute-start.10) | collective-permute-done | bytes 131104 | tf_op jit(solution)/shard_map/ppermute | solution.py:224
  150.8 3.8 %collective-permute-done.11 = f32[256,128]{1,0:T(8,128)S(1)} collective-permute-done((f32[256,128]{1,0:T(8,128)S(1)}, f32[256,128]{1,0:T(8,128)S(1)}, u32[]{:S(2)}, u32[]{:S(2)}) %collective-permute-start.11) | collective-permute-done | bytes 131104 | tf_op jit(solution)/shard_map/ppermute | solution.py:224
  155.5 4.3 %collective-permute-done.12 = f32[256,128]{1,0:T(8,128)S(1)} collective-permute-done((f32[256,128]{1,0:T(8,128)S(1)}, f32[256,128]{1,0:T(8,128)S(1)}, u32[]{:S(2)}, u32[]{:S(2)}) %collective-permute-start.12) | collective-permute-done | bytes 131104 | tf_op jit(solution)/shard_map/ppermute | solution.py:224
  159.8 7.4 %col_pass.3 = f32[768,128]{1,0:T(8,128)S(1)} custom-call(s32[256]{0:T(256)S(1)} %copy-done.5, bf16[256,128,128]{2,1,0:T(8,128)(2,1)S(1)} %bitcast.22, f32[256,128]{1,0:T(8,128)S(1)} %bitcast_subtract_fusion.pots_ref), custom_call_target="tpu_custom_call" | custom-call | tf_op jit(solution)/shard_map/col_pass/pallas_call | solution.py:142
  167.3 10.6 %all_to_all.32 = f32[16,48,128]{2,1,0:T(8,128)S(1)} all-to-all(f32[16,48,128]{2,1,0:T(8,128)S(1)} %bitcast.25), channel_id=1, replica_groups=mesh['row'=16,'col'=16] {'col'}, dimensions={0} | all-to-all | bytes 786432 | tf_op jit(solution)/shard_map/all_to_all | solution.py:210
  177.9 2.8 %segment.3 = f32[256,128]{1,0:T(8,128)S(1)} custom-call(s32[768]{0:T(1024)S(1)} %reshape.65.ids_ref, f32[768,128]{1,0:T(8,128)S(1)} %bitcast.27), custom_call_target="tpu_custom_call" | custom-call | tf_op jit(solution)/shard_map/segment/pallas_call | solution.py:197
  180.6 7.4 %collective-permute-start.13 = (f32[128,128]{1,0:T(8,128)S(1)}, f32[128,128]{1,0:T(8,128)S(1)}, u32[]{:S(2)}, u32[]{:S(2)}) collective-permute-start(f32[128,128]{1,0:T(8,128)S(1)} %constant_dynamic-slice_fusion), channel_id=1, source_target_pairs={{0,16},{16,0},{32,48},{48,32},{64,80},{80,64},{96,112},{112,96},{1... | collective-permute-start | bytes 196616 | tf_op jit(solution)/shard_map/ppermute | solution.py:224
  189.0 3.1 %collective-permute-done.14 = f32[128,128]{1,0:T(8,128)S(1)} collective-permute-done((f32[128,128]{1,0:T(8,128)S(1)}, f32[128,128]{1,0:T(8,128)S(1)}, u32[]{:S(2)}, u32[]{:S(2)}) %collective-permute-start.14) | collective-permute-done | bytes 65568 | tf_op jit(solution)/shard_map/ppermute | solution.py:224
  192.2 2.3 %collective-permute-start.15 = (f32[128,128]{1,0:T(8,128)S(1)}, f32[128,128]{1,0:T(8,128)S(1)}, u32[]{:S(2)}, u32[]{:S(2)}) collective-permute-start(f32[128,128]{1,0:T(8,128)S(1)} %log_add_fusion.7), channel_id=1, source_target_pairs={{0,224},{16,240},{32,64},{48,80},{64,32},{80,48},{96,128},{112,144... | collective-permute-start | bytes 196616 | tf_op jit(solution)/shard_map/ppermute | solution.py:224
  198.4 3.3 %collective-permute-done.16 = f32[128,128]{1,0:T(8,128)S(1)} collective-permute-done((f32[128,128]{1,0:T(8,128)S(1)}, f32[128,128]{1,0:T(8,128)S(1)}, u32[]{:S(2)}, u32[]{:S(2)}) %collective-permute-start.16) | collective-permute-done | bytes 65568 | tf_op jit(solution)/shard_map/ppermute | solution.py:224
  201.8 3.9 %collective-permute-start.17 = (f32[128,128]{1,0:T(8,128)S(1)}, f32[128,128]{1,0:T(8,128)S(1)}, u32[]{:S(2)}, u32[]{:S(2)}) collective-permute-start(f32[128,128]{1,0:T(8,128)S(1)} %add_subtract_fusion), channel_id=1, source_target_pairs={{0,16},{16,0},{32,48},{48,32},{64,80},{80,64},{96,112},{112,96},{1... | collective-permute-start | bytes 196616 | tf_op jit(solution)/shard_map/ppermute | solution.py:224
  (61 shorter events, 27.5 us)
Async XLA Ops:
  20.6 0.9 copy-start.3
  21.5 42.1 %copy-start.6 = (f32[32768]{0:T(1024)S(1)}, f32[32768]{0:T(1024)}, u32[]{:S(2)}) copy-start(f32[32768]{0:T(1024)} %param.9) | copy-start | bytes 393220
  34.1 3.4 %copy-start = (bf16[256,1,128,128]{3,2,1,0:T(8,128)(2,1)S(1)}, bf16[256,1,128,128]{3,2,1,0:T(8,128)(2,1)}, u32[]{:S(2)}) copy-start(bf16[256,1,128,128]{3,2,1,0:T(8,128)(2,1)} %param.6) | copy-start | bytes 25165828
  37.4 0.7 copy-start.4
  45.0 67.3 %copy-start.7 = (f32[32768]{0:T(1024)S(1)}, f32[32768]{0:T(1024)}, u32[]{:S(2)}) copy-start(f32[32768]{0:T(1024)} %param.11) | copy-start | bytes 393220
  45.0 67.3 %copy-start.8 = (f32[32768]{0:T(1024)S(1)}, f32[32768]{0:T(1024)}, u32[]{:S(2)}) copy-start(f32[32768]{0:T(1024)} %param.10) | copy-start | bytes 393220
  45.1 86.2 %copy-start.5 = (s32[256]{0:T(256)S(1)}, s32[256]{0:T(256)}, u32[]{:S(2)}) copy-start(s32[256]{0:T(256)} %get-tuple-element.4.slot_ref) | copy-start | bytes 3076
  45.1 3.9 %collective-permute-start = (f32[256,128]{1,0:T(8,128)S(1)}, f32[256,128]{1,0:T(8,128)S(1)}, u32[]{:S(2)}, u32[]{:S(2)}) collective-permute-start(f32[256,128]{1,0:T(8,128)S(1)} %row_pass.2), channel_id=1, source_target_pairs={{0,1},{1,0},{2,3},{3,2},{4,5},{5,4},{6,7},{7,6},{8,9},{9,8},{10,11... | collective-permute-start | bytes 393224 | tf_op jit(solution)/shard_map/ppermute | solution.py:224
  49.0 5.1 %collective-permute-start.1 = (f32[256,128]{1,0:T(8,128)S(1)}, f32[256,128]{1,0:T(8,128)S(1)}, u32[]{:S(2)}, u32[]{:S(2)}) collective-permute-start(f32[256,128]{1,0:T(8,128)S(1)} %log_add_fusion.5), channel_id=1, source_target_pairs={{0,3},{1,2},{2,1},{3,0},{4,7},{5,6},{6,5},{7,4},{8,11},{9,10},{10,... | collective-permute-start | bytes 393224 | tf_op jit(solution)/shard_map/ppermute | solution.py:224
  54.2 4.2 %collective-permute-start.2 = (f32[256,128]{1,0:T(8,128)S(1)}, f32[256,128]{1,0:T(8,128)S(1)}, u32[]{:S(2)}, u32[]{:S(2)}) collective-permute-start(f32[256,128]{1,0:T(8,128)S(1)} %log_add_fusion.4), channel_id=1, source_target_pairs={{0,4},{1,5},{2,6},{3,7},{4,0},{5,1},{6,2},{7,3},{8,12},{9,13},{10,... | collective-permute-start | bytes 393224 | tf_op jit(solution)/shard_map/ppermute | solution.py:224
  58.4 5.1 %collective-permute-start.3 = (f32[256,128]{1,0:T(8,128)S(1)}, f32[256,128]{1,0:T(8,128)S(1)}, u32[]{:S(2)}, u32[]{:S(2)}) collective-permute-start(f32[256,128]{1,0:T(8,128)S(1)} %log_add_fusion.3), channel_id=1, source_target_pairs={{0,12},{1,13},{2,14},{3,15},{4,8},{5,9},{6,10},{7,11},{8,4},{9,5},... | collective-permute-start | bytes 393224 | tf_op jit(solution)/shard_map/ppermute | solution.py:224
  71.8 11.5 %all-to-all-start.2 = ((f32[16,48,128]{2,1,0:T(8,128)}), f32[16,48,128]{2,1,0:T(8,128)S(1)}, u32[]{:S(2)}, u32[]{:S(2)}) async-start(f32[16,48,128]{2,1,0:T(8,128)} %bitcast.7), calls=%async_computation.2 | async-start | bytes 786432 | tf_op jit(solution)/shard_map/all_to_all | solution.py:210
  86.1 9.9 %collective-permute-start.4 = (f32[128,128]{1,0:T(8,128)S(1)}, f32[128,128]{1,0:T(8,128)S(1)}, u32[]{:S(2)}, u32[]{:S(2)}) collective-permute-start(f32[128,128]{1,0:T(8,128)S(1)} %constant_dynamic-slice_fusion.1), channel_id=1, source_target_pairs={{0,16},{16,0},{32,48},{48,32},{64,80},{80,64},{96,112},{112,96},{1... | collective-permute-start | bytes 196616 | tf_op jit(solution)/shard_map/ppermute | solution.py:224
  96.0 3.8 %collective-permute-start.5 = (f32[128,128]{1,0:T(8,128)S(1)}, f32[128,128]{1,0:T(8,128)S(1)}, u32[]{:S(2)}, u32[]{:S(2)}) collective-permute-start(f32[128,128]{1,0:T(8,128)S(1)} %log_add_fusion.11), channel_id=1, source_target_pairs={{0,32},{16,48},{32,0},{48,16},{64,96},{80,112},{96,64},{112,80},{1... | collective-permute-start | bytes 196616 | tf_op jit(solution)/shard_map/ppermute | solution.py:224
  99.9 6.7 %collective-permute-start.6 = (f32[128,128]{1,0:T(8,128)S(1)}, f32[128,128]{1,0:T(8,128)S(1)}, u32[]{:S(2)}, u32[]{:S(2)}) collective-permute-start(f32[128,128]{1,0:T(8,128)S(1)} %log_add_fusion.10), channel_id=1, source_target_pairs={{0,224},{16,240},{32,64},{48,80},{64,32},{80,48},{96,128},{112,144... | collective-permute-start | bytes 196616 | tf_op jit(solution)/shard_map/ppermute | solution.py:224
  106.6 5.7 %collective-permute-start.7 = (f32[128,128]{1,0:T(8,128)S(1)}, f32[128,128]{1,0:T(8,128)S(1)}, u32[]{:S(2)}, u32[]{:S(2)}) collective-permute-start(f32[128,128]{1,0:T(8,128)S(1)} %log_add_fusion.9), channel_id=1, source_target_pairs={{0,96},{16,112},{32,192},{48,208},{64,160},{80,176},{96,0},{112,16... | collective-permute-start | bytes 196616 | tf_op jit(solution)/shard_map/ppermute | solution.py:224
  112.4 4.5 %collective-permute-start.8 = (f32[128,128]{1,0:T(8,128)S(1)}, f32[128,128]{1,0:T(8,128)S(1)}, u32[]{:S(2)}, u32[]{:S(2)}) collective-permute-start(f32[128,128]{1,0:T(8,128)S(1)} %add_subtract_fusion.1), channel_id=1, source_target_pairs={{0,16},{16,0},{32,48},{48,32},{64,80},{80,64},{96,112},{112,96},{1... | collective-permute-start | bytes 196616 | tf_op jit(solution)/shard_map/ppermute | solution.py:224
  131.3 3.4 %copy-start.1 = (bf16[256,1,128,128]{3,2,1,0:T(8,128)(2,1)S(1)}, bf16[256,1,128,128]{3,2,1,0:T(8,128)(2,1)}, u32[]{:S(2)}) copy-start(bf16[256,1,128,128]{3,2,1,0:T(8,128)(2,1)} %param.6) | copy-start | bytes 25165828
  141.6 3.9 %collective-permute-start.9 = (f32[256,128]{1,0:T(8,128)S(1)}, f32[256,128]{1,0:T(8,128)S(1)}, u32[]{:S(2)}, u32[]{:S(2)}) collective-permute-start(f32[256,128]{1,0:T(8,128)S(1)} %row_pass.3), channel_id=1, source_target_pairs={{0,1},{1,0},{2,3},{3,2},{4,5},{5,4},{6,7},{7,6},{8,9},{9,8},{10,11... | collective-permute-start | bytes 393224 | tf_op jit(solution)/shard_map/ppermute | solution.py:224
  145.5 5.1 %collective-permute-start.10 = (f32[256,128]{1,0:T(8,128)S(1)}, f32[256,128]{1,0:T(8,128)S(1)}, u32[]{:S(2)}, u32[]{:S(2)}) collective-permute-start(f32[256,128]{1,0:T(8,128)S(1)} %log_add_fusion.2), channel_id=1, source_target_pairs={{0,3},{1,2},{2,1},{3,0},{4,7},{5,6},{6,5},{7,4},{8,11},{9,10},{10,... | collective-permute-start | bytes 393224 | tf_op jit(solution)/shard_map/ppermute | solution.py:224
  150.7 3.9 %collective-permute-start.11 = (f32[256,128]{1,0:T(8,128)S(1)}, f32[256,128]{1,0:T(8,128)S(1)}, u32[]{:S(2)}, u32[]{:S(2)}) collective-permute-start(f32[256,128]{1,0:T(8,128)S(1)} %log_add_fusion.1), channel_id=1, source_target_pairs={{0,4},{1,5},{2,6},{3,7},{4,0},{5,1},{6,2},{7,3},{8,12},{9,13},{10,... | collective-permute-start | bytes 393224 | tf_op jit(solution)/shard_map/ppermute | solution.py:224
  154.7 5.1 %collective-permute-start.12 = (f32[256,128]{1,0:T(8,128)S(1)}, f32[256,128]{1,0:T(8,128)S(1)}, u32[]{:S(2)}, u32[]{:S(2)}) collective-permute-start(f32[256,128]{1,0:T(8,128)S(1)} %log_add_fusion), channel_id=1, source_target_pairs={{0,12},{1,13},{2,14},{3,15},{4,8},{5,9},{6,10},{7,11},{8,4},{9,5},... | collective-permute-start | bytes 393224 | tf_op jit(solution)/shard_map/ppermute | solution.py:224
  159.8 47.5 %copy-start.2 = (f32[256,128]{1,0:T(8,128)}, f32[256,128]{1,0:T(8,128)S(1)}, u32[]{:S(2)}) copy-start(f32[256,128]{1,0:T(8,128)S(1)} %bitcast_subtract_fusion.pots_ref) | copy-start | bytes 393220
  180.6 8.3 %collective-permute-start.13 = (f32[128,128]{1,0:T(8,128)S(1)}, f32[128,128]{1,0:T(8,128)S(1)}, u32[]{:S(2)}, u32[]{:S(2)}) collective-permute-start(f32[128,128]{1,0:T(8,128)S(1)} %constant_dynamic-slice_fusion), channel_id=1, source_target_pairs={{0,16},{16,0},{32,48},{48,32},{64,80},{80,64},{96,112},{112,96},{1... | collective-permute-start | bytes 196616 | tf_op jit(solution)/shard_map/ppermute | solution.py:224
  188.9 3.2 %collective-permute-start.14 = (f32[128,128]{1,0:T(8,128)S(1)}, f32[128,128]{1,0:T(8,128)S(1)}, u32[]{:S(2)}, u32[]{:S(2)}) collective-permute-start(f32[128,128]{1,0:T(8,128)S(1)} %log_add_fusion.8), channel_id=1, source_target_pairs={{0,32},{16,48},{32,0},{48,16},{64,96},{80,112},{96,64},{112,80},{1... | collective-permute-start | bytes 196616 | tf_op jit(solution)/shard_map/ppermute | solution.py:224
  192.2 4.4 %collective-permute-start.15 = (f32[128,128]{1,0:T(8,128)S(1)}, f32[128,128]{1,0:T(8,128)S(1)}, u32[]{:S(2)}, u32[]{:S(2)}) collective-permute-start(f32[128,128]{1,0:T(8,128)S(1)} %log_add_fusion.7), channel_id=1, source_target_pairs={{0,224},{16,240},{32,64},{48,80},{64,32},{80,48},{96,128},{112,144... | collective-permute-start | bytes 196616 | tf_op jit(solution)/shard_map/ppermute | solution.py:224
  196.6 5.1 %collective-permute-start.16 = (f32[128,128]{1,0:T(8,128)S(1)}, f32[128,128]{1,0:T(8,128)S(1)}, u32[]{:S(2)}, u32[]{:S(2)}) collective-permute-start(f32[128,128]{1,0:T(8,128)S(1)} %log_add_fusion.6), channel_id=1, source_target_pairs={{0,96},{16,112},{32,192},{48,208},{64,160},{80,176},{96,0},{112,16... | collective-permute-start | bytes 196616 | tf_op jit(solution)/shard_map/ppermute | solution.py:224
  201.8 4.8 %collective-permute-start.17 = (f32[128,128]{1,0:T(8,128)S(1)}, f32[128,128]{1,0:T(8,128)S(1)}, u32[]{:S(2)}, u32[]{:S(2)}) collective-permute-start(f32[128,128]{1,0:T(8,128)S(1)} %add_subtract_fusion), channel_id=1, source_target_pairs={{0,16},{16,0},{32,48},{48,32},{64,80},{80,64},{96,112},{112,96},{1... | collective-permute-start | bytes 196616 | tf_op jit(solution)/shard_map/ppermute | solution.py:224

commit v2 on v1

v2 whole, which is shorter than its diff:
```python
import functools

import jax
import jax.numpy as jnp
from jax import lax
from jax.experimental import pallas as pl
from jax.experimental.pallas import tpu as pltpu
from jax.sharding import PartitionSpec as P

ITERS = 2
NEGATIVE = -1e30
VMEM = pltpu.VMEM
SMEM = pltpu.SMEM
VMEM_BYTES = 48 << 20
CHUNKS = 4
UNROLL = 64
EXTRA = 8


def spec(space):
    return pl.BlockSpec(memory_space=space)


def params():
    return pltpu.CompilerParams(vmem_limit_bytes=VMEM_BYTES)


def plan(cols, block_tiles, owners, width):
    owner = cols // block_tiles
    local = cols % block_tiles
    order = jnp.arange(cols.shape[0])
    before = (owner[:, None] == owner[None, :]) & (order[None, :] < order[:, None])
    rank = jnp.sum(before.astype(jnp.int32), axis=1)
    lane = (owner * width + rank)[:, None] == jnp.arange(owners * width)[None, :]
    ask = block_tiles + jnp.sum(jnp.where(lane, local[:, None] - block_tiles, 0), axis=0)
    return owner, local, rank, ask.reshape(owners, width).astype(jnp.float32)


def stream(tiles_ref, held_ref, sems):
    count = tiles_ref.shape[0]
    parts = count // UNROLL
    size = UNROLL // CHUNKS

    def copy(g, i):
        at = pl.ds(g * UNROLL + i * size, size)
        return pltpu.make_async_copy(tiles_ref.at[at], held_ref.at[at], sems.at[g, i])

    for g in range(parts):
        for i in range(CHUNKS):
            copy(g, i).start()

    def ready(g):
        for i in range(CHUNKS):
            copy(g, i).wait()

    return ready


def stream_scratch(tiles):
    return [
        VMEM(tiles.shape, tiles.dtype),
        pltpu.SemaphoreType.DMA((tiles.shape[0] // UNROLL, CHUNKS)),
    ]


def pick_kernel(ids_ref, rows_ref, out_ref):
    last = rows_ref.shape[0] - 1
    turn = 48

    def step(p, carry):
        for k in range(turn):
            row = jnp.minimum(ids_ref[p * turn + k], last)
            out_ref[pl.ds(p * turn + k, 1), :] = rows_ref[pl.ds(row, 1), :]
        return carry

    lax.fori_loop(0, out_ref.shape[0] // turn, step, 0)


def pick(ids, rows):
    return pl.pallas_call(
        pick_kernel,
        name="pick",
        out_shape=jax.ShapeDtypeStruct((ids.shape[0], rows.shape[1]), jnp.float32),
        in_specs=[spec(SMEM), spec(VMEM)],
        out_specs=spec(VMEM),
        compiler_params=params(),
    )(ids, rows)


def row_kernel(slot_ref, tiles_ref, *refs):
    *pots_refs, out_ref, held_ref, sems = refs
    size = pots_refs[0].shape[0]
    ready = stream(tiles_ref, held_ref, sems)

    def potential(slot):
        if len(pots_refs) == 1:
            return pots_refs[0][pl.ds(slot, 1), :]
        side = slot // size
        near, far = (ref[pl.ds(slot - side * size, 1), :] for ref in pots_refs)
        return jnp.where(side == 0, near, far)

    def step(g, carry):
        ready(g)
        tops, sums = [], []
        for k in range(UNROLL):
            n = g * UNROLL + k
            pot = potential(slot_ref[n])
            scores = jnp.transpose(held_ref[n].astype(jnp.float32) + pot)
            top = jnp.max(scores, axis=0, keepdims=True)
            tops.append(top)
            sums.append(jnp.sum(jnp.exp(scores - top), axis=0, keepdims=True))
        block = pl.ds(pl.multiple_of(g * UNROLL, UNROLL), UNROLL)
        out_ref[block, :] = jnp.concatenate(tops, 0) + jnp.log(jnp.concatenate(sums, 0))
        return carry

    lax.fori_loop(0, tiles_ref.shape[0] // UNROLL, step, 0)


def row_pass(slot, tiles, *pots):
    return pl.pallas_call(
        row_kernel,
        name="row_pass",
        out_shape=jax.ShapeDtypeStruct(tiles.shape[:2], jnp.float32),
        in_specs=[spec(SMEM), spec(pltpu.HBM)] + [spec(VMEM)] * len(pots),
        out_specs=spec(VMEM),
        scratch_shapes=stream_scratch(tiles),
        compiler_params=params(),
    )(slot, tiles, *pots)


def col_kernel(capacity, slot_ref, tiles_ref, pots_ref, *refs):
    *ask_refs, out_ref, row_ref, held_ref, sems = refs
    ready = stream(tiles_ref, held_ref, sems)
    out_ref[...] = jnp.full(out_ref.shape, NEGATIVE, jnp.float32)
    width = tiles_ref.shape[1]
    for ask_ref in ask_refs:
        for owner in range(ask_ref.shape[0]):
            row = owner * (capacity + EXTRA) + capacity
            out_ref[row : row + 1, :] = ask_ref[owner : owner + 1, :]

    def step(g, carry):
        ready(g)
        tops, sums = [], []
        for k in range(UNROLL):
            n = g * UNROLL + k
            pot = jnp.broadcast_to(pots_ref[pl.ds(n, 1), :], (width, width))
            scores = held_ref[n].astype(jnp.float32) + jnp.transpose(pot)
            top = jnp.max(scores, axis=0, keepdims=True)
            tops.append(top)
            sums.append(jnp.sum(jnp.exp(scores - top), axis=0, keepdims=True))
        row_ref[...] = jnp.concatenate(tops, 0) + jnp.log(jnp.concatenate(sums, 0))
        for k in range(UNROLL):
            out_ref[pl.ds(slot_ref[g * UNROLL + k], 1), :] = row_ref[pl.ds(k, 1), :]
        return carry

    lax.fori_loop(0, tiles_ref.shape[0] // UNROLL, step, 0)


def col_pass(slot, tiles, pots, slots, capacity, *ask):
    width = tiles.shape[1]
    return pl.pallas_call(
        functools.partial(col_kernel, capacity),
        name="col_pass",
        out_shape=jax.ShapeDtypeStruct((slots, width), jnp.float32),
        in_specs=[spec(SMEM), spec(pltpu.HBM)] + [spec(VMEM)] * (1 + len(ask)),
        out_specs=spec(VMEM),
        scratch_shapes=[VMEM((UNROLL, width), jnp.float32)] + stream_scratch(tiles),
        compiler_params=params(),
    )(slot, tiles, pots, *ask)


def segment_kernel(capacity, ids_ref, rows_ref, out_ref, top_ref, *parts):
    sources = ids_ref.shape[0] // capacity
    stride = rows_ref.shape[0] // sources
    groups = len(parts)
    turns = sources // groups

    def walk(visit):
        for turn in range(turns):

            def step(p, carry):
                for k in range(4):
                    for g, part in enumerate(parts):
                        source = g * turns + turn
                        rank = p * 4 + k
                        visit(
                            part,
                            pl.ds(ids_ref[source * capacity + rank], 1),
                            rows_ref[pl.ds(source * stride + rank, 1), :],
                        )
                return carry

            lax.fori_loop(0, capacity // 4, step, 0)

    for part in parts:
        part[...] = jnp.full(part.shape, NEGATIVE, jnp.float32)

    def highest(part, here, row):
        part[here, :] = jnp.maximum(part[here, :], row)

    walk(highest)
    top = parts[0][...]
    for part in parts[1:]:
        top = jnp.maximum(top, part[...])
    top_ref[...] = top
    for part in parts:
        part[...] = jnp.zeros(part.shape, jnp.float32)

    def add(part, here, row):
        part[here, :] = part[here, :] + jnp.exp(row - top_ref[here, :])

    walk(add)
    total = parts[0][...]
    for part in parts[1:]:
        total = total + part[...]
    count = out_ref.shape[0]
    total = total[:count]
    some = total > 0.0
    out_ref[...] = jnp.where(
        some, top_ref[:count, :] + jnp.log(jnp.where(some, total, 1.0)), NEGATIVE
    )


def segment(ids, rows, count, capacity):
    width = rows.shape[1]
    return pl.pallas_call(
        functools.partial(segment_kernel, capacity),
        name="segment",
        out_shape=jax.ShapeDtypeStruct((count, width), jnp.float32),
        in_specs=[spec(SMEM), spec(VMEM)],
        out_specs=spec(VMEM),
        scratch_shapes=[VMEM((count + 8, width), jnp.float32)] * 9,
        compiler_params=params(),
    )(ids, rows)


def exchange(value, owners):
    shape = value.shape
    return lax.all_to_all(
        value.reshape((owners, shape[0] // owners) + shape[1:]),
        "col",
        split_axis=0,
        concat_axis=0,
        tiled=True,
    ).reshape(shape)


def log_sum(first, *others):
    top = functools.reduce(jnp.maximum, others, first)
    return top + jnp.log(sum(jnp.exp(value - top) for value in (first, *others)))


def swap(value, axis, partner):
    return lax.ppermute(value, axis, [(j, i) for i, j in enumerate(partner)])


def col_phases(count):
    def near(i, step):
        return i - i % 4 + (i + step) % 4

    def far(i, step):
        return (i + 4 * step) % count

    return [[[move(i, step) for i in range(count)] for step in (1, 3, 2)] for move in (near, far)]


def row_phases(count):
    phases = (
        ([1, 0, 3, 2, 5, 4, 7, 6],),
        ([7, 2, 1, 4, 3, 6, 5, 0], [2, 7, 4, 1, 6, 3, 0, 5], [5, 4, 7, 6, 1, 0, 3, 2]),
    )
    return [[[2 * z[i // 2] + i % 2 for i in range(count)] for z in phase] for phase in phases]


def body(kernel, tile_cols, start_pot, log_source, log_target, dustbin):
    row_tiles, local_slots, width, _ = kernel.shape
    owners = lax.axis_size("col")
    block_tiles = start_pot.shape[0] // width
    tile_count = row_tiles * local_slots
    capacity = min(tile_count // 2, 3 * tile_count // owners)
    half = block_tiles // 2
    core = lax.axis_index("row") % 2
    other_core = [i ^ 1 for i in range(lax.axis_size("row"))]

    source_rows = log_source.reshape(row_tiles, width)

    def mine(value, side):
        return lax.dynamic_slice_in_dim(value, side * half, half, 0)

    start_half = mine(start_pot.reshape(block_tiles, width), core)
    target_half = mine(log_target.reshape(block_tiles, width), core)
    dust_half = mine(dustbin.reshape(block_tiles, width), core)

    tiles = kernel.reshape(tile_count, width, width)
    owner, local, rank, ask = plan(tile_cols.reshape(tile_count), block_tiles, owners, width)
    side = local // half
    place = (side ^ core) * (owners * half) + owner * half + local - side * half
    near = exchange(jnp.tile(start_half, (owners, 1)), owners)
    far = swap(near, "row", other_core)
    for repeat in range(ITERS):
        if repeat == 0:
            row_lse = row_pass(place, tiles, near, far)
        else:
            row_lse = row_pass(
                owner * capacity + rank, tiles, exchange(pick(ids, target_now), owners)
            )
        for phase in col_phases(owners):
            row_lse = log_sum(row_lse, *[swap(row_lse, "col", partner) for partner in phase])
        source_now = source_rows - row_lse
        if repeat == 0:
            stride = capacity + EXTRA
            rows = col_pass(
                owner * stride + rank, tiles, source_now, owners * stride, capacity, ask
            )
            rows = exchange(rows, owners)
            ids = rows.reshape(owners, stride, width)[:, capacity, :capacity]
            ids = ids.astype(jnp.int32).reshape(owners * capacity)
        else:
            rows = col_pass(
                owner * capacity + rank, tiles, source_now, owners * capacity, capacity
            )
            rows = exchange(rows, owners)
        part = segment(ids, rows, block_tiles, capacity)
        col_lse = log_sum(mine(part, core), swap(mine(part, 1 - core), "row", other_core))
        for phase in row_phases(len(other_core)):
            col_lse = log_sum(col_lse, *[swap(col_lse, "row", partner) for partner in phase])
        here = target_half - log_sum(col_lse, dust_half)
        there = swap(here, "row", other_core)
        target_now = jnp.where(
            core == 0, jnp.concatenate([here, there]), jnp.concatenate([there, here])
        )
    return source_now.reshape(log_source.shape), target_now.reshape(start_pot.shape)


def solution(mesh):
    placed = (P("row", "col", None, None), P("row", "col"), P("col"), P("row"), P("col"), P("col"))
    return jax.shard_map(
        body, mesh=mesh, in_specs=placed, out_specs=(P("row"), P("col")), check_vma=False
    )
```

time: 208 us -> 185 us (0.89)
  waiting for transfers between devices: 60 us -> 49.4 us
  local copies, waits for them, and re-layouts: 9.76 us -> 1.1 us
  Pallas kernels: 42.7 us -> 36.5 us
    ppermute x18 -> x25, waiting for transfers between devices: 52.1 us -> 40.8 us  [swap(): return lax.ppermute(value, axis, [(j, i) for i, j in enumerate(partner)])]
    unnamed x18 -> x12, local copies, waits for them, and re-layouts: 8.38 us -> 0.9 us
    pallas_call x5 -> x4, Pallas kernels: 25.2 us -> 20.6 us  [the longest x2 15.1 us: col_pass(): pl.pallas_call(functools.partial(col_kernel, capacity), name='col_pass',...]
    all_to_all x4 -> x3, blocking collectives: 47.6 us -> 49.3 us  [exchange(): lax.all_to_all(value.reshape((owners, shape[0] // owners) + shape[1:]), '...]
    ppermute x18 -> x25, starting transfers between devices: 40.7 us -> 40.6 us  [swap(): return lax.ppermute(value, axis, [(j, i) for i, j in enumerate(partner)])]
  transfers between devices with their start and end apart: 19 -> 26, of which waited for: 19 -> 22; matrix products, arithmetic and copies ran while one was open for 0% -> 0% of each run, Pallas kernels for 0% -> 0%
where the time goes in v2:
time: 185 us
  waiting for transfers between devices  49.4 us (27%)
  blocking collectives  49.3 us (27%)
  starting transfers between devices  45.4 us (25%)
  Pallas kernels  36.5 us (20%)
  other arithmetic  2.07 us (1%)
    all_to_all x3, blocking collectives, exchange(): lax.all_to_all(value.reshape((owners, shape[0] // owners) + shape[1:]), '...  49.3 us
    ppermute x25, waiting for transfers between devices, swap(): return lax.ppermute(value, axis, [(j, i) for i, j in enumerate(partner)])  40.8 us
    ppermute x25, starting transfers between devices, swap(): return lax.ppermute(value, axis, [(j, i) for i, j in enumerate(partner)])  40.6 us
    pallas_call x2, Pallas kernels, col_pass(): pl.pallas_call(functools.partial(col_kernel, capacity), name='col_pass',...  15.1 us
    pallas_call x2, Pallas kernels, row_pass(): pl.pallas_call(row_kernel, name='row_pass', out_shape=jax.ShapeDtypeStruc...  14.2 us
    all_to_all x1, waiting for transfers between devices, exchange(): lax.all_to_all(value.reshape((owners, shape[0] // owners) + shape[1:]), '...  8.62 us
    pallas_call x2, Pallas kernels, segment(): pl.pallas_call(functools.partial(segment_kernel, capacity), name='segment...  5.51 us
    all_to_all x1, starting transfers between devices, exchange(): lax.all_to_all(value.reshape((owners, shape[0] // owners) + shape[1:]), '...  4.81 us
  transfers between devices with their start and end apart: 26, of which 22 were waited for; matrix products, arithmetic and copies ran while one was open for 0% of the time, Pallas kernels for 0%

profile of v2, /device:TPU:1, one launch (start us, length us, event | category | flops | bytes accessed | tf_op | source)
XLA Modules:
  0.0 184.6 jit_solution(12021631225393520915)
XLA Ops:
  1.6 23.3 %all_to_all.20 = f32[16,128,128]{2,1,0:T(8,128)S(1)} all-to-all(f32[16,128,128]{2,1,0:T(8,128)S(1)} %reshape_tile.3), channel_id=1, replica_groups=mesh['row'=16,'col'=16] {'col'}, dimensions={0} | all-to-all | bytes 2097152 | tf_op jit(solution)/shard_map/all_to_all | solution.py:239
  24.9 1.9 %collective-permute-start = (f32[2048,128]{1,0:T(8,128)S(1)}, f32[2048,128]{1,0:T(8,128)S(1)}, u32[]{:S(2)}, u32[]{:S(2)}) collective-permute-start(f32[2048,128]{1,0:T(8,128)S(1)} %bitcast.25), channel_id=1, source_target_pairs={{16,0},{0,16},{48,32},{32,48},{80,64},{64,80},{112,96},{96,112},{1... | collective-permute-start | bytes 3145736 | tf_op jit(solution)/shard_map/ppermute | solution.py:254
  27.4 1.7 collective-permute-done.refs_1_
  29.1 7.2 %row_pass.2 = f32[256,128]{1,0:T(8,128)S(1)} custom-call(s32[256]{0:T(256)S(1)} %get-tuple-element.4.slot_ref, bf16[256,128,128]{2,1,0:T(8,128)(2,1)} %bitcast.33, f32[2048,128]{1,0:T(8,128)S(1)} %bitcast.26, f32[2048,128]{1,0:T(8,128)S(1)} %collective-permute-done.refs_1_), custom_call_target="tpu_custom_call" | custom-call | tf_op jit(solution)/shard_map/row_pass/pallas_call | solution.py:120
  39.1 2.1 %collective-permute-done.1 = f32[256,128]{1,0:T(8,128)S(1)} collective-permute-done((f32[256,128]{1,0:T(8,128)S(1)}, f32[256,128]{1,0:T(8,128)S(1)}, u32[]{:S(2)}, u32[]{:S(2)}) %collective-permute-start.1) | collective-permute-done | bytes 131104 | tf_op jit(solution)/shard_map/ppermute | solution.py:254
  41.1 2.2 %collective-permute-done.2 = f32[256,128]{1,0:T(8,128)S(1)} collective-permute-done((f32[256,128]{1,0:T(8,128)S(1)}, f32[256,128]{1,0:T(8,128)S(1)}, u32[]{:S(2)}, u32[]{:S(2)}) %collective-permute-start.2) | collective-permute-done | bytes 131104 | tf_op jit(solution)/shard_map/ppermute | solution.py:254
  48.8 4.1 %collective-permute-done.5 = f32[256,128]{1,0:T(8,128)S(1)} collective-permute-done((f32[256,128]{1,0:T(8,128)S(1)}, f32[256,128]{1,0:T(8,128)S(1)}, u32[]{:S(2)}, u32[]{:S(2)}) %collective-permute-start.5) | collective-permute-done | bytes 131104 | tf_op jit(solution)/shard_map/ppermute | solution.py:254
  53.1 7.9 %col_pass.2 = f32[896,128]{1,0:T(8,128)} custom-call(s32[256]{0:T(256)S(1)} %get-tuple-element.6.slot_ref, bf16[256,128,128]{2,1,0:T(8,128)(2,1)} %bitcast.34, f32[256,128]{1,0:T(8,128)S(1)} %bitcast_subtract_fusion.1.pots_ref, f32[16,128]{1,0:T(8,128)S(1)} %convert_bitcast_fusion.refs_0_), custom_call_target="tpu_custom_call" | custom-call | tf_op jit(solution)/shard_map/col_pass/pallas_call | solution.py:161
  61.0 4.8 %all-to-all-start.1 = ((f32[16,56,128]{2,1,0:T(8,128)}), f32[16,56,128]{2,1,0:T(8,128)S(1)}, u32[]{:S(2)}, u32[]{:S(2)}) async-start(f32[16,56,128]{2,1,0:T(8,128)} %bitcast.10), calls=%async_computation.1 | async-start | bytes 917504 | tf_op jit(solution)/shard_map/all_to_all | solution.py:239
  65.9 8.6 %all-to-all-done.1 = f32[16,56,128]{2,1,0:T(8,128)S(1)} async-done(((f32[16,56,128]{2,1,0:T(8,128)}), f32[16,56,128]{2,1,0:T(8,128)S(1)}, u32[]{:S(2)}, u32[]{:S(2)}) %all-to-all-start.1) | async-done | bytes 458784 | tf_op jit(solution)/shard_map/all_to_all | solution.py:239
  74.6 2.8 %segment.2 = f32[256,128]{1,0:T(8,128)S(1)} custom-call(s32[768]{0:T(1024)S(1)} %convert_element_type.19.ids_ref, f32[896,128]{1,0:T(8,128)S(1)} %bitcast.27), custom_call_target="tpu_custom_call" | custom-call | tf_op jit(solution)/shard_map/segment/pallas_call | solution.py:226
  77.4 4.1 %collective-permute-start.7 = (f32[128,128]{1,0:T(8,128)S(1)}, f32[128,128]{1,0:T(8,128)S(1)}, u32[]{:S(2)}, u32[]{:S(2)}) collective-permute-start(f32[128,128]{1,0:T(8,128)S(1)} %constant_dynamic-slice_fusion.1), channel_id=1, source_target_pairs={{16,0},{0,16},{48,32},{32,48},{80,64},{64,80},{112,96},{96,112},{1... | collective-permute-start | bytes 196616 | tf_op jit(solution)/shard_map/ppermute | solution.py:254
  82.4 1.7 collective-permute-start.8
  84.2 2.1 %collective-permute-done.8 = f32[128,128]{1,0:T(8,128)S(1)} collective-permute-done((f32[128,128]{1,0:T(8,128)S(1)}, f32[128,128]{1,0:T(8,128)S(1)}, u32[]{:S(2)}, u32[]{:S(2)}) %collective-permute-start.8) | collective-permute-done | bytes 65568 | tf_op jit(solution)/shard_map/ppermute | solution.py:254
  86.3 5.5 %collective-permute-start.10 = (f32[128,128]{1,0:T(8,128)S(1)}, f32[128,128]{1,0:T(8,128)S(1)}, u32[]{:S(2)}, u32[]{:S(2)}) collective-permute-start(f32[128,128]{1,0:T(8,128)S(1)} %log_add_fusion.4), channel_id=1, source_target_pairs={{64,0},{80,16},{224,32},{240,48},{128,64},{144,80},{32,96},{48,112... | collective-permute-start | bytes 196616 | tf_op jit(solution)/shard_map/ppermute | solution.py:254
  91.8 1.6 collective-permute-start.11
  93.4 4.6 %collective-permute-done.11 = f32[128,128]{1,0:T(8,128)S(1)} collective-permute-done((f32[128,128]{1,0:T(8,128)S(1)}, f32[128,128]{1,0:T(8,128)S(1)}, u32[]{:S(2)}, u32[]{:S(2)}) %collective-permute-start.11) | collective-permute-done | bytes 65568 | tf_op jit(solution)/shard_map/ppermute | solution.py:254
  98.6 3.2 %collective-permute-start.12 = (f32[128,128]{1,0:T(8,128)S(1)}, f32[128,128]{1,0:T(8,128)S(1)}, u32[]{:S(2)}, u32[]{:S(2)}) collective-permute-start(f32[128,128]{1,0:T(8,128)S(1)} %add_subtract_fusion.1), channel_id=1, source_target_pairs={{16,0},{0,16},{48,32},{32,48},{80,64},{64,80},{112,96},{96,112},{1... | collective-permute-start | bytes 196616 | tf_op jit(solution)/shard_map/ppermute | solution.py:254
  102.7 1.7 pick.1
  104.4 12.2 %all_to_all.21 = f32[16,48,128]{2,1,0:T(8,128)S(1)} all-to-all(f32[16,48,128]{2,1,0:T(8,128)S(1)} %bitcast.31), channel_id=1, replica_groups=mesh['row'=16,'col'=16] {'col'}, dimensions={0} | all-to-all | bytes 786432 | tf_op jit(solution)/shard_map/all_to_all | solution.py:239
  116.6 7.0 %row_pass.3 = f32[256,128]{1,0:T(8,128)S(1)} custom-call(s32[256]{0:T(256)S(1)} %get-tuple-element.7.slot_ref, bf16[256,128,128]{2,1,0:T(8,128)(2,1)} %bitcast.35, f32[768,128]{1,0:T(8,128)S(1)} %bitcast.28), custom_call_target="tpu_custom_call" | custom-call | tf_op jit(solution)/shard_map/row_pass/pallas_call | solution.py:120
  127.6 2.2 %collective-permute-done.14 = f32[256,128]{1,0:T(8,128)S(1)} collective-permute-done((f32[256,128]{1,0:T(8,128)S(1)}, f32[256,128]{1,0:T(8,128)S(1)}, u32[]{:S(2)}, u32[]{:S(2)}) %collective-permute-start.14) | collective-permute-done | bytes 131104 | tf_op jit(solution)/shard_map/ppermute | solution.py:254
  129.8 1.7 collective-permute-done.15
  135.5 3.3 %collective-permute-done.17 = f32[256,128]{1,0:T(8,128)S(1)} collective-permute-done((f32[256,128]{1,0:T(8,128)S(1)}, f32[256,128]{1,0:T(8,128)S(1)}, u32[]{:S(2)}, u32[]{:S(2)}) %collective-permute-start.17) | collective-permute-done | bytes 131104 | tf_op jit(solution)/shard_map/ppermute | solution.py:254
  138.9 7.1 %col_pass.3 = f32[768,128]{1,0:T(8,128)S(1)} custom-call(s32[256]{0:T(256)S(1)} %get-tuple-element.7.slot_ref, bf16[256,128,128]{2,1,0:T(8,128)(2,1)} %bitcast.36, f32[256,128]{1,0:T(8,128)S(1)} %bitcast_subtract_fusion.pots_ref), custom_call_target="tpu_custom_call" | custom-call | tf_op jit(solution)/shard_map/col_pass/pallas_call | solution.py:161
  146.1 13.8 %all_to_all.22 = f32[16,48,128]{2,1,0:T(8,128)S(1)} all-to-all(f32[16,48,128]{2,1,0:T(8,128)S(1)} %bitcast.29), channel_id=1, replica_groups=mesh['row'=16,'col'=16] {'col'}, dimensions={0} | all-to-all | bytes 786432 | tf_op jit(solution)/shard_map/all_to_all | solution.py:239
  159.9 2.8 %segment.3 = f32[256,128]{1,0:T(8,128)S(1)} custom-call(s32[768]{0:T(1024)S(1)} %convert_element_type.19.ids_ref, f32[768,128]{1,0:T(8,128)S(1)} %bitcast.30), custom_call_target="tpu_custom_call" | custom-call | tf_op jit(solution)/shard_map/segment/pallas_call | solution.py:226
  162.7 4.1 %collective-permute-start.19 = (f32[128,128]{1,0:T(8,128)S(1)}, f32[128,128]{1,0:T(8,128)S(1)}, u32[]{:S(2)}, u32[]{:S(2)}) collective-permute-start(f32[128,128]{1,0:T(8,128)S(1)} %constant_dynamic-slice_fusion), channel_id=1, source_target_pairs={{16,0},{0,16},{48,32},{32,48},{80,64},{64,80},{112,96},{96,112},{1... | collective-permute-start | bytes 196616 | tf_op jit(solution)/shard_map/ppermute | solution.py:254
  167.8 3.1 %collective-permute-done.20 = f32[128,128]{1,0:T(8,128)S(1)} collective-permute-done((f32[128,128]{1,0:T(8,128)S(1)}, f32[128,128]{1,0:T(8,128)S(1)}, u32[]{:S(2)}, u32[]{:S(2)}) %collective-permute-start.20) | collective-permute-done | bytes 65568 | tf_op jit(solution)/shard_map/ppermute | solution.py:254
  173.3 2.5 %collective-permute-start.23 = (f32[128,128]{1,0:T(8,128)S(1)}, f32[128,128]{1,0:T(8,128)S(1)}, u32[]{:S(2)}, u32[]{:S(2)}) collective-permute-start(f32[128,128]{1,0:T(8,128)S(1)} %log_add_fusion.2), channel_id=1, source_target_pairs={{160,0},{176,16},{128,32},{144,48},{224,64},{240,80},{192,96},{208... | collective-permute-start | bytes 196616 | tf_op jit(solution)/shard_map/ppermute | solution.py:254
  176.4 3.4 %collective-permute-done.23 = f32[128,128]{1,0:T(8,128)S(1)} collective-permute-done((f32[128,128]{1,0:T(8,128)S(1)}, f32[128,128]{1,0:T(8,128)S(1)}, u32[]{:S(2)}, u32[]{:S(2)}) %collective-permute-start.23) | collective-permute-done | bytes 65568 | tf_op jit(solution)/shard_map/ppermute | solution.py:254
  180.0 3.1 %collective-permute-start.24 = (f32[128,128]{1,0:T(8,128)S(1)}, f32[128,128]{1,0:T(8,128)S(1)}, u32[]{:S(2)}, u32[]{:S(2)}) collective-permute-start(f32[128,128]{1,0:T(8,128)S(1)} %add_subtract_fusion), channel_id=1, source_target_pairs={{16,0},{0,16},{48,32},{32,48},{80,64},{64,80},{112,96},{96,112},{1... | collective-permute-start | bytes 196616 | tf_op jit(solution)/shard_map/ppermute | solution.py:254
  (68 shorter events, 26.2 us)
Async XLA Ops:
  0.6 0.9 copy-start
  0.6 26.2 %copy-start.5 = (s32[256,1]{0,1:T(1,128)S(1)}, s32[256,1]{0,1:T(1,128)}, u32[]{:S(2)}) copy-start(s32[256,1]{0,1:T(1,128)} %param.7) | copy-start | bytes 3076
  24.9 4.2 %collective-permute-start = (f32[2048,128]{1,0:T(8,128)S(1)}, f32[2048,128]{1,0:T(8,128)S(1)}, u32[]{:S(2)}, u32[]{:S(2)}) collective-permute-start(f32[2048,128]{1,0:T(8,128)S(1)} %bitcast.25), channel_id=1, source_target_pairs={{16,0},{0,16},{48,32},{32,48},{80,64},{64,80},{112,96},{96,112},{1... | collective-permute-start | bytes 3145736 | tf_op jit(solution)/shard_map/ppermute | solution.py:254
  29.1 23.9 %copy-start.2 = (f32[32768]{0:T(1024)S(1)}, f32[32768]{0:T(1024)}, u32[]{:S(2)}) copy-start(f32[32768]{0:T(1024)} %param.9) | copy-start | bytes 393220
  36.3 4.8 %collective-permute-start.1 = (f32[256,128]{1,0:T(8,128)S(1)}, f32[256,128]{1,0:T(8,128)S(1)}, u32[]{:S(2)}, u32[]{:S(2)}) collective-permute-start(f32[256,128]{1,0:T(8,128)S(1)} %row_pass.2), channel_id=1, source_target_pairs={{1,0},{2,1},{3,2},{0,3},{5,4},{6,5},{7,6},{4,7},{9,8},{10,9},{11,1... | collective-permute-start | bytes 393224 | tf_op jit(solution)/shard_map/ppermute | solution.py:254
  37.1 6.3 %collective-permute-start.2 = (f32[256,128]{1,0:T(8,128)S(1)}, f32[256,128]{1,0:T(8,128)S(1)}, u32[]{:S(2)}, u32[]{:S(2)}) collective-permute-start(f32[256,128]{1,0:T(8,128)S(1)} %row_pass.2), channel_id=1, source_target_pairs={{3,0},{0,1},{1,2},{2,3},{7,4},{4,5},{5,6},{6,7},{11,8},{8,9},{9,10... | collective-permute-start | bytes 393224 | tf_op jit(solution)/shard_map/ppermute | solution.py:254
  37.9 7.0 %collective-permute-start.3 = (f32[256,128]{1,0:T(8,128)S(1)}, f32[256,128]{1,0:T(8,128)S(1)}, u32[]{:S(2)}, u32[]{:S(2)}) collective-permute-start(f32[256,128]{1,0:T(8,128)S(1)} %row_pass.2), channel_id=1, source_target_pairs={{2,0},{3,1},{0,2},{1,3},{6,4},{7,5},{4,6},{5,7},{10,8},{11,9},{8,1... | collective-permute-start | bytes 393224 | tf_op jit(solution)/shard_map/ppermute | solution.py:254
  45.0 3.9 %collective-permute-start.4 = (f32[256,128]{1,0:T(8,128)S(1)}, f32[256,128]{1,0:T(8,128)S(1)}, u32[]{:S(2)}, u32[]{:S(2)}) collective-permute-start(f32[256,128]{1,0:T(8,128)S(1)} %log_add_fusion.1), channel_id=1, source_target_pairs={{4,0},{5,1},{6,2},{7,3},{8,4},{9,5},{10,6},{11,7},{12,8},{13,9},{1... | collective-permute-start | bytes 393224 | tf_op jit(solution)/shard_map/ppermute | solution.py:254
  46.1 6.9 %collective-permute-start.5 = (f32[256,128]{1,0:T(8,128)S(1)}, f32[256,128]{1,0:T(8,128)S(1)}, u32[]{:S(2)}, u32[]{:S(2)}) collective-permute-start(f32[256,128]{1,0:T(8,128)S(1)} %log_add_fusion.1), channel_id=1, source_target_pairs={{12,0},{13,1},{14,2},{15,3},{0,4},{1,5},{2,6},{3,7},{4,8},{5,9},{6... | collective-permute-start | bytes 393224 | tf_op jit(solution)/shard_map/ppermute | solution.py:254
  46.5 6.5 %collective-permute-start.6 = (f32[256,128]{1,0:T(8,128)S(1)}, f32[256,128]{1,0:T(8,128)S(1)}, u32[]{:S(2)}, u32[]{:S(2)}) collective-permute-start(f32[256,128]{1,0:T(8,128)S(1)} %log_add_fusion.1), channel_id=1, source_target_pairs={{8,0},{9,1},{10,2},{11,3},{12,4},{13,5},{14,6},{15,7},{0,8},{1,9},... | collective-permute-start | bytes 393224 | tf_op jit(solution)/shard_map/ppermute | solution.py:254
  61.0 37.4 %copy-start.3 = (f32[32768]{0:T(1024)S(1)}, f32[32768]{0:T(1024)}, u32[]{:S(2)}) copy-start(f32[32768]{0:T(1024)} %param.11) | copy-start | bytes 393220
  61.0 37.4 %copy-start.4 = (f32[32768]{0:T(1024)S(1)}, f32[32768]{0:T(1024)}, u32[]{:S(2)}) copy-start(f32[32768]{0:T(1024)} %param.10) | copy-start | bytes 393220
  61.0 13.4 %all-to-all-start.1 = ((f32[16,56,128]{2,1,0:T(8,128)}), f32[16,56,128]{2,1,0:T(8,128)S(1)}, u32[]{:S(2)}, u32[]{:S(2)}) async-start(f32[16,56,128]{2,1,0:T(8,128)} %bitcast.10), calls=%async_computation.1 | async-start | bytes 917504 | tf_op jit(solution)/shard_map/all_to_all | solution.py:239
  77.4 5.0 %collective-permute-start.7 = (f32[128,128]{1,0:T(8,128)S(1)}, f32[128,128]{1,0:T(8,128)S(1)}, u32[]{:S(2)}, u32[]{:S(2)}) collective-permute-start(f32[128,128]{1,0:T(8,128)S(1)} %constant_dynamic-slice_fusion.1), channel_id=1, source_target_pairs={{16,0},{0,16},{48,32},{32,48},{80,64},{64,80},{112,96},{96,112},{1... | collective-permute-start | bytes 196616 | tf_op jit(solution)/shard_map/ppermute | solution.py:254
  82.4 3.8 %collective-permute-start.8 = (f32[128,128]{1,0:T(8,128)S(1)}, f32[128,128]{1,0:T(8,128)S(1)}, u32[]{:S(2)}, u32[]{:S(2)}) collective-permute-start(f32[128,128]{1,0:T(8,128)S(1)} %log_add_fusion.5), channel_id=1, source_target_pairs={{32,0},{48,16},{0,32},{16,48},{96,64},{112,80},{64,96},{80,112},{1... | collective-permute-start | bytes 196616 | tf_op jit(solution)/shard_map/ppermute | solution.py:254
  86.3 7.1 %collective-permute-start.10 = (f32[128,128]{1,0:T(8,128)S(1)}, f32[128,128]{1,0:T(8,128)S(1)}, u32[]{:S(2)}, u32[]{:S(2)}) collective-permute-start(f32[128,128]{1,0:T(8,128)S(1)} %log_add_fusion.4), channel_id=1, source_target_pairs={{64,0},{80,16},{224,32},{240,48},{128,64},{144,80},{32,96},{48,112... | collective-permute-start | bytes 196616 | tf_op jit(solution)/shard_map/ppermute | solution.py:254
  91.8 6.2 %collective-permute-start.11 = (f32[128,128]{1,0:T(8,128)S(1)}, f32[128,128]{1,0:T(8,128)S(1)}, u32[]{:S(2)}, u32[]{:S(2)}) collective-permute-start(f32[128,128]{1,0:T(8,128)S(1)} %log_add_fusion.4), channel_id=1, source_target_pairs={{160,0},{176,16},{128,32},{144,48},{224,64},{240,80},{192,96},{208... | collective-permute-start | bytes 196616 | tf_op jit(solution)/shard_map/ppermute | solution.py:254
  93.4 5.0 %collective-permute-start.9 = (f32[128,128]{1,0:T(8,128)S(1)}, f32[128,128]{1,0:T(8,128)S(1)}, u32[]{:S(2)}, u32[]{:S(2)}) collective-permute-start(f32[128,128]{1,0:T(8,128)S(1)} %log_add_fusion.4), channel_id=1, source_target_pairs={{224,0},{240,16},{64,32},{80,48},{32,64},{48,80},{128,96},{144,112... | collective-permute-start | bytes 196616 | tf_op jit(solution)/shard_map/ppermute | solution.py:254
  98.6 4.1 %collective-permute-start.12 = (f32[128,128]{1,0:T(8,128)S(1)}, f32[128,128]{1,0:T(8,128)S(1)}, u32[]{:S(2)}, u32[]{:S(2)}) collective-permute-start(f32[128,128]{1,0:T(8,128)S(1)} %add_subtract_fusion.1), channel_id=1, source_target_pairs={{16,0},{0,16},{48,32},{32,48},{80,64},{64,80},{112,96},{96,112},{1... | collective-permute-start | bytes 196616 | tf_op jit(solution)/shard_map/ppermute | solution.py:254
  123.7 3.9 %collective-permute-start.13 = (f32[256,128]{1,0:T(8,128)S(1)}, f32[256,128]{1,0:T(8,128)S(1)}, u32[]{:S(2)}, u32[]{:S(2)}) collective-permute-start(f32[256,128]{1,0:T(8,128)S(1)} %row_pass.3), channel_id=1, source_target_pairs={{1,0},{2,1},{3,2},{0,3},{5,4},{6,5},{7,6},{4,7},{9,8},{10,9},{11,1... | collective-permute-start | bytes 393224 | tf_op jit(solution)/shard_map/ppermute | solution.py:254
  124.2 5.6 %collective-permute-start.14 = (f32[256,128]{1,0:T(8,128)S(1)}, f32[256,128]{1,0:T(8,128)S(1)}, u32[]{:S(2)}, u32[]{:S(2)}) collective-permute-start(f32[256,128]{1,0:T(8,128)S(1)} %row_pass.3), channel_id=1, source_target_pairs={{3,0},{0,1},{1,2},{2,3},{7,4},{4,5},{5,6},{6,7},{11,8},{8,9},{9,10... | collective-permute-start | bytes 393224 | tf_op jit(solution)/shard_map/ppermute | solution.py:254
  125.2 6.3 %collective-permute-start.15 = (f32[256,128]{1,0:T(8,128)S(1)}, f32[256,128]{1,0:T(8,128)S(1)}, u32[]{:S(2)}, u32[]{:S(2)}) collective-permute-start(f32[256,128]{1,0:T(8,128)S(1)} %row_pass.3), channel_id=1, source_target_pairs={{2,0},{3,1},{0,2},{1,3},{6,4},{7,5},{4,6},{5,7},{10,8},{11,9},{8,1... | collective-permute-start | bytes 393224 | tf_op jit(solution)/shard_map/ppermute | solution.py:254
  131.7 3.9 %collective-permute-start.16 = (f32[256,128]{1,0:T(8,128)S(1)}, f32[256,128]{1,0:T(8,128)S(1)}, u32[]{:S(2)}, u32[]{:S(2)}) collective-permute-start(f32[256,128]{1,0:T(8,128)S(1)} %log_add_fusion), channel_id=1, source_target_pairs={{4,0},{5,1},{6,2},{7,3},{8,4},{9,5},{10,6},{11,7},{12,8},{13,9},{1... | collective-permute-start | bytes 393224 | tf_op jit(solution)/shard_map/ppermute | solution.py:254
  132.4 6.4 %collective-permute-start.17 = (f32[256,128]{1,0:T(8,128)S(1)}, f32[256,128]{1,0:T(8,128)S(1)}, u32[]{:S(2)}, u32[]{:S(2)}) collective-permute-start(f32[256,128]{1,0:T(8,128)S(1)} %log_add_fusion), channel_id=1, source_target_pairs={{12,0},{13,1},{14,2},{15,3},{0,4},{1,5},{2,6},{3,7},{4,8},{5,9},{6... | collective-permute-start | bytes 393224 | tf_op jit(solution)/shard_map/ppermute | solution.py:254
  133.2 5.6 %collective-permute-start.18 = (f32[256,128]{1,0:T(8,128)S(1)}, f32[256,128]{1,0:T(8,128)S(1)}, u32[]{:S(2)}, u32[]{:S(2)}) collective-permute-start(f32[256,128]{1,0:T(8,128)S(1)} %log_add_fusion), channel_id=1, source_target_pairs={{8,0},{9,1},{10,2},{11,3},{12,4},{13,5},{14,6},{15,7},{0,8},{1,9},... | collective-permute-start | bytes 393224 | tf_op jit(solution)/shard_map/ppermute | solution.py:254
  138.9 7.2 %copy-start.1 = (f32[256,128]{1,0:T(8,128)}, f32[256,128]{1,0:T(8,128)S(1)}, u32[]{:S(2)}) copy-start(f32[256,128]{1,0:T(8,128)S(1)} %bitcast_subtract_fusion.pots_ref) | copy-start | bytes 393220
  162.7 5.0 %collective-permute-start.19 = (f32[128,128]{1,0:T(8,128)S(1)}, f32[128,128]{1,0:T(8,128)S(1)}, u32[]{:S(2)}, u32[]{:S(2)}) collective-permute-start(f32[128,128]{1,0:T(8,128)S(1)} %constant_dynamic-slice_fusion), channel_id=1, source_target_pairs={{16,0},{0,16},{48,32},{32,48},{80,64},{64,80},{112,96},{96,112},{1... | collective-permute-start | bytes 196616 | tf_op jit(solution)/shard_map/ppermute | solution.py:254
  167.7 3.2 %collective-permute-start.20 = (f32[128,128]{1,0:T(8,128)S(1)}, f32[128,128]{1,0:T(8,128)S(1)}, u32[]{:S(2)}, u32[]{:S(2)}) collective-permute-start(f32[128,128]{1,0:T(8,128)S(1)} %log_add_fusion.3), channel_id=1, source_target_pairs={{32,0},{48,16},{0,32},{16,48},{96,64},{112,80},{64,96},{80,112},{1... | collective-permute-start | bytes 196616 | tf_op jit(solution)/shard_map/ppermute | solution.py:254
  171.0 4.8 %collective-permute-start.21 = (f32[128,128]{1,0:T(8,128)S(1)}, f32[128,128]{1,0:T(8,128)S(1)}, u32[]{:S(2)}, u32[]{:S(2)}) collective-permute-start(f32[128,128]{1,0:T(8,128)S(1)} %log_add_fusion.2), channel_id=1, source_target_pairs={{224,0},{240,16},{64,32},{80,48},{32,64},{48,80},{128,96},{144,112... | collective-permute-start | bytes 196616 | tf_op jit(solution)/shard_map/ppermute | solution.py:254
  171.9 4.5 %collective-permute-start.22 = (f32[128,128]{1,0:T(8,128)S(1)}, f32[128,128]{1,0:T(8,128)S(1)}, u32[]{:S(2)}, u32[]{:S(2)}) collective-permute-start(f32[128,128]{1,0:T(8,128)S(1)} %log_add_fusion.2), channel_id=1, source_target_pairs={{64,0},{80,16},{224,32},{240,48},{128,64},{144,80},{32,96},{48,112... | collective-permute-start | bytes 196616 | tf_op jit(solution)/shard_map/ppermute | solution.py:254
  173.3 6.6 %collective-permute-start.23 = (f32[128,128]{1,0:T(8,128)S(1)}, f32[128,128]{1,0:T(8,128)S(1)}, u32[]{:S(2)}, u32[]{:S(2)}) collective-permute-start(f32[128,128]{1,0:T(8,128)S(1)} %log_add_fusion.2), channel_id=1, source_target_pairs={{160,0},{176,16},{128,32},{144,48},{224,64},{240,80},{192,96},{208... | collective-permute-start | bytes 196616 | tf_op jit(solution)/shard_map/ppermute | solution.py:254
  180.0 4.0 %collective-permute-start.24 = (f32[128,128]{1,0:T(8,128)S(1)}, f32[128,128]{1,0:T(8,128)S(1)}, u32[]{:S(2)}, u32[]{:S(2)}) collective-permute-start(f32[128,128]{1,0:T(8,128)S(1)} %add_subtract_fusion), channel_id=1, source_target_pairs={{16,0},{0,16},{48,32},{32,48},{80,64},{64,80},{112,96},{96,112},{1... | collective-permute-start | bytes 196616 | tf_op jit(solution)/shard_map/ppermute | solution.py:254

commit v3 on v2

--- a/solution.py
+++ b/solution.py
@@ -11,7 +11,7 @@
 NEGATIVE = -1e30
 VMEM = pltpu.VMEM
 SMEM = pltpu.SMEM
-VMEM_BYTES = 48 << 20
+VMEM_BYTES = 40 << 20
 CHUNKS = 4
 UNROLL = 64
 EXTRA = 8
@@ -54,13 +54,6 @@
             copy(g, i).wait()
 
     return ready
-
-
-def stream_scratch(tiles):
-    return [
-        VMEM(tiles.shape, tiles.dtype),
-        pltpu.SemaphoreType.DMA((tiles.shape[0] // UNROLL, CHUNKS)),
-    ]
 
 
 def pick_kernel(ids_ref, rows_ref, out_ref):
@@ -120,17 +113,19 @@
     return pl.pallas_call(
         row_kernel,
         name="row_pass",
-        out_shape=jax.ShapeDtypeStruct(tiles.shape[:2], jnp.float32),
+        out_shape=(
+            jax.ShapeDtypeStruct(tiles.shape[:2], jnp.float32),
+            VMEM(tiles.shape, tiles.dtype),
+        ),
         in_specs=[spec(SMEM), spec(pltpu.HBM)] + [spec(VMEM)] * len(pots),
-        out_specs=spec(VMEM),
-        scratch_shapes=stream_scratch(tiles),
+        out_specs=(spec(VMEM), spec(VMEM)),
+        scratch_shapes=[pltpu.SemaphoreType.DMA((tiles.shape[0] // UNROLL, CHUNKS))],
         compiler_params=params(),
     )(slot, tiles, *pots)
 
 
 def col_kernel(capacity, slot_ref, tiles_ref, pots_ref, *refs):
-    *ask_refs, out_ref, row_ref, held_ref, sems = refs
-    ready = stream(tiles_ref, held_ref, sems)
+    *ask_refs, out_ref, row_ref = refs
     out_ref[...] = jnp.full(out_ref.shape, NEGATIVE, jnp.float32)
     width = tiles_ref.shape[1]
     for ask_ref in ask_refs:
@@ -139,12 +134,11 @@
             out_ref[row : row + 1, :] = ask_ref[owner : owner + 1, :]
 
     def step(g, carry):
-        ready(g)
         tops, sums = [], []
         for k in range(UNROLL):
             n = g * UNROLL + k
             pot = jnp.broadcast_to(pots_ref[pl.ds(n, 1), :], (width, width))
-            scores = held_ref[n].astype(jnp.float32) + jnp.transpose(pot)
+            scores = tiles_ref[n].astype(jnp.float32) + jnp.transpose(pot)
             top = jnp.max(scores, axis=0, keepdims=True)
             tops.append(top)
             sums.append(jnp.sum(jnp.exp(scores - top), axis=0, keepdims=True))
@@ -162,9 +156,9 @@
         functools.partial(col_kernel, capacity),
         name="col_pass",
         out_shape=jax.ShapeDtypeStruct((slots, width), jnp.float32),
-        in_specs=[spec(SMEM), spec(pltpu.HBM)] + [spec(VMEM)] * (1 + len(ask)),
+        in_specs=[spec(SMEM)] + [spec(VMEM)] * (2 + len(ask)),
         out_specs=spec(VMEM),
-        scratch_shapes=[VMEM((UNROLL, width), jnp.float32)] + stream_scratch(tiles),
+        scratch_shapes=[VMEM((UNROLL, width), jnp.float32)],
         compiler_params=params(),
     )(slot, tiles, pots, *ask)
 
@@ -261,13 +255,13 @@
     def far(i, step):
         return (i + 4 * step) % count
 
-    return [[[move(i, step) for i in range(count)] for step in (1, 3, 2)] for move in (near, far)]
+    return [[[move(i, step) for i in range(count)] for step in (2, 1, 3)] for move in (near, far)]
 
 
 def row_phases(count):
     phases = (
         ([1, 0, 3, 2, 5, 4, 7, 6],),
-        ([7, 2, 1, 4, 3, 6, 5, 0], [2, 7, 4, 1, 6, 3, 0, 5], [5, 4, 7, 6, 1, 0, 3, 2]),
+        ([5, 4, 7, 6, 1, 0, 3, 2], [7, 2, 1, 4, 3, 6, 5, 0], [2, 7, 4, 1, 6, 3, 0, 5]),
     )
     return [[[2 * z[i // 2] + i % 2 for i in range(count)] for z in phase] for phase in phases]
 
@@ -279,17 +273,21 @@
     tile_count = row_tiles * local_slots
     capacity = min(tile_count // 2, 3 * tile_count // owners)
     half = block_tiles // 2
-    core = lax.axis_index("row") % 2
+    core = lax.axis_index("row") & 1
+    first = core == 0
     other_core = [i ^ 1 for i in range(lax.axis_size("row"))]
 
     source_rows = log_source.reshape(row_tiles, width)
 
-    def mine(value, side):
-        return lax.dynamic_slice_in_dim(value, side * half, half, 0)
-
-    start_half = mine(start_pot.reshape(block_tiles, width), core)
-    target_half = mine(log_target.reshape(block_tiles, width), core)
-    dust_half = mine(dustbin.reshape(block_tiles, width), core)
+    def mine(value):
+        return jnp.where(first, value[:half], value[half:])
+
+    def others(value):
+        return jnp.where(first, value[half:], value[:half])
+
+    start_half = mine(start_pot.reshape(block_tiles, width))
+    target_half = mine(log_target.reshape(block_tiles, width))
+    dust_half = mine(dustbin.reshape(block_tiles, width))
 
     tiles = kernel.reshape(tile_count, width, width)
     owner, local, rank, ask = plan(tile_cols.reshape(tile_count), block_tiles, owners, width)
@@ -299,9 +297,9 @@
     far = swap(near, "row", other_core)
     for repeat in range(ITERS):
         if repeat == 0:
-            row_lse = row_pass(place, tiles, near, far)
+            row_lse, held = row_pass(place, tiles, near, far)
         else:
-            row_lse = row_pass(
+            row_lse, held = row_pass(
                 owner * capacity + rank, tiles, exchange(pick(ids, target_now), owners)
             )
         for phase in col_phases(owners):
@@ -310,24 +308,24 @@
         if repeat == 0:
             stride = capacity + EXTRA
             rows = col_pass(
-                owner * stride + rank, tiles, source_now, owners * stride, capacity, ask
+                owner * stride + rank, held, source_now, owners * stride, capacity, ask
             )
             rows = exchange(rows, owners)
             ids = rows.reshape(owners, stride, width)[:, capacity, :capacity]
             ids = ids.astype(jnp.int32).reshape(owners * capacity)
         else:
             rows = col_pass(
-                owner * capacity + rank, tiles, source_now, owners * capacity, capacity
+                owner * capacity + rank, held, source_now, owners * capacity, capacity
             )
             rows = exchange(rows, owners)
         part = segment(ids, rows, block_tiles, capacity)
-        col_lse = log_sum(mine(part, core), swap(mine(part, 1 - core), "row", other_core))
+        col_lse = log_sum(mine(part), swap(others(part), "row", other_core))
         for phase in row_phases(len(other_core)):
             col_lse = log_sum(col_lse, *[swap(col_lse, "row", partner) for partner in phase])
         here = target_half - log_sum(col_lse, dust_half)
         there = swap(here, "row", other_core)
         target_now = jnp.where(
-            core == 0, jnp.concatenate([here, there]), jnp.concatenate([there, here])
+            first, jnp.concatenate([here, there]), jnp.concatenate([there, here])
         )
     return source_now.reshape(log_source.shape), target_now.reshape(start_pot.shape)
 

time: 185 us -> 181 us (0.978)
  blocking collectives: 49.3 us -> 61.9 us
  starting transfers between devices: 45.4 us -> 37.1 us
  waiting for transfers between devices: 49.4 us -> 44.3 us
  Pallas kernels: 36.5 us -> 33.4 us
    all_to_all x3 -> x4, blocking collectives: 49.3 us -> 61.9 us  [exchange(): lax.all_to_all(value.reshape((owners, shape[0] // owners) + shape[1:]), '...]
    all_to_all x1 -> x0, waiting for transfers between devices: 8.62 us -> none  [exchange(): lax.all_to_all(value.reshape((owners, shape[0] // owners) + shape[1:]), '...]
    all_to_all x1 -> x0, starting transfers between devices: 4.81 us -> none  [exchange(): lax.all_to_all(value.reshape((owners, shape[0] // owners) + shape[1:]), '...]
    ppermute x25, waiting for transfers between devices: 40.8 us -> 44.3 us  [swap(): return lax.ppermute(value, axis, [(j, i) for i, j in enumerate(partner)])]
    ppermute x25, starting transfers between devices: 40.6 us -> 37.1 us  [swap(): return lax.ppermute(value, axis, [(j, i) for i, j in enumerate(partner)])]
    pallas_call x2, Pallas kernels: 15.1 us -> 11.9 us  [col_pass(): pl.pallas_call(functools.partial(col_kernel, capacity), name='col_pass',...]
  transfers between devices with their start and end apart: 26 -> 25, of which waited for: 22 -> 23; matrix products, arithmetic and copies ran while one was open for 0% -> 0% of each run, Pallas kernels for 0% -> 0%
where the time goes in v3:
time: 181 us
  blocking collectives  61.9 us (34%)
  waiting for transfers between devices  44.3 us (24%)
  starting transfers between devices  37.1 us (20%)
  Pallas kernels  33.4 us (18%)
  other arithmetic  2.98 us (2%)
    all_to_all x4, blocking collectives, exchange(): lax.all_to_all(value.reshape((owners, shape[0] // owners) + shape[1:]), '...  61.9 us
    ppermute x25, waiting for transfers between devices, swap(): return lax.ppermute(value, axis, [(j, i) for i, j in enumerate(partner)])  44.3 us
    ppermute x25, starting transfers between devices, swap(): return lax.ppermute(value, axis, [(j, i) for i, j in enumerate(partner)])  37.1 us
    pallas_call x2, Pallas kernels, row_pass(): pl.pallas_call(row_kernel, name='row_pass', out_shape=(jax.ShapeDtypeStru...  14.3 us
    pallas_call x2, Pallas kernels, col_pass(): pl.pallas_call(functools.partial(col_kernel, capacity), name='col_pass',...  11.9 us
    pallas_call x2, Pallas kernels, segment(): pl.pallas_call(functools.partial(segment_kernel, capacity), name='segment...  5.52 us
  transfers between devices with their start and end apart: 25, of which 23 were waited for; matrix products, arithmetic and copies ran while one was open for 0% of the time, Pallas kernels for 0%

profile of v3, /device:TPU:1, one launch (start us, length us, event | category | flops | bytes accessed | tf_op | source)
XLA Modules:
  0.0 180.8 jit_solution(15121393824758278779)
XLA Ops:
  1.6 23.3 %all_to_all.20 = f32[16,128,128]{2,1,0:T(8,128)S(1)} all-to-all(f32[16,128,128]{2,1,0:T(8,128)S(1)} %reshape_tile.3), channel_id=1, replica_groups=mesh['row'=16,'col'=16] {'col'}, dimensions={0} | all-to-all | bytes 2097152 | tf_op jit(solution)/shard_map/all_to_all | solution.py:233
  24.9 1.9 %collective-permute-start = (f32[2048,128]{1,0:T(8,128)S(1)}, f32[2048,128]{1,0:T(8,128)S(1)}, u32[]{:S(2)}, u32[]{:S(2)}) collective-permute-start(f32[2048,128]{1,0:T(8,128)S(1)} %bitcast.67), channel_id=1, source_target_pairs={{16,0},{0,16},{48,32},{32,48},{80,64},{64,80},{112,96},{96,112},{1... | collective-permute-start | bytes 3145736 | tf_op jit(solution)/shard_map/ppermute | solution.py:248
  27.4 1.7 collective-permute-done.refs_1_
  29.1 7.2 %row_pass.2 = (f32[256,128]{1,0:T(8,128)S(1)}, bf16[256,128,128]{2,1,0:T(8,128)(2,1)S(1)}) custom-call(s32[256]{0:T(256)S(1)} %get-tuple-element.12.slot_ref, bf16[256,128,128]{2,1,0:T(8,128)(2,1)} %bitcast.76, f32[2048,128]{1,0:T(8,128)S(1)} %bitcast.68, f32[2048,128]{1,0:T(8,128)S(1)} %collective-permute-done.refs_1_), custom_call_target="tpu_custom_call" | custom-call | tf_op jit(solution)/shard_map/row_pass/pallas_call | solution.py:113
  39.1 3.6 %collective-permute-done.1 = f32[256,128]{1,0:T(8,128)S(1)} collective-permute-done((f32[256,128]{1,0:T(8,128)S(1)}, f32[256,128]{1,0:T(8,128)S(1)}, u32[]{:S(2)}, u32[]{:S(2)}) %collective-permute-start.1) | collective-permute-done | bytes 131104 | tf_op jit(solution)/shard_map/ppermute | solution.py:248
  43.8 1.9 %collective-permute-done.3 = f32[256,128]{1,0:T(8,128)S(1)} collective-permute-done((f32[256,128]{1,0:T(8,128)S(1)}, f32[256,128]{1,0:T(8,128)S(1)}, u32[]{:S(2)}, u32[]{:S(2)}) %collective-permute-start.3) | collective-permute-done | bytes 131104 | tf_op jit(solution)/shard_map/ppermute | solution.py:248
  48.3 2.8 %collective-permute-done.4 = f32[256,128]{1,0:T(8,128)S(1)} collective-permute-done((f32[256,128]{1,0:T(8,128)S(1)}, f32[256,128]{1,0:T(8,128)S(1)}, u32[]{:S(2)}, u32[]{:S(2)}) %collective-permute-start.4) | collective-permute-done | bytes 131104 | tf_op jit(solution)/shard_map/ppermute | solution.py:248
  52.7 2.2 %collective-permute-done.6 = f32[256,128]{1,0:T(8,128)S(1)} collective-permute-done((f32[256,128]{1,0:T(8,128)S(1)}, f32[256,128]{1,0:T(8,128)S(1)}, u32[]{:S(2)}, u32[]{:S(2)}) %collective-permute-start.6) | collective-permute-done | bytes 131104 | tf_op jit(solution)/shard_map/ppermute | solution.py:248
  55.0 5.9 %col_pass.2 = f32[896,128]{1,0:T(8,128)S(1)} custom-call(s32[256]{0:T(256)S(1)} %get-tuple-element.14.slot_ref, bf16[256,128,128]{2,1,0:T(8,128)(2,1)S(1)} %get-tuple-element.6.tiles_ref, f32[256,128]{1,0:T(8,128)S(1)} %bitcast_subtract_fusion.1.pots_ref, f32[16,128]{1,0:T(8,128)S(1)} %convert_bitcast_fusion.refs_0_), custom_call_target="tpu_custom_call" | custom-call | tf_op jit(solution)/shard_map/col_pass/pallas_call | solution.py:155
  61.0 14.5 %all_to_all.21 = f32[16,56,128]{2,1,0:T(8,128)S(1)} all-to-all(f32[16,56,128]{2,1,0:T(8,128)S(1)} %bitcast.70), channel_id=1, replica_groups=mesh['row'=16,'col'=16] {'col'}, dimensions={0} | all-to-all | bytes 917504 | tf_op jit(solution)/shard_map/all_to_all | solution.py:233
  75.6 2.8 %segment.2 = f32[256,128]{1,0:T(8,128)S(1)} custom-call(s32[768]{0:T(1024)S(1)} %convert_element_type.19.ids_ref, f32[896,128]{1,0:T(8,128)S(1)} %bitcast.69), custom_call_target="tpu_custom_call" | custom-call | tf_op jit(solution)/shard_map/segment/pallas_call | solution.py:220
  78.3 2.0 %collective-permute-start.7 = (f32[128,128]{1,0:T(8,128)S(1)}, f32[128,128]{1,0:T(8,128)S(1)}, u32[]{:S(2)}, u32[]{:S(2)}) collective-permute-start(f32[128,128]{1,0:T(8,128)S(1)} %slice_select_fusion.3), channel_id=1, source_target_pairs={{16,0},{0,16},{48,32},{32,48},{80,64},{64,80},{112,96},{96,112},{1... | collective-permute-start | bytes 196616 | tf_op jit(solution)/shard_map/ppermute | solution.py:248
  81.3 1.8 collective-permute-start.8
  83.1 2.1 %collective-permute-done.8 = f32[128,128]{1,0:T(8,128)S(1)} collective-permute-done((f32[128,128]{1,0:T(8,128)S(1)}, f32[128,128]{1,0:T(8,128)S(1)}, u32[]{:S(2)}, u32[]{:S(2)}) %collective-permute-start.8) | collective-permute-done | bytes 65568 | tf_op jit(solution)/shard_map/ppermute | solution.py:248
  85.2 5.0 %collective-permute-start.10 = (f32[128,128]{1,0:T(8,128)S(1)}, f32[128,128]{1,0:T(8,128)S(1)}, u32[]{:S(2)}, u32[]{:S(2)}) collective-permute-start(f32[128,128]{1,0:T(8,128)S(1)} %log_add_fusion.4), channel_id=1, source_target_pairs={{224,0},{240,16},{64,32},{80,48},{32,64},{48,80},{128,96},{144,112... | collective-permute-start | bytes 196616 | tf_op jit(solution)/shard_map/ppermute | solution.py:248
  92.4 1.8 %collective-permute-done.11 = f32[128,128]{1,0:T(8,128)S(1)} collective-permute-done((f32[128,128]{1,0:T(8,128)S(1)}, f32[128,128]{1,0:T(8,128)S(1)}, u32[]{:S(2)}, u32[]{:S(2)}) %collective-permute-start.11) | collective-permute-done | bytes 65568 | tf_op jit(solution)/shard_map/ppermute | solution.py:248
  94.3 3.6 %collective-permute-done.9 = f32[128,128]{1,0:T(8,128)S(1)} collective-permute-done((f32[128,128]{1,0:T(8,128)S(1)}, f32[128,128]{1,0:T(8,128)S(1)}, u32[]{:S(2)}, u32[]{:S(2)}) %collective-permute-start.9) | collective-permute-done | bytes 65568 | tf_op jit(solution)/shard_map/ppermute | solution.py:248
  98.0 3.3 %collective-permute-start.12 = (f32[128,128]{1,0:T(8,128)S(1)}, f32[128,128]{1,0:T(8,128)S(1)}, u32[]{:S(2)}, u32[]{:S(2)}) collective-permute-start(f32[128,128]{1,0:T(8,128)S(1)} %fusion.8), channel_id=1, source_target_pairs={{16,0},{0,16},{48,32},{32,48},{80,64},{64,80},{112,96},{96,112},{1... | collective-permute-start | bytes 196616 | tf_op jit(solution)/shard_map/ppermute | solution.py:248
  103.9 12.3 %all_to_all.22 = f32[16,48,128]{2,1,0:T(8,128)S(1)} all-to-all(f32[16,48,128]{2,1,0:T(8,128)S(1)} %bitcast.74), channel_id=1, replica_groups=mesh['row'=16,'col'=16] {'col'}, dimensions={0} | all-to-all | bytes 786432 | tf_op jit(solution)/shard_map/all_to_all | solution.py:233
  116.2 7.1 %row_pass.3 = (f32[256,128]{1,0:T(8,128)S(1)}, bf16[256,128,128]{2,1,0:T(8,128)(2,1)S(1)}) custom-call(s32[256]{0:T(256)S(1)} %get-tuple-element.15.slot_ref, bf16[256,128,128]{2,1,0:T(8,128)(2,1)} %bitcast.77, f32[768,128]{1,0:T(8,128)S(1)} %bitcast.71), custom_call_target="tpu_custom_call" | custom-call | tf_op jit(solution)/shard_map/row_pass/pallas_call | solution.py:113
  124.3 1.8 collective-permute-start.14
  126.0 2.6 %collective-permute-done.13 = f32[256,128]{1,0:T(8,128)S(1)} collective-permute-done((f32[256,128]{1,0:T(8,128)S(1)}, f32[256,128]{1,0:T(8,128)S(1)}, u32[]{:S(2)}, u32[]{:S(2)}) %collective-permute-start.13) | collective-permute-done | bytes 131104 | tf_op jit(solution)/shard_map/ppermute | solution.py:248
  129.5 3.2 %collective-permute-done.15 = f32[256,128]{1,0:T(8,128)S(1)} collective-permute-done((f32[256,128]{1,0:T(8,128)S(1)}, f32[256,128]{1,0:T(8,128)S(1)}, u32[]{:S(2)}, u32[]{:S(2)}) %collective-permute-start.15) | collective-permute-done | bytes 131104 | tf_op jit(solution)/shard_map/ppermute | solution.py:248
  135.1 3.1 %collective-permute-done.16 = f32[256,128]{1,0:T(8,128)S(1)} collective-permute-done((f32[256,128]{1,0:T(8,128)S(1)}, f32[256,128]{1,0:T(8,128)S(1)}, u32[]{:S(2)}, u32[]{:S(2)}) %collective-permute-start.16) | collective-permute-done | bytes 131104 | tf_op jit(solution)/shard_map/ppermute | solution.py:248
  138.3 2.5 %collective-permute-done.18 = f32[256,128]{1,0:T(8,128)S(1)} collective-permute-done((f32[256,128]{1,0:T(8,128)S(1)}, f32[256,128]{1,0:T(8,128)S(1)}, u32[]{:S(2)}, u32[]{:S(2)}) %collective-permute-start.18) | collective-permute-done | bytes 131104 | tf_op jit(solution)/shard_map/ppermute | solution.py:248
  140.9 5.9 %col_pass.3 = f32[768,128]{1,0:T(8,128)S(1)} custom-call(s32[256]{0:T(256)S(1)} %get-tuple-element.15.slot_ref, bf16[256,128,128]{2,1,0:T(8,128)(2,1)S(1)} %get-tuple-element.9.tiles_ref, f32[256,128]{1,0:T(8,128)S(1)} %bitcast_subtract_fusion.pots_ref), custom_call_target="tpu_custom_call" | custom-call | tf_op jit(solution)/shard_map/col_pass/pallas_call | solution.py:155
  146.8 11.9 %all_to_all.23 = f32[16,48,128]{2,1,0:T(8,128)S(1)} all-to-all(f32[16,48,128]{2,1,0:T(8,128)S(1)} %bitcast.72), channel_id=1, replica_groups=mesh['row'=16,'col'=16] {'col'}, dimensions={0} | all-to-all | bytes 786432 | tf_op jit(solution)/shard_map/all_to_all | solution.py:233
  158.8 2.8 %segment.3 = f32[256,128]{1,0:T(8,128)S(1)} custom-call(s32[768]{0:T(1024)S(1)} %convert_element_type.19.ids_ref, f32[768,128]{1,0:T(8,128)S(1)} %bitcast.73), custom_call_target="tpu_custom_call" | custom-call | tf_op jit(solution)/shard_map/segment/pallas_call | solution.py:220
  161.5 2.6 %collective-permute-start.19 = (f32[128,128]{1,0:T(8,128)S(1)}, f32[128,128]{1,0:T(8,128)S(1)}, u32[]{:S(2)}, u32[]{:S(2)}) collective-permute-start(f32[128,128]{1,0:T(8,128)S(1)} %slice_select_fusion.2), channel_id=1, source_target_pairs={{16,0},{0,16},{48,32},{32,48},{80,64},{64,80},{112,96},{96,112},{1... | collective-permute-start | bytes 196616 | tf_op jit(solution)/shard_map/ppermute | solution.py:248
  165.7 2.7 %collective-permute-done.20 = f32[128,128]{1,0:T(8,128)S(1)} collective-permute-done((f32[128,128]{1,0:T(8,128)S(1)}, f32[128,128]{1,0:T(8,128)S(1)}, u32[]{:S(2)}, u32[]{:S(2)}) %collective-permute-start.20) | collective-permute-done | bytes 65568 | tf_op jit(solution)/shard_map/ppermute | solution.py:248
  170.0 1.8 %collective-permute-start.22 = (f32[128,128]{1,0:T(8,128)S(1)}, f32[128,128]{1,0:T(8,128)S(1)}, u32[]{:S(2)}, u32[]{:S(2)}) collective-permute-start(f32[128,128]{1,0:T(8,128)S(1)} %log_add_fusion.2), channel_id=1, source_target_pairs={{224,0},{240,16},{64,32},{80,48},{32,64},{48,80},{128,96},{144,112... | collective-permute-start | bytes 196616 | tf_op jit(solution)/shard_map/ppermute | solution.py:248
  176.7 2.6 %collective-permute-start.24 = (f32[128,128]{1,0:T(8,128)S(1)}, f32[128,128]{1,0:T(8,128)S(1)}, u32[]{:S(2)}, u32[]{:S(2)}) collective-permute-start(f32[128,128]{1,0:T(8,128)S(1)} %fusion.15), channel_id=1, source_target_pairs={{16,0},{0,16},{48,32},{32,48},{80,64},{64,80},{112,96},{96,112},{1... | collective-permute-start | bytes 196616 | tf_op jit(solution)/shard_map/ppermute | solution.py:248
  (65 shorter events, 29.7 us)
Async XLA Ops:
  0.6 26.2 %copy-start.4 = (s32[256,1]{0,1:T(1,128)S(1)}, s32[256,1]{0,1:T(1,128)}, u32[]{:S(2)}) copy-start(s32[256,1]{0,1:T(1,128)} %param.7) | copy-start | bytes 3076
  24.9 4.2 %collective-permute-start = (f32[2048,128]{1,0:T(8,128)S(1)}, f32[2048,128]{1,0:T(8,128)S(1)}, u32[]{:S(2)}, u32[]{:S(2)}) collective-permute-start(f32[2048,128]{1,0:T(8,128)S(1)} %bitcast.67), channel_id=1, source_target_pairs={{16,0},{0,16},{48,32},{32,48},{80,64},{64,80},{112,96},{96,112},{1... | collective-permute-start | bytes 3145736 | tf_op jit(solution)/shard_map/ppermute | solution.py:248
  29.1 25.8 %copy-start.1 = (f32[32768]{0:T(1024)S(1)}, f32[32768]{0:T(1024)}, u32[]{:S(2)}) copy-start(f32[32768]{0:T(1024)} %param.9) | copy-start | bytes 393220
  36.4 6.3 %collective-permute-start.1 = (f32[256,128]{1,0:T(8,128)S(1)}, f32[256,128]{1,0:T(8,128)S(1)}, u32[]{:S(2)}, u32[]{:S(2)}) collective-permute-start(f32[256,128]{1,0:T(8,128)S(1)} %get-tuple-element.7), channel_id=1, source_target_pairs={{2,0},{3,1},{0,2},{1,3},{6,4},{7,5},{4,6},{5,7},{10,8},{11,9},{8,1... | collective-permute-start | bytes 393224 | tf_op jit(solution)/shard_map/ppermute | solution.py:248
  37.6 6.1 %collective-permute-start.2 = (f32[256,128]{1,0:T(8,128)S(1)}, f32[256,128]{1,0:T(8,128)S(1)}, u32[]{:S(2)}, u32[]{:S(2)}) collective-permute-start(f32[256,128]{1,0:T(8,128)S(1)} %get-tuple-element.7), channel_id=1, source_target_pairs={{1,0},{2,1},{3,2},{0,3},{5,4},{6,5},{7,6},{4,7},{9,8},{10,9},{11,1... | collective-permute-start | bytes 393224 | tf_op jit(solution)/shard_map/ppermute | solution.py:248
  39.0 6.7 %collective-permute-start.3 = (f32[256,128]{1,0:T(8,128)S(1)}, f32[256,128]{1,0:T(8,128)S(1)}, u32[]{:S(2)}, u32[]{:S(2)}) collective-permute-start(f32[256,128]{1,0:T(8,128)S(1)} %get-tuple-element.7), channel_id=1, source_target_pairs={{3,0},{0,1},{1,2},{2,3},{7,4},{4,5},{5,6},{6,7},{11,8},{8,9},{9,10... | collective-permute-start | bytes 393224 | tf_op jit(solution)/shard_map/ppermute | solution.py:248
  45.7 5.4 %collective-permute-start.4 = (f32[256,128]{1,0:T(8,128)S(1)}, f32[256,128]{1,0:T(8,128)S(1)}, u32[]{:S(2)}, u32[]{:S(2)}) collective-permute-start(f32[256,128]{1,0:T(8,128)S(1)} %log_add_fusion.1), channel_id=1, source_target_pairs={{8,0},{9,1},{10,2},{11,3},{12,4},{13,5},{14,6},{15,7},{0,8},{1,9},... | collective-permute-start | bytes 393224 | tf_op jit(solution)/shard_map/ppermute | solution.py:248
  46.9 5.8 %collective-permute-start.5 = (f32[256,128]{1,0:T(8,128)S(1)}, f32[256,128]{1,0:T(8,128)S(1)}, u32[]{:S(2)}, u32[]{:S(2)}) collective-permute-start(f32[256,128]{1,0:T(8,128)S(1)} %log_add_fusion.1), channel_id=1, source_target_pairs={{4,0},{5,1},{6,2},{7,3},{8,4},{9,5},{10,6},{11,7},{12,8},{13,9},{1... | collective-permute-start | bytes 393224 | tf_op jit(solution)/shard_map/ppermute | solution.py:248
  48.1 6.8 %collective-permute-start.6 = (f32[256,128]{1,0:T(8,128)S(1)}, f32[256,128]{1,0:T(8,128)S(1)}, u32[]{:S(2)}, u32[]{:S(2)}) collective-permute-start(f32[256,128]{1,0:T(8,128)S(1)} %log_add_fusion.1), channel_id=1, source_target_pairs={{12,0},{13,1},{14,2},{15,3},{0,4},{1,5},{2,6},{3,7},{4,8},{5,9},{6... | collective-permute-start | bytes 393224 | tf_op jit(solution)/shard_map/ppermute | solution.py:248
  60.9 37.0 %copy-start.2 = (f32[32768]{0:T(1024)S(1)}, f32[32768]{0:T(1024)}, u32[]{:S(2)}) copy-start(f32[32768]{0:T(1024)} %param.10) | copy-start | bytes 393220
  60.9 37.0 %copy-start.3 = (f32[32768]{0:T(1024)S(1)}, f32[32768]{0:T(1024)}, u32[]{:S(2)}) copy-start(f32[32768]{0:T(1024)} %param.11) | copy-start | bytes 393220
  78.3 2.9 %collective-permute-start.7 = (f32[128,128]{1,0:T(8,128)S(1)}, f32[128,128]{1,0:T(8,128)S(1)}, u32[]{:S(2)}, u32[]{:S(2)}) collective-permute-start(f32[128,128]{1,0:T(8,128)S(1)} %slice_select_fusion.3), channel_id=1, source_target_pairs={{16,0},{0,16},{48,32},{32,48},{80,64},{64,80},{112,96},{96,112},{1... | collective-permute-start | bytes 196616 | tf_op jit(solution)/shard_map/ppermute | solution.py:248
  81.3 3.9 %collective-permute-start.8 = (f32[128,128]{1,0:T(8,128)S(1)}, f32[128,128]{1,0:T(8,128)S(1)}, u32[]{:S(2)}, u32[]{:S(2)}) collective-permute-start(f32[128,128]{1,0:T(8,128)S(1)} %log_add_fusion.5), channel_id=1, source_target_pairs={{32,0},{48,16},{0,32},{16,48},{96,64},{112,80},{64,96},{80,112},{1... | collective-permute-start | bytes 196616 | tf_op jit(solution)/shard_map/ppermute | solution.py:248
  85.2 7.2 %collective-permute-start.10 = (f32[128,128]{1,0:T(8,128)S(1)}, f32[128,128]{1,0:T(8,128)S(1)}, u32[]{:S(2)}, u32[]{:S(2)}) collective-permute-start(f32[128,128]{1,0:T(8,128)S(1)} %log_add_fusion.4), channel_id=1, source_target_pairs={{224,0},{240,16},{64,32},{80,48},{32,64},{48,80},{128,96},{144,112... | collective-permute-start | bytes 196616 | tf_op jit(solution)/shard_map/ppermute | solution.py:248
  90.2 4.0 %collective-permute-start.11 = (f32[128,128]{1,0:T(8,128)S(1)}, f32[128,128]{1,0:T(8,128)S(1)}, u32[]{:S(2)}, u32[]{:S(2)}) collective-permute-start(f32[128,128]{1,0:T(8,128)S(1)} %log_add_fusion.4), channel_id=1, source_target_pairs={{64,0},{80,16},{224,32},{240,48},{128,64},{144,80},{32,96},{48,112... | collective-permute-start | bytes 196616 | tf_op jit(solution)/shard_map/ppermute | solution.py:248
  91.4 6.5 %collective-permute-start.9 = (f32[128,128]{1,0:T(8,128)S(1)}, f32[128,128]{1,0:T(8,128)S(1)}, u32[]{:S(2)}, u32[]{:S(2)}) collective-permute-start(f32[128,128]{1,0:T(8,128)S(1)} %log_add_fusion.4), channel_id=1, source_target_pairs={{160,0},{176,16},{128,32},{144,48},{224,64},{240,80},{192,96},{208... | collective-permute-start | bytes 196616 | tf_op jit(solution)/shard_map/ppermute | solution.py:248
  98.0 4.2 %collective-permute-start.12 = (f32[128,128]{1,0:T(8,128)S(1)}, f32[128,128]{1,0:T(8,128)S(1)}, u32[]{:S(2)}, u32[]{:S(2)}) collective-permute-start(f32[128,128]{1,0:T(8,128)S(1)} %fusion.8), channel_id=1, source_target_pairs={{16,0},{0,16},{48,32},{32,48},{80,64},{64,80},{112,96},{96,112},{1... | collective-permute-start | bytes 196616 | tf_op jit(solution)/shard_map/ppermute | solution.py:248
  123.3 5.4 %collective-permute-start.13 = (f32[256,128]{1,0:T(8,128)S(1)}, f32[256,128]{1,0:T(8,128)S(1)}, u32[]{:S(2)}, u32[]{:S(2)}) collective-permute-start(f32[256,128]{1,0:T(8,128)S(1)} %get-tuple-element.8), channel_id=1, source_target_pairs={{2,0},{3,1},{0,2},{1,3},{6,4},{7,5},{4,6},{5,7},{10,8},{11,9},{8,1... | collective-permute-start | bytes 393224 | tf_op jit(solution)/shard_map/ppermute | solution.py:248
  124.3 5.3 %collective-permute-start.14 = (f32[256,128]{1,0:T(8,128)S(1)}, f32[256,128]{1,0:T(8,128)S(1)}, u32[]{:S(2)}, u32[]{:S(2)}) collective-permute-start(f32[256,128]{1,0:T(8,128)S(1)} %get-tuple-element.8), channel_id=1, source_target_pairs={{1,0},{2,1},{3,2},{0,3},{5,4},{6,5},{7,6},{4,7},{9,8},{10,9},{11,1... | collective-permute-start | bytes 393224 | tf_op jit(solution)/shard_map/ppermute | solution.py:248
  126.0 6.7 %collective-permute-start.15 = (f32[256,128]{1,0:T(8,128)S(1)}, f32[256,128]{1,0:T(8,128)S(1)}, u32[]{:S(2)}, u32[]{:S(2)}) collective-permute-start(f32[256,128]{1,0:T(8,128)S(1)} %get-tuple-element.8), channel_id=1, source_target_pairs={{3,0},{0,1},{1,2},{2,3},{7,4},{4,5},{5,6},{6,7},{11,8},{8,9},{9,10... | collective-permute-start | bytes 393224 | tf_op jit(solution)/shard_map/ppermute | solution.py:248
  132.8 5.4 %collective-permute-start.16 = (f32[256,128]{1,0:T(8,128)S(1)}, f32[256,128]{1,0:T(8,128)S(1)}, u32[]{:S(2)}, u32[]{:S(2)}) collective-permute-start(f32[256,128]{1,0:T(8,128)S(1)} %log_add_fusion), channel_id=1, source_target_pairs={{8,0},{9,1},{10,2},{11,3},{12,4},{13,5},{14,6},{15,7},{0,8},{1,9},... | collective-permute-start | bytes 393224 | tf_op jit(solution)/shard_map/ppermute | solution.py:248
  133.7 4.6 %collective-permute-start.17 = (f32[256,128]{1,0:T(8,128)S(1)}, f32[256,128]{1,0:T(8,128)S(1)}, u32[]{:S(2)}, u32[]{:S(2)}) collective-permute-start(f32[256,128]{1,0:T(8,128)S(1)} %log_add_fusion), channel_id=1, source_target_pairs={{4,0},{5,1},{6,2},{7,3},{8,4},{9,5},{10,6},{11,7},{12,8},{13,9},{1... | collective-permute-start | bytes 393224 | tf_op jit(solution)/shard_map/ppermute | solution.py:248
  134.4 6.4 %collective-permute-start.18 = (f32[256,128]{1,0:T(8,128)S(1)}, f32[256,128]{1,0:T(8,128)S(1)}, u32[]{:S(2)}, u32[]{:S(2)}) collective-permute-start(f32[256,128]{1,0:T(8,128)S(1)} %log_add_fusion), channel_id=1, source_target_pairs={{12,0},{13,1},{14,2},{15,3},{0,4},{1,5},{2,6},{3,7},{4,8},{5,9},{6... | collective-permute-start | bytes 393224 | tf_op jit(solution)/shard_map/ppermute | solution.py:248
  140.9 5.9 %copy-start = (f32[256,128]{1,0:T(8,128)}, f32[256,128]{1,0:T(8,128)S(1)}, u32[]{:S(2)}) copy-start(f32[256,128]{1,0:T(8,128)S(1)} %bitcast_subtract_fusion.pots_ref) | copy-start | bytes 393220
  161.5 3.5 %collective-permute-start.19 = (f32[128,128]{1,0:T(8,128)S(1)}, f32[128,128]{1,0:T(8,128)S(1)}, u32[]{:S(2)}, u32[]{:S(2)}) collective-permute-start(f32[128,128]{1,0:T(8,128)S(1)} %slice_select_fusion.2), channel_id=1, source_target_pairs={{16,0},{0,16},{48,32},{32,48},{80,64},{64,80},{112,96},{96,112},{1... | collective-permute-start | bytes 196616 | tf_op jit(solution)/shard_map/ppermute | solution.py:248
  165.1 3.2 %collective-permute-start.20 = (f32[128,128]{1,0:T(8,128)S(1)}, f32[128,128]{1,0:T(8,128)S(1)}, u32[]{:S(2)}, u32[]{:S(2)}) collective-permute-start(f32[128,128]{1,0:T(8,128)S(1)} %log_add_fusion.3), channel_id=1, source_target_pairs={{32,0},{48,16},{0,32},{16,48},{96,64},{112,80},{64,96},{80,112},{1... | collective-permute-start | bytes 196616 | tf_op jit(solution)/shard_map/ppermute | solution.py:248
  168.4 6.3 %collective-permute-start.21 = (f32[128,128]{1,0:T(8,128)S(1)}, f32[128,128]{1,0:T(8,128)S(1)}, u32[]{:S(2)}, u32[]{:S(2)}) collective-permute-start(f32[128,128]{1,0:T(8,128)S(1)} %log_add_fusion.2), channel_id=1, source_target_pairs={{160,0},{176,16},{128,32},{144,48},{224,64},{240,80},{192,96},{208... | collective-permute-start | bytes 196616 | tf_op jit(solution)/shard_map/ppermute | solution.py:248
  170.0 5.3 %collective-permute-start.22 = (f32[128,128]{1,0:T(8,128)S(1)}, f32[128,128]{1,0:T(8,128)S(1)}, u32[]{:S(2)}, u32[]{:S(2)}) collective-permute-start(f32[128,128]{1,0:T(8,128)S(1)} %log_add_fusion.2), channel_id=1, source_target_pairs={{224,0},{240,16},{64,32},{80,48},{32,64},{48,80},{128,96},{144,112... | collective-permute-start | bytes 196616 | tf_op jit(solution)/shard_map/ppermute | solution.py:248
  171.8 4.8 %collective-permute-start.23 = (f32[128,128]{1,0:T(8,128)S(1)}, f32[128,128]{1,0:T(8,128)S(1)}, u32[]{:S(2)}, u32[]{:S(2)}) collective-permute-start(f32[128,128]{1,0:T(8,128)S(1)} %log_add_fusion.2), channel_id=1, source_target_pairs={{64,0},{80,16},{224,32},{240,48},{128,64},{144,80},{32,96},{48,112... | collective-permute-start | bytes 196616 | tf_op jit(solution)/shard_map/ppermute | solution.py:248
  176.7 3.5 %collective-permute-start.24 = (f32[128,128]{1,0:T(8,128)S(1)}, f32[128,128]{1,0:T(8,128)S(1)}, u32[]{:S(2)}, u32[]{:S(2)}) collective-permute-start(f32[128,128]{1,0:T(8,128)S(1)} %fusion.15), channel_id=1, source_target_pairs={{16,0},{0,16},{48,32},{32,48},{80,64},{64,80},{112,96},{96,112},{1... | collective-permute-start | bytes 196616 | tf_op jit(solution)/shard_map/ppermute | solution.py:248

commit v4 on v3

--- a/solution.py
+++ b/solution.py
@@ -12,8 +12,9 @@
 VMEM = pltpu.VMEM
 SMEM = pltpu.SMEM
 VMEM_BYTES = 40 << 20
-CHUNKS = 4
+CHUNK = 16
 UNROLL = 64
+COL_UNROLL = 128
 EXTRA = 8
 
 
@@ -36,34 +37,13 @@
     return owner, local, rank, ask.reshape(owners, width).astype(jnp.float32)
 
 
-def stream(tiles_ref, held_ref, sems):
-    count = tiles_ref.shape[0]
-    parts = count // UNROLL
-    size = UNROLL // CHUNKS
-
-    def copy(g, i):
-        at = pl.ds(g * UNROLL + i * size, size)
-        return pltpu.make_async_copy(tiles_ref.at[at], held_ref.at[at], sems.at[g, i])
-
-    for g in range(parts):
-        for i in range(CHUNKS):
-            copy(g, i).start()
-
-    def ready(g):
-        for i in range(CHUNKS):
-            copy(g, i).wait()
-
-    return ready
-
-
 def pick_kernel(ids_ref, rows_ref, out_ref):
-    last = rows_ref.shape[0] - 1
     turn = 48
 
     def step(p, carry):
         for k in range(turn):
-            row = jnp.minimum(ids_ref[p * turn + k], last)
-            out_ref[pl.ds(p * turn + k, 1), :] = rows_ref[pl.ds(row, 1), :]
+            n = p * turn + k
+            out_ref[pl.ds(n, 1), :] = rows_ref[pl.ds(ids_ref[n], 1), :]
         return carry
 
     lax.fori_loop(0, out_ref.shape[0] // turn, step, 0)
@@ -83,7 +63,14 @@
 def row_kernel(slot_ref, tiles_ref, *refs):
     *pots_refs, out_ref, held_ref, sems = refs
     size = pots_refs[0].shape[0]
-    ready = stream(tiles_ref, held_ref, sems)
+    chunks = sems.shape[0]
+
+    def copy(c):
+        at = pl.ds(c * CHUNK, CHUNK)
+        return pltpu.make_async_copy(tiles_ref.at[at], held_ref.at[at], sems.at[c])
+
+    for c in range(chunks):
+        copy(c).start()
 
     def potential(slot):
         if len(pots_refs) == 1:
@@ -92,21 +79,23 @@
         near, far = (ref[pl.ds(slot - side * size, 1), :] for ref in pots_refs)
         return jnp.where(side == 0, near, far)
 
-    def step(g, carry):
-        ready(g)
+    def step(count, g, carry):
+        for c in range(count // CHUNK):
+            copy(g * (count // CHUNK) + c).wait()
         tops, sums = [], []
-        for k in range(UNROLL):
-            n = g * UNROLL + k
+        for k in range(count):
+            n = g * count + k
             pot = potential(slot_ref[n])
             scores = jnp.transpose(held_ref[n].astype(jnp.float32) + pot)
             top = jnp.max(scores, axis=0, keepdims=True)
             tops.append(top)
             sums.append(jnp.sum(jnp.exp(scores - top), axis=0, keepdims=True))
-        block = pl.ds(pl.multiple_of(g * UNROLL, UNROLL), UNROLL)
+        block = pl.ds(pl.multiple_of(g * count, count), count)
         out_ref[block, :] = jnp.concatenate(tops, 0) + jnp.log(jnp.concatenate(sums, 0))
         return carry
 
-    lax.fori_loop(0, tiles_ref.shape[0] // UNROLL, step, 0)
+    lax.fori_loop(0, UNROLL // CHUNK, functools.partial(step, CHUNK), 0)
+    lax.fori_loop(1, tiles_ref.shape[0] // UNROLL, functools.partial(step, UNROLL), 0)
 
 
 def row_pass(slot, tiles, *pots):
@@ -119,7 +108,7 @@
         ),
         in_specs=[spec(SMEM), spec(pltpu.HBM)] + [spec(VMEM)] * len(pots),
         out_specs=(spec(VMEM), spec(VMEM)),
-        scratch_shapes=[pltpu.SemaphoreType.DMA((tiles.shape[0] // UNROLL, CHUNKS))],
+        scratch_shapes=[pltpu.SemaphoreType.DMA((tiles.shape[0] // CHUNK,))],
         compiler_params=params(),
     )(slot, tiles, *pots)
 
@@ -135,19 +124,19 @@
 
     def step(g, carry):
         tops, sums = [], []
-        for k in range(UNROLL):
-            n = g * UNROLL + k
+        for k in range(COL_UNROLL):
+            n = g * COL_UNROLL + k
             pot = jnp.broadcast_to(pots_ref[pl.ds(n, 1), :], (width, width))
             scores = tiles_ref[n].astype(jnp.float32) + jnp.transpose(pot)
             top = jnp.max(scores, axis=0, keepdims=True)
             tops.append(top)
             sums.append(jnp.sum(jnp.exp(scores - top), axis=0, keepdims=True))
         row_ref[...] = jnp.concatenate(tops, 0) + jnp.log(jnp.concatenate(sums, 0))
-        for k in range(UNROLL):
-            out_ref[pl.ds(slot_ref[g * UNROLL + k], 1), :] = row_ref[pl.ds(k, 1), :]
+        for k in range(COL_UNROLL):
+            out_ref[pl.ds(slot_ref[g * COL_UNROLL + k], 1), :] = row_ref[pl.ds(k, 1), :]
         return carry
 
-    lax.fori_loop(0, tiles_ref.shape[0] // UNROLL, step, 0)
+    lax.fori_loop(0, tiles_ref.shape[0] // COL_UNROLL, step, 0)
 
 
 def col_pass(slot, tiles, pots, slots, capacity, *ask):
@@ -158,7 +147,7 @@
         out_shape=jax.ShapeDtypeStruct((slots, width), jnp.float32),
         in_specs=[spec(SMEM)] + [spec(VMEM)] * (2 + len(ask)),
         out_specs=spec(VMEM),
-        scratch_shapes=[VMEM((UNROLL, width), jnp.float32)],
+        scratch_shapes=[VMEM((COL_UNROLL, width), jnp.float32)],
         compiler_params=params(),
     )(slot, tiles, pots, *ask)
 
@@ -173,10 +162,10 @@
         for turn in range(turns):
 
             def step(p, carry):
-                for k in range(4):
+                for k in range(12):
                     for g, part in enumerate(parts):
                         source = g * turns + turn
-                        rank = p * 4 + k
+                        rank = p * 12 + k
                         visit(
                             part,
                             pl.ds(ids_ref[source * capacity + rank], 1),
@@ -184,7 +173,7 @@
                         )
                 return carry
 
-            lax.fori_loop(0, capacity // 4, step, 0)
+            lax.fori_loop(0, capacity // 12, step, 0)
 
     for part in parts:
         part[...] = jnp.full(part.shape, NEGATIVE, jnp.float32)
@@ -285,7 +274,9 @@
     def others(value):
         return jnp.where(first, value[half:], value[:half])
 
-    start_half = mine(start_pot.reshape(block_tiles, width))
+    start_half = lax.dynamic_slice_in_dim(
+        start_pot.reshape(block_tiles, width), core * half, half, 0
+    )
     target_half = mine(log_target.reshape(block_tiles, width))
     dust_half = mine(dustbin.reshape(block_tiles, width))
 
@@ -300,7 +291,7 @@
             row_lse, held = row_pass(place, tiles, near, far)
         else:
             row_lse, held = row_pass(
-                owner * capacity + rank, tiles, exchange(pick(ids, target_now), owners)
+                owner * capacity + rank, tiles, exchange(pick(picked, target_now), owners)
             )
         for phase in col_phases(owners):
             row_lse = log_sum(row_lse, *[swap(row_lse, "col", partner) for partner in phase])
@@ -313,6 +304,7 @@
             rows = exchange(rows, owners)
             ids = rows.reshape(owners, stride, width)[:, capacity, :capacity]
             ids = ids.astype(jnp.int32).reshape(owners * capacity)
+            picked = jnp.minimum(ids, block_tiles - 1)
         else:
             rows = col_pass(
                 owner * capacity + rank, held, source_now, owners * capacity, capacity

time: 181 us -> 181 us (level)
  blocking collectives: 61.9 us -> 47.4 us
  waiting for transfers between devices: 44.3 us -> 54 us
  starting transfers between devices: 37.1 us -> 42.4 us
    all_to_all x4 -> x3, blocking collectives: 61.9 us -> 47.4 us  [exchange(): lax.all_to_all(value.reshape((owners, shape[0] // owners) + shape[1:]), '...]
    all_to_all x0 -> x1, waiting for transfers between devices: none -> 9.78 us  [exchange(): lax.all_to_all(value.reshape((owners, shape[0] // owners) + shape[1:]), '...]
    all_to_all x0 -> x1, starting transfers between devices: none -> 4.91 us  [exchange(): lax.all_to_all(value.reshape((owners, shape[0] // owners) + shape[1:]), '...]
  transfers between devices with their start and end apart: 25 -> 26, of which waited for: 23 -> 24; matrix products, arithmetic and copies ran while one was open for 0% -> 0% of each run, Pallas kernels for 0% -> 0%
where the time goes in v4:
time: 181 us; the launch traced here: 180 us
  waiting for transfers between devices  54 us (30%)
  blocking collectives  47.4 us (26%)
  starting transfers between devices  42.4 us (23%)
  Pallas kernels  32.5 us (18%)
  other arithmetic  2.11 us (1%)
    all_to_all x3, blocking collectives, exchange(): lax.all_to_all(value.reshape((owners, shape[0] // owners) + shape[1:]), '...  47.4 us
    ppermute x25, waiting for transfers between devices, swap(): return lax.ppermute(value, axis, [(j, i) for i, j in enumerate(partner)])  44.2 us
    ppermute x25, starting transfers between devices, swap(): return lax.ppermute(value, axis, [(j, i) for i, j in enumerate(partner)])  37.5 us
    pallas_call x2, Pallas kernels, row_pass(): pl.pallas_call(row_kernel, name='row_pass', out_shape=(jax.ShapeDtypeStru...  14.1 us
    pallas_call x2, Pallas kernels, col_pass(): pl.pallas_call(functools.partial(col_kernel, capacity), name='col_pass',...  12.1 us
    all_to_all x1, waiting for transfers between devices, exchange(): lax.all_to_all(value.reshape((owners, shape[0] // owners) + shape[1:]), '...  9.78 us
    pallas_call x2, Pallas kernels, segment(): pl.pallas_call(functools.partial(segment_kernel, capacity), name='segment...  5.01 us
    all_to_all x1, starting transfers between devices, exchange(): lax.all_to_all(value.reshape((owners, shape[0] // owners) + shape[1:]), '...  4.91 us
  transfers between devices with their start and end apart: 26, of which 24 were waited for; matrix products, arithmetic and copies ran while one was open for 0% of the time, Pallas kernels for 0%

profile of v4, /device:TPU:1, one launch (start us, length us, event | category | flops | bytes accessed | tf_op | source)
XLA Modules:
  0.0 180.3 jit_solution(15080852378872690197)
XLA Ops:
  1.6 23.3 %all_to_all.20 = f32[16,128,128]{2,1,0:T(8,128)S(1)} all-to-all(f32[16,128,128]{2,1,0:T(8,128)S(1)} %reshape_tile.3), channel_id=1, replica_groups=mesh['row'=16,'col'=16] {'col'}, dimensions={0} | all-to-all | bytes 2097152 | tf_op jit(solution)/shard_map/all_to_all | solution.py:222
  24.9 1.9 %collective-permute-start = (f32[2048,128]{1,0:T(8,128)S(1)}, f32[2048,128]{1,0:T(8,128)S(1)}, u32[]{:S(2)}, u32[]{:S(2)}) collective-permute-start(f32[2048,128]{1,0:T(8,128)S(1)} %bitcast.67), channel_id=1, source_target_pairs={{16,0},{0,16},{48,32},{32,48},{80,64},{64,80},{112,96},{96,112},{1... | collective-permute-start | bytes 3145736 | tf_op jit(solution)/shard_map/ppermute | solution.py:237
  29.1 7.1 %row_pass.2 = (f32[256,128]{1,0:T(8,128)S(1)}, bf16[256,128,128]{2,1,0:T(8,128)(2,1)S(1)}) custom-call(s32[256]{0:T(256)S(1)} %get-tuple-element.12.slot_ref, bf16[256,128,128]{2,1,0:T(8,128)(2,1)} %bitcast.75, f32[2048,128]{1,0:T(8,128)S(1)} %bitcast.68, f32[2048,128]{1,0:T(8,128)S(1)} %collective-permute-done.refs_1_), custom_call_target="tpu_custom_call" | custom-call | tf_op jit(solution)/shard_map/row_pass/pallas_call | solution.py:102
  39.0 3.5 %collective-permute-done.1 = f32[256,128]{1,0:T(8,128)S(1)} collective-permute-done((f32[256,128]{1,0:T(8,128)S(1)}, f32[256,128]{1,0:T(8,128)S(1)}, u32[]{:S(2)}, u32[]{:S(2)}) %collective-permute-start.1) | collective-permute-done | bytes 131104 | tf_op jit(solution)/shard_map/ppermute | solution.py:237
  43.7 1.9 %collective-permute-done.3 = f32[256,128]{1,0:T(8,128)S(1)} collective-permute-done((f32[256,128]{1,0:T(8,128)S(1)}, f32[256,128]{1,0:T(8,128)S(1)}, u32[]{:S(2)}, u32[]{:S(2)}) %collective-permute-start.3) | collective-permute-done | bytes 131104 | tf_op jit(solution)/shard_map/ppermute | solution.py:237
  48.3 2.8 %collective-permute-done.4 = f32[256,128]{1,0:T(8,128)S(1)} collective-permute-done((f32[256,128]{1,0:T(8,128)S(1)}, f32[256,128]{1,0:T(8,128)S(1)}, u32[]{:S(2)}, u32[]{:S(2)}) %collective-permute-start.4) | collective-permute-done | bytes 131104 | tf_op jit(solution)/shard_map/ppermute | solution.py:237
  52.6 2.2 %collective-permute-done.6 = f32[256,128]{1,0:T(8,128)S(1)} collective-permute-done((f32[256,128]{1,0:T(8,128)S(1)}, f32[256,128]{1,0:T(8,128)S(1)}, u32[]{:S(2)}, u32[]{:S(2)}) %collective-permute-start.6) | collective-permute-done | bytes 131104 | tf_op jit(solution)/shard_map/ppermute | solution.py:237
  54.9 6.4 %col_pass.2 = f32[896,128]{1,0:T(8,128)} custom-call(s32[256]{0:T(256)S(1)} %get-tuple-element.14.slot_ref, bf16[256,128,128]{2,1,0:T(8,128)(2,1)S(1)} %get-tuple-element.6.tiles_ref, f32[256,128]{1,0:T(8,128)S(1)} %bitcast_subtract_fusion.1.pots_ref, f32[16,128]{1,0:T(8,128)S(1)} %convert_bitcast_fusion.refs_0_), custom_call_target="tpu_custom_call" | custom-call | tf_op jit(solution)/shard_map/col_pass/pallas_call | solution.py:144
  61.4 4.9 %all-to-all-start.1 = ((f32[16,56,128]{2,1,0:T(8,128)}), f32[16,56,128]{2,1,0:T(8,128)S(1)}, u32[]{:S(2)}, u32[]{:S(2)}) async-start(f32[16,56,128]{2,1,0:T(8,128)} %bitcast.10), calls=%async_computation.1 | async-start | bytes 917504 | tf_op jit(solution)/shard_map/all_to_all | solution.py:222
  66.3 9.8 %all-to-all-done.1 = f32[16,56,128]{2,1,0:T(8,128)S(1)} async-done(((f32[16,56,128]{2,1,0:T(8,128)}), f32[16,56,128]{2,1,0:T(8,128)S(1)}, u32[]{:S(2)}, u32[]{:S(2)}) %all-to-all-start.1) | async-done | bytes 458784 | tf_op jit(solution)/shard_map/all_to_all | solution.py:222
  76.2 2.5 %segment.2 = f32[256,128]{1,0:T(8,128)S(1)} custom-call(s32[768]{0:T(1024)S(1)} %convert_element_type.19.ids_ref, f32[896,128]{1,0:T(8,128)S(1)} %bitcast.69), custom_call_target="tpu_custom_call" | custom-call | tf_op jit(solution)/shard_map/segment/pallas_call | solution.py:209
  78.7 2.0 %collective-permute-start.7 = (f32[128,128]{1,0:T(8,128)S(1)}, f32[128,128]{1,0:T(8,128)S(1)}, u32[]{:S(2)}, u32[]{:S(2)}) collective-permute-start(f32[128,128]{1,0:T(8,128)S(1)} %slice_select_fusion.3), channel_id=1, source_target_pairs={{16,0},{0,16},{48,32},{32,48},{80,64},{64,80},{112,96},{96,112},{1... | collective-permute-start | bytes 196616 | tf_op jit(solution)/shard_map/ppermute | solution.py:237
  81.7 1.9 %collective-permute-start.8 = (f32[128,128]{1,0:T(8,128)S(1)}, f32[128,128]{1,0:T(8,128)S(1)}, u32[]{:S(2)}, u32[]{:S(2)}) collective-permute-start(f32[128,128]{1,0:T(8,128)S(1)} %log_add_fusion.5), channel_id=1, source_target_pairs={{32,0},{48,16},{0,32},{16,48},{96,64},{112,80},{64,96},{80,112},{1... | collective-permute-start | bytes 196616 | tf_op jit(solution)/shard_map/ppermute | solution.py:237
  83.6 2.1 %collective-permute-done.8 = f32[128,128]{1,0:T(8,128)S(1)} collective-permute-done((f32[128,128]{1,0:T(8,128)S(1)}, f32[128,128]{1,0:T(8,128)S(1)}, u32[]{:S(2)}, u32[]{:S(2)}) %collective-permute-start.8) | collective-permute-done | bytes 65568 | tf_op jit(solution)/shard_map/ppermute | solution.py:237
  85.7 5.1 %collective-permute-start.10 = (f32[128,128]{1,0:T(8,128)S(1)}, f32[128,128]{1,0:T(8,128)S(1)}, u32[]{:S(2)}, u32[]{:S(2)}) collective-permute-start(f32[128,128]{1,0:T(8,128)S(1)} %log_add_fusion.4), channel_id=1, source_target_pairs={{224,0},{240,16},{64,32},{80,48},{32,64},{48,80},{128,96},{144,112... | collective-permute-start | bytes 196616 | tf_op jit(solution)/shard_map/ppermute | solution.py:237
  93.0 1.8 %collective-permute-done.11 = f32[128,128]{1,0:T(8,128)S(1)} collective-permute-done((f32[128,128]{1,0:T(8,128)S(1)}, f32[128,128]{1,0:T(8,128)S(1)}, u32[]{:S(2)}, u32[]{:S(2)}) %collective-permute-start.11) | collective-permute-done | bytes 65568 | tf_op jit(solution)/shard_map/ppermute | solution.py:237
  94.8 3.6 %collective-permute-done.9 = f32[128,128]{1,0:T(8,128)S(1)} collective-permute-done((f32[128,128]{1,0:T(8,128)S(1)}, f32[128,128]{1,0:T(8,128)S(1)}, u32[]{:S(2)}, u32[]{:S(2)}) %collective-permute-start.9) | collective-permute-done | bytes 65568 | tf_op jit(solution)/shard_map/ppermute | solution.py:237
  98.6 3.3 %collective-permute-start.12 = (f32[128,128]{1,0:T(8,128)S(1)}, f32[128,128]{1,0:T(8,128)S(1)}, u32[]{:S(2)}, u32[]{:S(2)}) collective-permute-start(f32[128,128]{1,0:T(8,128)S(1)} %fusion.8), channel_id=1, source_target_pairs={{16,0},{0,16},{48,32},{32,48},{80,64},{64,80},{112,96},{96,112},{1... | collective-permute-start | bytes 196616 | tf_op jit(solution)/shard_map/ppermute | solution.py:237
  104.0 12.3 %all_to_all.21 = f32[16,48,128]{2,1,0:T(8,128)S(1)} all-to-all(f32[16,48,128]{2,1,0:T(8,128)S(1)} %bitcast.72), channel_id=1, replica_groups=mesh['row'=16,'col'=16] {'col'}, dimensions={0} | all-to-all | bytes 786432 | tf_op jit(solution)/shard_map/all_to_all | solution.py:222
  116.3 7.0 %row_pass.3 = (f32[256,128]{1,0:T(8,128)S(1)}, bf16[256,128,128]{2,1,0:T(8,128)(2,1)S(1)}) custom-call(s32[256]{0:T(256)S(1)} %get-tuple-element.15.slot_ref, bf16[256,128,128]{2,1,0:T(8,128)(2,1)} %bitcast.76, f32[768,128]{1,0:T(8,128)S(1)} %bitcast.70), custom_call_target="tpu_custom_call" | custom-call | tf_op jit(solution)/shard_map/row_pass/pallas_call | solution.py:102
  124.3 1.8 collective-permute-start.14
  126.1 2.6 %collective-permute-done.13 = f32[256,128]{1,0:T(8,128)S(1)} collective-permute-done((f32[256,128]{1,0:T(8,128)S(1)}, f32[256,128]{1,0:T(8,128)S(1)}, u32[]{:S(2)}, u32[]{:S(2)}) %collective-permute-start.13) | collective-permute-done | bytes 131104 | tf_op jit(solution)/shard_map/ppermute | solution.py:237
  129.6 3.2 %collective-permute-done.15 = f32[256,128]{1,0:T(8,128)S(1)} collective-permute-done((f32[256,128]{1,0:T(8,128)S(1)}, f32[256,128]{1,0:T(8,128)S(1)}, u32[]{:S(2)}, u32[]{:S(2)}) %collective-permute-start.15) | collective-permute-done | bytes 131104 | tf_op jit(solution)/shard_map/ppermute | solution.py:237
  135.2 3.1 %collective-permute-done.16 = f32[256,128]{1,0:T(8,128)S(1)} collective-permute-done((f32[256,128]{1,0:T(8,128)S(1)}, f32[256,128]{1,0:T(8,128)S(1)}, u32[]{:S(2)}, u32[]{:S(2)}) %collective-permute-start.16) | collective-permute-done | bytes 131104 | tf_op jit(solution)/shard_map/ppermute | solution.py:237
  138.3 2.5 %collective-permute-done.18 = f32[256,128]{1,0:T(8,128)S(1)} collective-permute-done((f32[256,128]{1,0:T(8,128)S(1)}, f32[256,128]{1,0:T(8,128)S(1)}, u32[]{:S(2)}, u32[]{:S(2)}) %collective-permute-start.18) | collective-permute-done | bytes 131104 | tf_op jit(solution)/shard_map/ppermute | solution.py:237
  141.0 5.7 %col_pass.3 = f32[768,128]{1,0:T(8,128)S(1)} custom-call(s32[256]{0:T(256)S(1)} %get-tuple-element.15.slot_ref, bf16[256,128,128]{2,1,0:T(8,128)(2,1)S(1)} %get-tuple-element.9.tiles_ref, f32[256,128]{1,0:T(8,128)S(1)} %bitcast_subtract_fusion.pots_ref), custom_call_target="tpu_custom_call" | custom-call | tf_op jit(solution)/shard_map/col_pass/pallas_call | solution.py:144
  146.6 11.9 %all_to_all.22 = f32[16,48,128]{2,1,0:T(8,128)S(1)} all-to-all(f32[16,48,128]{2,1,0:T(8,128)S(1)} %bitcast.71), channel_id=1, replica_groups=mesh['row'=16,'col'=16] {'col'}, dimensions={0} | all-to-all | bytes 786432 | tf_op jit(solution)/shard_map/all_to_all | solution.py:222
  158.5 2.5 %segment.3 = f32[256,128]{1,0:T(8,128)S(1)} custom-call(s32[768]{0:T(1024)S(1)} %convert_element_type.19.ids_ref, f32[768,128]{1,0:T(8,128)S(1)} %bitcast.73), custom_call_target="tpu_custom_call" | custom-call | tf_op jit(solution)/shard_map/segment/pallas_call | solution.py:209
  161.1 2.7 %collective-permute-start.19 = (f32[128,128]{1,0:T(8,128)S(1)}, f32[128,128]{1,0:T(8,128)S(1)}, u32[]{:S(2)}, u32[]{:S(2)}) collective-permute-start(f32[128,128]{1,0:T(8,128)S(1)} %slice_select_fusion.2), channel_id=1, source_target_pairs={{16,0},{0,16},{48,32},{32,48},{80,64},{64,80},{112,96},{96,112},{1... | collective-permute-start | bytes 196616 | tf_op jit(solution)/shard_map/ppermute | solution.py:237
  165.2 2.8 %collective-permute-done.20 = f32[128,128]{1,0:T(8,128)S(1)} collective-permute-done((f32[128,128]{1,0:T(8,128)S(1)}, f32[128,128]{1,0:T(8,128)S(1)}, u32[]{:S(2)}, u32[]{:S(2)}) %collective-permute-start.20) | collective-permute-done | bytes 65568 | tf_op jit(solution)/shard_map/ppermute | solution.py:237
  169.5 1.8 %collective-permute-start.22 = (f32[128,128]{1,0:T(8,128)S(1)}, f32[128,128]{1,0:T(8,128)S(1)}, u32[]{:S(2)}, u32[]{:S(2)}) collective-permute-start(f32[128,128]{1,0:T(8,128)S(1)} %log_add_fusion.2), channel_id=1, source_target_pairs={{224,0},{240,16},{64,32},{80,48},{32,64},{48,80},{128,96},{144,112... | collective-permute-start | bytes 196616 | tf_op jit(solution)/shard_map/ppermute | solution.py:237
  176.1 2.7 %collective-permute-start.24 = (f32[128,128]{1,0:T(8,128)S(1)}, f32[128,128]{1,0:T(8,128)S(1)}, u32[]{:S(2)}, u32[]{:S(2)}) collective-permute-start(f32[128,128]{1,0:T(8,128)S(1)} %fusion.15), channel_id=1, source_target_pairs={{16,0},{0,16},{48,32},{32,48},{80,64},{64,80},{112,96},{96,112},{1... | collective-permute-start | bytes 196616 | tf_op jit(solution)/shard_map/ppermute | solution.py:237
  (69 shorter events, 30.7 us)
Async XLA Ops:
  0.6 0.9 copy-start
  0.6 26.2 %copy-start.5 = (s32[256,1]{0,1:T(1,128)S(1)}, s32[256,1]{0,1:T(1,128)}, u32[]{:S(2)}) copy-start(s32[256,1]{0,1:T(1,128)} %param.7) | copy-start | bytes 3076
  24.9 4.2 %collective-permute-start = (f32[2048,128]{1,0:T(8,128)S(1)}, f32[2048,128]{1,0:T(8,128)S(1)}, u32[]{:S(2)}, u32[]{:S(2)}) collective-permute-start(f32[2048,128]{1,0:T(8,128)S(1)} %bitcast.67), channel_id=1, source_target_pairs={{16,0},{0,16},{48,32},{32,48},{80,64},{64,80},{112,96},{96,112},{1... | collective-permute-start | bytes 3145736 | tf_op jit(solution)/shard_map/ppermute | solution.py:237
  29.1 25.7 %copy-start.2 = (f32[32768]{0:T(1024)S(1)}, f32[32768]{0:T(1024)}, u32[]{:S(2)}) copy-start(f32[32768]{0:T(1024)} %param.9) | copy-start | bytes 393220
  36.3 6.3 %collective-permute-start.1 = (f32[256,128]{1,0:T(8,128)S(1)}, f32[256,128]{1,0:T(8,128)S(1)}, u32[]{:S(2)}, u32[]{:S(2)}) collective-permute-start(f32[256,128]{1,0:T(8,128)S(1)} %get-tuple-element.7), channel_id=1, source_target_pairs={{2,0},{3,1},{0,2},{1,3},{6,4},{7,5},{4,6},{5,7},{10,8},{11,9},{8,1... | collective-permute-start | bytes 393224 | tf_op jit(solution)/shard_map/ppermute | solution.py:237
  37.5 6.1 %collective-permute-start.2 = (f32[256,128]{1,0:T(8,128)S(1)}, f32[256,128]{1,0:T(8,128)S(1)}, u32[]{:S(2)}, u32[]{:S(2)}) collective-permute-start(f32[256,128]{1,0:T(8,128)S(1)} %get-tuple-element.7), channel_id=1, source_target_pairs={{1,0},{2,1},{3,2},{0,3},{5,4},{6,5},{7,6},{4,7},{9,8},{10,9},{11,1... | collective-permute-start | bytes 393224 | tf_op jit(solution)/shard_map/ppermute | solution.py:237
  38.9 6.7 %collective-permute-start.3 = (f32[256,128]{1,0:T(8,128)S(1)}, f32[256,128]{1,0:T(8,128)S(1)}, u32[]{:S(2)}, u32[]{:S(2)}) collective-permute-start(f32[256,128]{1,0:T(8,128)S(1)} %get-tuple-element.7), channel_id=1, source_target_pairs={{3,0},{0,1},{1,2},{2,3},{7,4},{4,5},{5,6},{6,7},{11,8},{8,9},{9,10... | collective-permute-start | bytes 393224 | tf_op jit(solution)/shard_map/ppermute | solution.py:237
  45.7 5.4 %collective-permute-start.4 = (f32[256,128]{1,0:T(8,128)S(1)}, f32[256,128]{1,0:T(8,128)S(1)}, u32[]{:S(2)}, u32[]{:S(2)}) collective-permute-start(f32[256,128]{1,0:T(8,128)S(1)} %log_add_fusion.1), channel_id=1, source_target_pairs={{8,0},{9,1},{10,2},{11,3},{12,4},{13,5},{14,6},{15,7},{0,8},{1,9},... | collective-permute-start | bytes 393224 | tf_op jit(solution)/shard_map/ppermute | solution.py:237
  46.8 5.8 %collective-permute-start.5 = (f32[256,128]{1,0:T(8,128)S(1)}, f32[256,128]{1,0:T(8,128)S(1)}, u32[]{:S(2)}, u32[]{:S(2)}) collective-permute-start(f32[256,128]{1,0:T(8,128)S(1)} %log_add_fusion.1), channel_id=1, source_target_pairs={{4,0},{5,1},{6,2},{7,3},{8,4},{9,5},{10,6},{11,7},{12,8},{13,9},{1... | collective-permute-start | bytes 393224 | tf_op jit(solution)/shard_map/ppermute | solution.py:237
  48.0 6.8 %collective-permute-start.6 = (f32[256,128]{1,0:T(8,128)S(1)}, f32[256,128]{1,0:T(8,128)S(1)}, u32[]{:S(2)}, u32[]{:S(2)}) collective-permute-start(f32[256,128]{1,0:T(8,128)S(1)} %log_add_fusion.1), channel_id=1, source_target_pairs={{12,0},{13,1},{14,2},{15,3},{0,4},{1,5},{2,6},{3,7},{4,8},{5,9},{6... | collective-permute-start | bytes 393224 | tf_op jit(solution)/shard_map/ppermute | solution.py:237
  61.3 37.1 %copy-start.3 = (f32[32768]{0:T(1024)S(1)}, f32[32768]{0:T(1024)}, u32[]{:S(2)}) copy-start(f32[32768]{0:T(1024)} %param.10) | copy-start | bytes 393220
  61.3 37.1 %copy-start.4 = (f32[32768]{0:T(1024)S(1)}, f32[32768]{0:T(1024)}, u32[]{:S(2)}) copy-start(f32[32768]{0:T(1024)} %param.11) | copy-start | bytes 393220
  61.4 14.7 %all-to-all-start.1 = ((f32[16,56,128]{2,1,0:T(8,128)}), f32[16,56,128]{2,1,0:T(8,128)S(1)}, u32[]{:S(2)}, u32[]{:S(2)}) async-start(f32[16,56,128]{2,1,0:T(8,128)} %bitcast.10), calls=%async_computation.1 | async-start | bytes 917504 | tf_op jit(solution)/shard_map/all_to_all | solution.py:222
  78.7 2.9 %collective-permute-start.7 = (f32[128,128]{1,0:T(8,128)S(1)}, f32[128,128]{1,0:T(8,128)S(1)}, u32[]{:S(2)}, u32[]{:S(2)}) collective-permute-start(f32[128,128]{1,0:T(8,128)S(1)} %slice_select_fusion.3), channel_id=1, source_target_pairs={{16,0},{0,16},{48,32},{32,48},{80,64},{64,80},{112,96},{96,112},{1... | collective-permute-start | bytes 196616 | tf_op jit(solution)/shard_map/ppermute | solution.py:237
  81.7 4.0 %collective-permute-start.8 = (f32[128,128]{1,0:T(8,128)S(1)}, f32[128,128]{1,0:T(8,128)S(1)}, u32[]{:S(2)}, u32[]{:S(2)}) collective-permute-start(f32[128,128]{1,0:T(8,128)S(1)} %log_add_fusion.5), channel_id=1, source_target_pairs={{32,0},{48,16},{0,32},{16,48},{96,64},{112,80},{64,96},{80,112},{1... | collective-permute-start | bytes 196616 | tf_op jit(solution)/shard_map/ppermute | solution.py:237
  85.7 7.2 %collective-permute-start.10 = (f32[128,128]{1,0:T(8,128)S(1)}, f32[128,128]{1,0:T(8,128)S(1)}, u32[]{:S(2)}, u32[]{:S(2)}) collective-permute-start(f32[128,128]{1,0:T(8,128)S(1)} %log_add_fusion.4), channel_id=1, source_target_pairs={{224,0},{240,16},{64,32},{80,48},{32,64},{48,80},{128,96},{144,112... | collective-permute-start | bytes 196616 | tf_op jit(solution)/shard_map/ppermute | solution.py:237
  90.8 4.0 %collective-permute-start.11 = (f32[128,128]{1,0:T(8,128)S(1)}, f32[128,128]{1,0:T(8,128)S(1)}, u32[]{:S(2)}, u32[]{:S(2)}) collective-permute-start(f32[128,128]{1,0:T(8,128)S(1)} %log_add_fusion.4), channel_id=1, source_target_pairs={{64,0},{80,16},{224,32},{240,48},{128,64},{144,80},{32,96},{48,112... | collective-permute-start | bytes 196616 | tf_op jit(solution)/shard_map/ppermute | solution.py:237
  92.0 6.5 %collective-permute-start.9 = (f32[128,128]{1,0:T(8,128)S(1)}, f32[128,128]{1,0:T(8,128)S(1)}, u32[]{:S(2)}, u32[]{:S(2)}) collective-permute-start(f32[128,128]{1,0:T(8,128)S(1)} %log_add_fusion.4), channel_id=1, source_target_pairs={{160,0},{176,16},{128,32},{144,48},{224,64},{240,80},{192,96},{208... | collective-permute-start | bytes 196616 | tf_op jit(solution)/shard_map/ppermute | solution.py:237
  98.6 4.2 %collective-permute-start.12 = (f32[128,128]{1,0:T(8,128)S(1)}, f32[128,128]{1,0:T(8,128)S(1)}, u32[]{:S(2)}, u32[]{:S(2)}) collective-permute-start(f32[128,128]{1,0:T(8,128)S(1)} %fusion.8), channel_id=1, source_target_pairs={{16,0},{0,16},{48,32},{32,48},{80,64},{64,80},{112,96},{96,112},{1... | collective-permute-start | bytes 196616 | tf_op jit(solution)/shard_map/ppermute | solution.py:237
  123.3 5.4 %collective-permute-start.13 = (f32[256,128]{1,0:T(8,128)S(1)}, f32[256,128]{1,0:T(8,128)S(1)}, u32[]{:S(2)}, u32[]{:S(2)}) collective-permute-start(f32[256,128]{1,0:T(8,128)S(1)} %get-tuple-element.8), channel_id=1, source_target_pairs={{2,0},{3,1},{0,2},{1,3},{6,4},{7,5},{4,6},{5,7},{10,8},{11,9},{8,1... | collective-permute-start | bytes 393224 | tf_op jit(solution)/shard_map/ppermute | solution.py:237
  124.3 5.3 %collective-permute-start.14 = (f32[256,128]{1,0:T(8,128)S(1)}, f32[256,128]{1,0:T(8,128)S(1)}, u32[]{:S(2)}, u32[]{:S(2)}) collective-permute-start(f32[256,128]{1,0:T(8,128)S(1)} %get-tuple-element.8), channel_id=1, source_target_pairs={{1,0},{2,1},{3,2},{0,3},{5,4},{6,5},{7,6},{4,7},{9,8},{10,9},{11,1... | collective-permute-start | bytes 393224 | tf_op jit(solution)/shard_map/ppermute | solution.py:237
  126.1 6.7 %collective-permute-start.15 = (f32[256,128]{1,0:T(8,128)S(1)}, f32[256,128]{1,0:T(8,128)S(1)}, u32[]{:S(2)}, u32[]{:S(2)}) collective-permute-start(f32[256,128]{1,0:T(8,128)S(1)} %get-tuple-element.8), channel_id=1, source_target_pairs={{3,0},{0,1},{1,2},{2,3},{7,4},{4,5},{5,6},{6,7},{11,8},{8,9},{9,10... | collective-permute-start | bytes 393224 | tf_op jit(solution)/shard_map/ppermute | solution.py:237
  132.9 5.4 %collective-permute-start.16 = (f32[256,128]{1,0:T(8,128)S(1)}, f32[256,128]{1,0:T(8,128)S(1)}, u32[]{:S(2)}, u32[]{:S(2)}) collective-permute-start(f32[256,128]{1,0:T(8,128)S(1)} %log_add_fusion), channel_id=1, source_target_pairs={{8,0},{9,1},{10,2},{11,3},{12,4},{13,5},{14,6},{15,7},{0,8},{1,9},... | collective-permute-start | bytes 393224 | tf_op jit(solution)/shard_map/ppermute | solution.py:237
  133.7 4.6 %collective-permute-start.17 = (f32[256,128]{1,0:T(8,128)S(1)}, f32[256,128]{1,0:T(8,128)S(1)}, u32[]{:S(2)}, u32[]{:S(2)}) collective-permute-start(f32[256,128]{1,0:T(8,128)S(1)} %log_add_fusion), channel_id=1, source_target_pairs={{4,0},{5,1},{6,2},{7,3},{8,4},{9,5},{10,6},{11,7},{12,8},{13,9},{1... | collective-permute-start | bytes 393224 | tf_op jit(solution)/shard_map/ppermute | solution.py:237
  134.5 6.4 %collective-permute-start.18 = (f32[256,128]{1,0:T(8,128)S(1)}, f32[256,128]{1,0:T(8,128)S(1)}, u32[]{:S(2)}, u32[]{:S(2)}) collective-permute-start(f32[256,128]{1,0:T(8,128)S(1)} %log_add_fusion), channel_id=1, source_target_pairs={{12,0},{13,1},{14,2},{15,3},{0,4},{1,5},{2,6},{3,7},{4,8},{5,9},{6... | collective-permute-start | bytes 393224 | tf_op jit(solution)/shard_map/ppermute | solution.py:237
  141.0 5.7 %copy-start.1 = (f32[256,128]{1,0:T(8,128)}, f32[256,128]{1,0:T(8,128)S(1)}, u32[]{:S(2)}) copy-start(f32[256,128]{1,0:T(8,128)S(1)} %bitcast_subtract_fusion.pots_ref) | copy-start | bytes 393220
  161.1 3.6 %collective-permute-start.19 = (f32[128,128]{1,0:T(8,128)S(1)}, f32[128,128]{1,0:T(8,128)S(1)}, u32[]{:S(2)}, u32[]{:S(2)}) collective-permute-start(f32[128,128]{1,0:T(8,128)S(1)} %slice_select_fusion.2), channel_id=1, source_target_pairs={{16,0},{0,16},{48,32},{32,48},{80,64},{64,80},{112,96},{96,112},{1... | collective-permute-start | bytes 196616 | tf_op jit(solution)/shard_map/ppermute | solution.py:237
  164.7 3.2 %collective-permute-start.20 = (f32[128,128]{1,0:T(8,128)S(1)}, f32[128,128]{1,0:T(8,128)S(1)}, u32[]{:S(2)}, u32[]{:S(2)}) collective-permute-start(f32[128,128]{1,0:T(8,128)S(1)} %log_add_fusion.3), channel_id=1, source_target_pairs={{32,0},{48,16},{0,32},{16,48},{96,64},{112,80},{64,96},{80,112},{1... | collective-permute-start | bytes 196616 | tf_op jit(solution)/shard_map/ppermute | solution.py:237
  168.0 6.3 %collective-permute-start.21 = (f32[128,128]{1,0:T(8,128)S(1)}, f32[128,128]{1,0:T(8,128)S(1)}, u32[]{:S(2)}, u32[]{:S(2)}) collective-permute-start(f32[128,128]{1,0:T(8,128)S(1)} %log_add_fusion.2), channel_id=1, source_target_pairs={{160,0},{176,16},{128,32},{144,48},{224,64},{240,80},{192,96},{208... | collective-permute-start | bytes 196616 | tf_op jit(solution)/shard_map/ppermute | solution.py:237
  169.5 5.2 %collective-permute-start.22 = (f32[128,128]{1,0:T(8,128)S(1)}, f32[128,128]{1,0:T(8,128)S(1)}, u32[]{:S(2)}, u32[]{:S(2)}) collective-permute-start(f32[128,128]{1,0:T(8,128)S(1)} %log_add_fusion.2), channel_id=1, source_target_pairs={{224,0},{240,16},{64,32},{80,48},{32,64},{48,80},{128,96},{144,112... | collective-permute-start | bytes 196616 | tf_op jit(solution)/shard_map/ppermute | solution.py:237
  171.3 4.7 %collective-permute-start.23 = (f32[128,128]{1,0:T(8,128)S(1)}, f32[128,128]{1,0:T(8,128)S(1)}, u32[]{:S(2)}, u32[]{:S(2)}) collective-permute-start(f32[128,128]{1,0:T(8,128)S(1)} %log_add_fusion.2), channel_id=1, source_target_pairs={{64,0},{80,16},{224,32},{240,48},{128,64},{144,80},{32,96},{48,112... | collective-permute-start | bytes 196616 | tf_op jit(solution)/shard_map/ppermute | solution.py:237
  176.1 3.6 %collective-permute-start.24 = (f32[128,128]{1,0:T(8,128)S(1)}, f32[128,128]{1,0:T(8,128)S(1)}, u32[]{:S(2)}, u32[]{:S(2)}) collective-permute-start(f32[128,128]{1,0:T(8,128)S(1)} %fusion.15), channel_id=1, source_target_pairs={{16,0},{0,16},{48,32},{32,48},{80,64},{64,80},{112,96},{96,112},{1... | collective-permute-start | bytes 196616 | tf_op jit(solution)/shard_map/ppermute | solution.py:237

commit v5 on v4

--- a/solution.py
+++ b/solution.py
@@ -263,7 +263,6 @@
     capacity = min(tile_count // 2, 3 * tile_count // owners)
     half = block_tiles // 2
     core = lax.axis_index("row") & 1
-    first = core == 0
     other_core = [i ^ 1 for i in range(lax.axis_size("row"))]
 
     source_rows = log_source.reshape(row_tiles, width)
@@ -277,15 +276,15 @@
     start_half = lax.dynamic_slice_in_dim(
         start_pot.reshape(block_tiles, width), core * half, half, 0
     )
-    target_half = mine(log_target.reshape(block_tiles, width))
-    dust_half = mine(dustbin.reshape(block_tiles, width))
-
     tiles = kernel.reshape(tile_count, width, width)
     owner, local, rank, ask = plan(tile_cols.reshape(tile_count), block_tiles, owners, width)
     side = local // half
     place = (side ^ core) * (owners * half) + owner * half + local - side * half
     near = exchange(jnp.tile(start_half, (owners, 1)), owners)
     far = swap(near, "row", other_core)
+    place, first = lax.optimization_barrier((place, core == 0))
+    target_half = mine(log_target.reshape(block_tiles, width))
+    dust_half = mine(dustbin.reshape(block_tiles, width))
     for repeat in range(ITERS):
         if repeat == 0:
             row_lse, held = row_pass(place, tiles, near, far)

time: 181 us -> 180 us (level)
  blocking collectives: 47.4 us -> 62 us
  waiting for transfers between devices: 54 us -> 44.3 us
  starting transfers between devices: 42.4 us -> 37.3 us
    all_to_all x3 -> x4, blocking collectives: 47.4 us -> 62 us  [exchange(): lax.all_to_all(value.reshape((owners, shape[0] // owners) + shape[1:]), '...]
    all_to_all x1 -> x0, waiting for transfers between devices: 9.78 us -> none  [exchange(): lax.all_to_all(value.reshape((owners, shape[0] // owners) + shape[1:]), '...]
    all_to_all x1 -> x0, starting transfers between devices: 4.91 us -> none  [exchange(): lax.all_to_all(value.reshape((owners, shape[0] // owners) + shape[1:]), '...]
  transfers between devices with their start and end apart: 26 -> 25, of which waited for: 24 -> 23; matrix products, arithmetic and copies ran while one was open for 0% -> 0% of each run, Pallas kernels for 0% -> 0%
where the time goes in v5:
time: 180 us; the launch traced here: 179 us
  blocking collectives  62 us (34%)
  waiting for transfers between devices  44.3 us (25%)
  starting transfers between devices  37.3 us (21%)
  Pallas kernels  31.7 us (18%)
  other arithmetic  2.11 us (1%)
    all_to_all x4, blocking collectives, exchange(): lax.all_to_all(value.reshape((owners, shape[0] // owners) + shape[1:]), '...  62 us
    ppermute x25, waiting for transfers between devices, swap(): return lax.ppermute(value, axis, [(j, i) for i, j in enumerate(partner)])  44.3 us
    ppermute x25, starting transfers between devices, swap(): return lax.ppermute(value, axis, [(j, i) for i, j in enumerate(partner)])  37.3 us
    pallas_call x2, Pallas kernels, row_pass(): pl.pallas_call(row_kernel, name='row_pass', out_shape=(jax.ShapeDtypeStru...  14.1 us
    pallas_call x2, Pallas kernels, col_pass(): pl.pallas_call(functools.partial(col_kernel, capacity), name='col_pass',...  11.4 us
    pallas_call x2, Pallas kernels, segment(): pl.pallas_call(functools.partial(segment_kernel, capacity), name='segment...  5.01 us
  transfers between devices with their start and end apart: 25, of which 23 were waited for; matrix products, arithmetic and copies ran while one was open for 0% of the time, Pallas kernels for 0%

profile of v5, /device:TPU:1, one launch (start us, length us, event | category | flops | bytes accessed | tf_op | source)
XLA Modules:
  0.0 179.3 jit_solution(8883767944124275731)
XLA Ops:
  1.6 23.3 %all_to_all.20 = f32[16,128,128]{2,1,0:T(8,128)S(1)} all-to-all(f32[16,128,128]{2,1,0:T(8,128)S(1)} %reshape_tile.3), channel_id=1, replica_groups=mesh['row'=16,'col'=16] {'col'}, dimensions={0} | all-to-all | bytes 2097152 | tf_op jit(solution)/shard_map/all_to_all | solution.py:222
  24.9 1.9 %collective-permute-start = (f32[2048,128]{1,0:T(8,128)S(1)}, f32[2048,128]{1,0:T(8,128)S(1)}, u32[]{:S(2)}, u32[]{:S(2)}) collective-permute-start(f32[2048,128]{1,0:T(8,128)S(1)} %bitcast.67), channel_id=1, source_target_pairs={{16,0},{0,16},{48,32},{32,48},{80,64},{64,80},{112,96},{96,112},{1... | collective-permute-start | bytes 3145736 | tf_op jit(solution)/shard_map/ppermute | solution.py:237
  27.4 1.7 collective-permute-done.refs_1_
  29.1 7.1 %row_pass.2 = (f32[256,128]{1,0:T(8,128)S(1)}, bf16[256,128,128]{2,1,0:T(8,128)(2,1)S(1)}) custom-call(s32[256]{0:T(256)S(1)} %get-tuple-element.8.slot_ref, bf16[256,128,128]{2,1,0:T(8,128)(2,1)} %bitcast.76, f32[2048,128]{1,0:T(8,128)S(1)} %bitcast.68, f32[2048,128]{1,0:T(8,128)S(1)} %collective-permute-done.refs_1_), custom_call_target="tpu_custom_call" | custom-call | tf_op jit(solution)/shard_map/row_pass/pallas_call | solution.py:102
  39.0 3.6 %collective-permute-done.1 = f32[256,128]{1,0:T(8,128)S(1)} collective-permute-done((f32[256,128]{1,0:T(8,128)S(1)}, f32[256,128]{1,0:T(8,128)S(1)}, u32[]{:S(2)}, u32[]{:S(2)}) %collective-permute-start.1) | collective-permute-done | bytes 131104 | tf_op jit(solution)/shard_map/ppermute | solution.py:237
  43.7 1.9 %collective-permute-done.3 = f32[256,128]{1,0:T(8,128)S(1)} collective-permute-done((f32[256,128]{1,0:T(8,128)S(1)}, f32[256,128]{1,0:T(8,128)S(1)}, u32[]{:S(2)}, u32[]{:S(2)}) %collective-permute-start.3) | collective-permute-done | bytes 131104 | tf_op jit(solution)/shard_map/ppermute | solution.py:237
  48.3 2.8 %collective-permute-done.4 = f32[256,128]{1,0:T(8,128)S(1)} collective-permute-done((f32[256,128]{1,0:T(8,128)S(1)}, f32[256,128]{1,0:T(8,128)S(1)}, u32[]{:S(2)}, u32[]{:S(2)}) %collective-permute-start.4) | collective-permute-done | bytes 131104 | tf_op jit(solution)/shard_map/ppermute | solution.py:237
  52.6 2.2 %collective-permute-done.6 = f32[256,128]{1,0:T(8,128)S(1)} collective-permute-done((f32[256,128]{1,0:T(8,128)S(1)}, f32[256,128]{1,0:T(8,128)S(1)}, u32[]{:S(2)}, u32[]{:S(2)}) %collective-permute-start.6) | collective-permute-done | bytes 131104 | tf_op jit(solution)/shard_map/ppermute | solution.py:237
  54.9 5.7 %col_pass.2 = f32[896,128]{1,0:T(8,128)S(1)} custom-call(s32[256]{0:T(256)S(1)} %get-tuple-element.18.slot_ref, bf16[256,128,128]{2,1,0:T(8,128)(2,1)S(1)} %get-tuple-element.9.tiles_ref, f32[256,128]{1,0:T(8,128)S(1)} %bitcast_subtract_fusion.1.pots_ref, f32[16,128]{1,0:T(8,128)S(1)} %convert_bitcast_fusion.refs_0_), custom_call_target="tpu_custom_call" | custom-call | tf_op jit(solution)/shard_map/col_pass/pallas_call | solution.py:144
  60.6 14.5 %all_to_all.21 = f32[16,56,128]{2,1,0:T(8,128)S(1)} all-to-all(f32[16,56,128]{2,1,0:T(8,128)S(1)} %bitcast.70), channel_id=1, replica_groups=mesh['row'=16,'col'=16] {'col'}, dimensions={0} | all-to-all | bytes 917504 | tf_op jit(solution)/shard_map/all_to_all | solution.py:222
  75.2 2.5 %segment.2 = f32[256,128]{1,0:T(8,128)S(1)} custom-call(s32[768]{0:T(1024)S(1)} %convert_element_type.19.ids_ref, f32[896,128]{1,0:T(8,128)S(1)} %bitcast.69), custom_call_target="tpu_custom_call" | custom-call | tf_op jit(solution)/shard_map/segment/pallas_call | solution.py:209
  77.8 2.0 %collective-permute-start.7 = (f32[128,128]{1,0:T(8,128)S(1)}, f32[128,128]{1,0:T(8,128)S(1)}, u32[]{:S(2)}, u32[]{:S(2)}) collective-permute-start(f32[128,128]{1,0:T(8,128)S(1)} %slice_select_fusion.3), channel_id=1, source_target_pairs={{16,0},{0,16},{48,32},{32,48},{80,64},{64,80},{112,96},{96,112},{1... | collective-permute-start | bytes 196616 | tf_op jit(solution)/shard_map/ppermute | solution.py:237
  80.7 2.0 %collective-permute-start.8 = (f32[128,128]{1,0:T(8,128)S(1)}, f32[128,128]{1,0:T(8,128)S(1)}, u32[]{:S(2)}, u32[]{:S(2)}) collective-permute-start(f32[128,128]{1,0:T(8,128)S(1)} %log_add_fusion.5), channel_id=1, source_target_pairs={{32,0},{48,16},{0,32},{16,48},{96,64},{112,80},{64,96},{80,112},{1... | collective-permute-start | bytes 196616 | tf_op jit(solution)/shard_map/ppermute | solution.py:237
  82.7 2.2 %collective-permute-done.8 = f32[128,128]{1,0:T(8,128)S(1)} collective-permute-done((f32[128,128]{1,0:T(8,128)S(1)}, f32[128,128]{1,0:T(8,128)S(1)}, u32[]{:S(2)}, u32[]{:S(2)}) %collective-permute-start.8) | collective-permute-done | bytes 65568 | tf_op jit(solution)/shard_map/ppermute | solution.py:237
  84.9 5.0 %collective-permute-start.10 = (f32[128,128]{1,0:T(8,128)S(1)}, f32[128,128]{1,0:T(8,128)S(1)}, u32[]{:S(2)}, u32[]{:S(2)}) collective-permute-start(f32[128,128]{1,0:T(8,128)S(1)} %log_add_fusion.4), channel_id=1, source_target_pairs={{224,0},{240,16},{64,32},{80,48},{32,64},{48,80},{128,96},{144,112... | collective-permute-start | bytes 196616 | tf_op jit(solution)/shard_map/ppermute | solution.py:237
  92.0 1.8 %collective-permute-done.11 = f32[128,128]{1,0:T(8,128)S(1)} collective-permute-done((f32[128,128]{1,0:T(8,128)S(1)}, f32[128,128]{1,0:T(8,128)S(1)}, u32[]{:S(2)}, u32[]{:S(2)}) %collective-permute-start.11) | collective-permute-done | bytes 65568 | tf_op jit(solution)/shard_map/ppermute | solution.py:237
  93.9 3.6 %collective-permute-done.9 = f32[128,128]{1,0:T(8,128)S(1)} collective-permute-done((f32[128,128]{1,0:T(8,128)S(1)}, f32[128,128]{1,0:T(8,128)S(1)}, u32[]{:S(2)}, u32[]{:S(2)}) %collective-permute-start.9) | collective-permute-done | bytes 65568 | tf_op jit(solution)/shard_map/ppermute | solution.py:237
  97.6 3.3 %collective-permute-start.12 = (f32[128,128]{1,0:T(8,128)S(1)}, f32[128,128]{1,0:T(8,128)S(1)}, u32[]{:S(2)}, u32[]{:S(2)}) collective-permute-start(f32[128,128]{1,0:T(8,128)S(1)} %fusion.8), channel_id=1, source_target_pairs={{16,0},{0,16},{48,32},{32,48},{80,64},{64,80},{112,96},{96,112},{1... | collective-permute-start | bytes 196616 | tf_op jit(solution)/shard_map/ppermute | solution.py:237
  103.1 12.3 %all_to_all.22 = f32[16,48,128]{2,1,0:T(8,128)S(1)} all-to-all(f32[16,48,128]{2,1,0:T(8,128)S(1)} %bitcast.73), channel_id=1, replica_groups=mesh['row'=16,'col'=16] {'col'}, dimensions={0} | all-to-all | bytes 786432 | tf_op jit(solution)/shard_map/all_to_all | solution.py:222
  115.4 7.0 %row_pass.3 = (f32[256,128]{1,0:T(8,128)S(1)}, bf16[256,128,128]{2,1,0:T(8,128)(2,1)S(1)}) custom-call(s32[256]{0:T(256)S(1)} %get-tuple-element.19.slot_ref, bf16[256,128,128]{2,1,0:T(8,128)(2,1)} %bitcast.77, f32[768,128]{1,0:T(8,128)S(1)} %bitcast.71), custom_call_target="tpu_custom_call" | custom-call | tf_op jit(solution)/shard_map/row_pass/pallas_call | solution.py:102
  123.4 1.8 collective-permute-start.14
  125.1 2.6 %collective-permute-done.13 = f32[256,128]{1,0:T(8,128)S(1)} collective-permute-done((f32[256,128]{1,0:T(8,128)S(1)}, f32[256,128]{1,0:T(8,128)S(1)}, u32[]{:S(2)}, u32[]{:S(2)}) %collective-permute-start.13) | collective-permute-done | bytes 131104 | tf_op jit(solution)/shard_map/ppermute | solution.py:237
  128.6 3.2 %collective-permute-done.15 = f32[256,128]{1,0:T(8,128)S(1)} collective-permute-done((f32[256,128]{1,0:T(8,128)S(1)}, f32[256,128]{1,0:T(8,128)S(1)}, u32[]{:S(2)}, u32[]{:S(2)}) %collective-permute-start.15) | collective-permute-done | bytes 131104 | tf_op jit(solution)/shard_map/ppermute | solution.py:237
  134.3 3.1 %collective-permute-done.16 = f32[256,128]{1,0:T(8,128)S(1)} collective-permute-done((f32[256,128]{1,0:T(8,128)S(1)}, f32[256,128]{1,0:T(8,128)S(1)}, u32[]{:S(2)}, u32[]{:S(2)}) %collective-permute-start.16) | collective-permute-done | bytes 131104 | tf_op jit(solution)/shard_map/ppermute | solution.py:237
  137.4 2.5 %collective-permute-done.18 = f32[256,128]{1,0:T(8,128)S(1)} collective-permute-done((f32[256,128]{1,0:T(8,128)S(1)}, f32[256,128]{1,0:T(8,128)S(1)}, u32[]{:S(2)}, u32[]{:S(2)}) %collective-permute-start.18) | collective-permute-done | bytes 131104 | tf_op jit(solution)/shard_map/ppermute | solution.py:237
  140.0 5.7 %col_pass.3 = f32[768,128]{1,0:T(8,128)S(1)} custom-call(s32[256]{0:T(256)S(1)} %get-tuple-element.19.slot_ref, bf16[256,128,128]{2,1,0:T(8,128)(2,1)S(1)} %get-tuple-element.13.tiles_ref, f32[256,128]{1,0:T(8,128)S(1)} %bitcast_subtract_fusion.pots_ref), custom_call_target="tpu_custom_call" | custom-call | tf_op jit(solution)/shard_map/col_pass/pallas_call | solution.py:144
  145.7 11.9 %all_to_all.23 = f32[16,48,128]{2,1,0:T(8,128)S(1)} all-to-all(f32[16,48,128]{2,1,0:T(8,128)S(1)} %bitcast.72), channel_id=1, replica_groups=mesh['row'=16,'col'=16] {'col'}, dimensions={0} | all-to-all | bytes 786432 | tf_op jit(solution)/shard_map/all_to_all | solution.py:222
  157.6 2.5 %segment.3 = f32[256,128]{1,0:T(8,128)S(1)} custom-call(s32[768]{0:T(1024)S(1)} %convert_element_type.19.ids_ref, f32[768,128]{1,0:T(8,128)S(1)} %bitcast.74), custom_call_target="tpu_custom_call" | custom-call | tf_op jit(solution)/shard_map/segment/pallas_call | solution.py:209
  160.1 2.7 %collective-permute-start.19 = (f32[128,128]{1,0:T(8,128)S(1)}, f32[128,128]{1,0:T(8,128)S(1)}, u32[]{:S(2)}, u32[]{:S(2)}) collective-permute-start(f32[128,128]{1,0:T(8,128)S(1)} %slice_select_fusion.2), channel_id=1, source_target_pairs={{16,0},{0,16},{48,32},{32,48},{80,64},{64,80},{112,96},{96,112},{1... | collective-permute-start | bytes 196616 | tf_op jit(solution)/shard_map/ppermute | solution.py:237
  164.3 2.7 %collective-permute-done.20 = f32[128,128]{1,0:T(8,128)S(1)} collective-permute-done((f32[128,128]{1,0:T(8,128)S(1)}, f32[128,128]{1,0:T(8,128)S(1)}, u32[]{:S(2)}, u32[]{:S(2)}) %collective-permute-start.20) | collective-permute-done | bytes 65568 | tf_op jit(solution)/shard_map/ppermute | solution.py:237
  168.6 1.7 collective-permute-start.22
  175.2 2.6 %collective-permute-start.24 = (f32[128,128]{1,0:T(8,128)S(1)}, f32[128,128]{1,0:T(8,128)S(1)}, u32[]{:S(2)}, u32[]{:S(2)}) collective-permute-start(f32[128,128]{1,0:T(8,128)S(1)} %fusion.15), channel_id=1, source_target_pairs={{16,0},{0,16},{48,32},{32,48},{80,64},{64,80},{112,96},{96,112},{1... | collective-permute-start | bytes 196616 | tf_op jit(solution)/shard_map/ppermute | solution.py:237
  (68 shorter events, 29.2 us)
Async XLA Ops:
  0.6 0.9 copy-start
  0.6 26.2 %copy-start.5 = (s32[256,1]{0,1:T(1,128)S(1)}, s32[256,1]{0,1:T(1,128)}, u32[]{:S(2)}) copy-start(s32[256,1]{0,1:T(1,128)} %param.7) | copy-start | bytes 3076
  24.9 4.2 %collective-permute-start = (f32[2048,128]{1,0:T(8,128)S(1)}, f32[2048,128]{1,0:T(8,128)S(1)}, u32[]{:S(2)}, u32[]{:S(2)}) collective-permute-start(f32[2048,128]{1,0:T(8,128)S(1)} %bitcast.67), channel_id=1, source_target_pairs={{16,0},{0,16},{48,32},{32,48},{80,64},{64,80},{112,96},{96,112},{1... | collective-permute-start | bytes 3145736 | tf_op jit(solution)/shard_map/ppermute | solution.py:237
  29.1 25.7 %copy-start.2 = (f32[32768]{0:T(1024)S(1)}, f32[32768]{0:T(1024)}, u32[]{:S(2)}) copy-start(f32[32768]{0:T(1024)} %param.9) | copy-start | bytes 393220
  36.3 6.3 %collective-permute-start.1 = (f32[256,128]{1,0:T(8,128)S(1)}, f32[256,128]{1,0:T(8,128)S(1)}, u32[]{:S(2)}, u32[]{:S(2)}) collective-permute-start(f32[256,128]{1,0:T(8,128)S(1)} %get-tuple-element.10), channel_id=1, source_target_pairs={{2,0},{3,1},{0,2},{1,3},{6,4},{7,5},{4,6},{5,7},{10,8},{11,9},{8,1... | collective-permute-start | bytes 393224 | tf_op jit(solution)/shard_map/ppermute | solution.py:237
  37.5 6.1 %collective-permute-start.2 = (f32[256,128]{1,0:T(8,128)S(1)}, f32[256,128]{1,0:T(8,128)S(1)}, u32[]{:S(2)}, u32[]{:S(2)}) collective-permute-start(f32[256,128]{1,0:T(8,128)S(1)} %get-tuple-element.10), channel_id=1, source_target_pairs={{1,0},{2,1},{3,2},{0,3},{5,4},{6,5},{7,6},{4,7},{9,8},{10,9},{11,1... | collective-permute-start | bytes 393224 | tf_op jit(solution)/shard_map/ppermute | solution.py:237
  38.9 6.7 %collective-permute-start.3 = (f32[256,128]{1,0:T(8,128)S(1)}, f32[256,128]{1,0:T(8,128)S(1)}, u32[]{:S(2)}, u32[]{:S(2)}) collective-permute-start(f32[256,128]{1,0:T(8,128)S(1)} %get-tuple-element.10), channel_id=1, source_target_pairs={{3,0},{0,1},{1,2},{2,3},{7,4},{4,5},{5,6},{6,7},{11,8},{8,9},{9,10... | collective-permute-start | bytes 393224 | tf_op jit(solution)/shard_map/ppermute | solution.py:237
  45.7 5.4 %collective-permute-start.4 = (f32[256,128]{1,0:T(8,128)S(1)}, f32[256,128]{1,0:T(8,128)S(1)}, u32[]{:S(2)}, u32[]{:S(2)}) collective-permute-start(f32[256,128]{1,0:T(8,128)S(1)} %log_add_fusion.1), channel_id=1, source_target_pairs={{8,0},{9,1},{10,2},{11,3},{12,4},{13,5},{14,6},{15,7},{0,8},{1,9},... | collective-permute-start | bytes 393224 | tf_op jit(solution)/shard_map/ppermute | solution.py:237
  46.8 5.8 %collective-permute-start.5 = (f32[256,128]{1,0:T(8,128)S(1)}, f32[256,128]{1,0:T(8,128)S(1)}, u32[]{:S(2)}, u32[]{:S(2)}) collective-permute-start(f32[256,128]{1,0:T(8,128)S(1)} %log_add_fusion.1), channel_id=1, source_target_pairs={{4,0},{5,1},{6,2},{7,3},{8,4},{9,5},{10,6},{11,7},{12,8},{13,9},{1... | collective-permute-start | bytes 393224 | tf_op jit(solution)/shard_map/ppermute | solution.py:237
  48.0 6.8 %collective-permute-start.6 = (f32[256,128]{1,0:T(8,128)S(1)}, f32[256,128]{1,0:T(8,128)S(1)}, u32[]{:S(2)}, u32[]{:S(2)}) collective-permute-start(f32[256,128]{1,0:T(8,128)S(1)} %log_add_fusion.1), channel_id=1, source_target_pairs={{12,0},{13,1},{14,2},{15,3},{0,4},{1,5},{2,6},{3,7},{4,8},{5,9},{6... | collective-permute-start | bytes 393224 | tf_op jit(solution)/shard_map/ppermute | solution.py:237
  60.6 36.9 %copy-start.3 = (f32[32768]{0:T(1024)S(1)}, f32[32768]{0:T(1024)}, u32[]{:S(2)}) copy-start(f32[32768]{0:T(1024)} %param.10) | copy-start | bytes 393220
  60.6 36.9 %copy-start.4 = (f32[32768]{0:T(1024)S(1)}, f32[32768]{0:T(1024)}, u32[]{:S(2)}) copy-start(f32[32768]{0:T(1024)} %param.11) | copy-start | bytes 393220
  77.8 2.9 %collective-permute-start.7 = (f32[128,128]{1,0:T(8,128)S(1)}, f32[128,128]{1,0:T(8,128)S(1)}, u32[]{:S(2)}, u32[]{:S(2)}) collective-permute-start(f32[128,128]{1,0:T(8,128)S(1)} %slice_select_fusion.3), channel_id=1, source_target_pairs={{16,0},{0,16},{48,32},{32,48},{80,64},{64,80},{112,96},{96,112},{1... | collective-permute-start | bytes 196616 | tf_op jit(solution)/shard_map/ppermute | solution.py:237
  80.7 4.1 %collective-permute-start.8 = (f32[128,128]{1,0:T(8,128)S(1)}, f32[128,128]{1,0:T(8,128)S(1)}, u32[]{:S(2)}, u32[]{:S(2)}) collective-permute-start(f32[128,128]{1,0:T(8,128)S(1)} %log_add_fusion.5), channel_id=1, source_target_pairs={{32,0},{48,16},{0,32},{16,48},{96,64},{112,80},{64,96},{80,112},{1... | collective-permute-start | bytes 196616 | tf_op jit(solution)/shard_map/ppermute | solution.py:237
  84.9 7.2 %collective-permute-start.10 = (f32[128,128]{1,0:T(8,128)S(1)}, f32[128,128]{1,0:T(8,128)S(1)}, u32[]{:S(2)}, u32[]{:S(2)}) collective-permute-start(f32[128,128]{1,0:T(8,128)S(1)} %log_add_fusion.4), channel_id=1, source_target_pairs={{224,0},{240,16},{64,32},{80,48},{32,64},{48,80},{128,96},{144,112... | collective-permute-start | bytes 196616 | tf_op jit(solution)/shard_map/ppermute | solution.py:237
  89.9 4.0 %collective-permute-start.11 = (f32[128,128]{1,0:T(8,128)S(1)}, f32[128,128]{1,0:T(8,128)S(1)}, u32[]{:S(2)}, u32[]{:S(2)}) collective-permute-start(f32[128,128]{1,0:T(8,128)S(1)} %log_add_fusion.4), channel_id=1, source_target_pairs={{64,0},{80,16},{224,32},{240,48},{128,64},{144,80},{32,96},{48,112... | collective-permute-start | bytes 196616 | tf_op jit(solution)/shard_map/ppermute | solution.py:237
  91.0 6.5 %collective-permute-start.9 = (f32[128,128]{1,0:T(8,128)S(1)}, f32[128,128]{1,0:T(8,128)S(1)}, u32[]{:S(2)}, u32[]{:S(2)}) collective-permute-start(f32[128,128]{1,0:T(8,128)S(1)} %log_add_fusion.4), channel_id=1, source_target_pairs={{160,0},{176,16},{128,32},{144,48},{224,64},{240,80},{192,96},{208... | collective-permute-start | bytes 196616 | tf_op jit(solution)/shard_map/ppermute | solution.py:237
  97.6 4.2 %collective-permute-start.12 = (f32[128,128]{1,0:T(8,128)S(1)}, f32[128,128]{1,0:T(8,128)S(1)}, u32[]{:S(2)}, u32[]{:S(2)}) collective-permute-start(f32[128,128]{1,0:T(8,128)S(1)} %fusion.8), channel_id=1, source_target_pairs={{16,0},{0,16},{48,32},{32,48},{80,64},{64,80},{112,96},{96,112},{1... | collective-permute-start | bytes 196616 | tf_op jit(solution)/shard_map/ppermute | solution.py:237
  122.4 5.4 %collective-permute-start.13 = (f32[256,128]{1,0:T(8,128)S(1)}, f32[256,128]{1,0:T(8,128)S(1)}, u32[]{:S(2)}, u32[]{:S(2)}) collective-permute-start(f32[256,128]{1,0:T(8,128)S(1)} %get-tuple-element.12), channel_id=1, source_target_pairs={{2,0},{3,1},{0,2},{1,3},{6,4},{7,5},{4,6},{5,7},{10,8},{11,9},{8,1... | collective-permute-start | bytes 393224 | tf_op jit(solution)/shard_map/ppermute | solution.py:237
  123.4 5.3 %collective-permute-start.14 = (f32[256,128]{1,0:T(8,128)S(1)}, f32[256,128]{1,0:T(8,128)S(1)}, u32[]{:S(2)}, u32[]{:S(2)}) collective-permute-start(f32[256,128]{1,0:T(8,128)S(1)} %get-tuple-element.12), channel_id=1, source_target_pairs={{1,0},{2,1},{3,2},{0,3},{5,4},{6,5},{7,6},{4,7},{9,8},{10,9},{11,1... | collective-permute-start | bytes 393224 | tf_op jit(solution)/shard_map/ppermute | solution.py:237
  125.1 6.7 %collective-permute-start.15 = (f32[256,128]{1,0:T(8,128)S(1)}, f32[256,128]{1,0:T(8,128)S(1)}, u32[]{:S(2)}, u32[]{:S(2)}) collective-permute-start(f32[256,128]{1,0:T(8,128)S(1)} %get-tuple-element.12), channel_id=1, source_target_pairs={{3,0},{0,1},{1,2},{2,3},{7,4},{4,5},{5,6},{6,7},{11,8},{8,9},{9,10... | collective-permute-start | bytes 393224 | tf_op jit(solution)/shard_map/ppermute | solution.py:237
  132.0 5.4 %collective-permute-start.16 = (f32[256,128]{1,0:T(8,128)S(1)}, f32[256,128]{1,0:T(8,128)S(1)}, u32[]{:S(2)}, u32[]{:S(2)}) collective-permute-start(f32[256,128]{1,0:T(8,128)S(1)} %log_add_fusion), channel_id=1, source_target_pairs={{8,0},{9,1},{10,2},{11,3},{12,4},{13,5},{14,6},{15,7},{0,8},{1,9},... | collective-permute-start | bytes 393224 | tf_op jit(solution)/shard_map/ppermute | solution.py:237
  132.8 4.6 %collective-permute-start.17 = (f32[256,128]{1,0:T(8,128)S(1)}, f32[256,128]{1,0:T(8,128)S(1)}, u32[]{:S(2)}, u32[]{:S(2)}) collective-permute-start(f32[256,128]{1,0:T(8,128)S(1)} %log_add_fusion), channel_id=1, source_target_pairs={{4,0},{5,1},{6,2},{7,3},{8,4},{9,5},{10,6},{11,7},{12,8},{13,9},{1... | collective-permute-start | bytes 393224 | tf_op jit(solution)/shard_map/ppermute | solution.py:237
  133.5 6.4 %collective-permute-start.18 = (f32[256,128]{1,0:T(8,128)S(1)}, f32[256,128]{1,0:T(8,128)S(1)}, u32[]{:S(2)}, u32[]{:S(2)}) collective-permute-start(f32[256,128]{1,0:T(8,128)S(1)} %log_add_fusion), channel_id=1, source_target_pairs={{12,0},{13,1},{14,2},{15,3},{0,4},{1,5},{2,6},{3,7},{4,8},{5,9},{6... | collective-permute-start | bytes 393224 | tf_op jit(solution)/shard_map/ppermute | solution.py:237
  140.0 5.7 %copy-start.1 = (f32[256,128]{1,0:T(8,128)}, f32[256,128]{1,0:T(8,128)S(1)}, u32[]{:S(2)}) copy-start(f32[256,128]{1,0:T(8,128)S(1)} %bitcast_subtract_fusion.pots_ref) | copy-start | bytes 393220
  160.1 3.6 %collective-permute-start.19 = (f32[128,128]{1,0:T(8,128)S(1)}, f32[128,128]{1,0:T(8,128)S(1)}, u32[]{:S(2)}, u32[]{:S(2)}) collective-permute-start(f32[128,128]{1,0:T(8,128)S(1)} %slice_select_fusion.2), channel_id=1, source_target_pairs={{16,0},{0,16},{48,32},{32,48},{80,64},{64,80},{112,96},{96,112},{1... | collective-permute-start | bytes 196616 | tf_op jit(solution)/shard_map/ppermute | solution.py:237
  163.7 3.2 %collective-permute-start.20 = (f32[128,128]{1,0:T(8,128)S(1)}, f32[128,128]{1,0:T(8,128)S(1)}, u32[]{:S(2)}, u32[]{:S(2)}) collective-permute-start(f32[128,128]{1,0:T(8,128)S(1)} %log_add_fusion.3), channel_id=1, source_target_pairs={{32,0},{48,16},{0,32},{16,48},{96,64},{112,80},{64,96},{80,112},{1... | collective-permute-start | bytes 196616 | tf_op jit(solution)/shard_map/ppermute | solution.py:237
  167.0 6.3 %collective-permute-start.21 = (f32[128,128]{1,0:T(8,128)S(1)}, f32[128,128]{1,0:T(8,128)S(1)}, u32[]{:S(2)}, u32[]{:S(2)}) collective-permute-start(f32[128,128]{1,0:T(8,128)S(1)} %log_add_fusion.2), channel_id=1, source_target_pairs={{160,0},{176,16},{128,32},{144,48},{224,64},{240,80},{192,96},{208... | collective-permute-start | bytes 196616 | tf_op jit(solution)/shard_map/ppermute | solution.py:237
  168.6 5.3 %collective-permute-start.22 = (f32[128,128]{1,0:T(8,128)S(1)}, f32[128,128]{1,0:T(8,128)S(1)}, u32[]{:S(2)}, u32[]{:S(2)}) collective-permute-start(f32[128,128]{1,0:T(8,128)S(1)} %log_add_fusion.2), channel_id=1, source_target_pairs={{224,0},{240,16},{64,32},{80,48},{32,64},{48,80},{128,96},{144,112... | collective-permute-start | bytes 196616 | tf_op jit(solution)/shard_map/ppermute | solution.py:237
  170.3 4.8 %collective-permute-start.23 = (f32[128,128]{1,0:T(8,128)S(1)}, f32[128,128]{1,0:T(8,128)S(1)}, u32[]{:S(2)}, u32[]{:S(2)}) collective-permute-start(f32[128,128]{1,0:T(8,128)S(1)} %log_add_fusion.2), channel_id=1, source_target_pairs={{64,0},{80,16},{224,32},{240,48},{128,64},{144,80},{32,96},{48,112... | collective-permute-start | bytes 196616 | tf_op jit(solution)/shard_map/ppermute | solution.py:237
  175.2 3.5 %collective-permute-start.24 = (f32[128,128]{1,0:T(8,128)S(1)}, f32[128,128]{1,0:T(8,128)S(1)}, u32[]{:S(2)}, u32[]{:S(2)}) collective-permute-start(f32[128,128]{1,0:T(8,128)S(1)} %fusion.15), channel_id=1, source_target_pairs={{16,0},{0,16},{48,32},{32,48},{80,64},{64,80},{112,96},{96,112},{1... | collective-permute-start | bytes 196616 | tf_op jit(solution)/shard_map/ppermute | solution.py:237
